TPU v7x, 256 devices: a whole 4x4x8 slice. The times are simulated.
256 devices in a mesh: row: 64 (over y, z, core), col: 4 (over x).
Axes of the slice: x: 4, y: 4, z: 8, core: 2. Of those that a mesh axis runs over, the one named last changes fastest.
Arguments:
- layout: bfloat16 [512, 8192], P('row', 'col'), may hold values from -1 to 1
- target: bfloat16 [512, 8192], P('row', 'col'), may hold values from 0 to 1
- kernel_real: float32 [24, 128, 128], replicated, may hold values from -320 to 320
- kernel_imaginary: float32 [24, 128, 128], replicated, may hold values from -320 to 320
- weights: float32 [24], replicated, may hold values from 0.02 to 0.5
- first_taps: float32 [9, 64], replicated, may hold values from -2 to 2
- first_bias: float32 [64], replicated, may hold values from -3 to 3
- second_taps: float32 [9, 64], replicated, may hold values from -0.25 to 0.25
- second_bias: float32 [1], replicated, may hold values from -3 to 3
Outputs:
- resist: float32 [512, 8192], P('row', 'col')
- kernel_grads: float32 [2, 24, 128, 128], P(None, None, None, 'row')
All inputs are finite; a program needn't handle non-finite values.
Results may differ from a plain program's by a relative error of at most 0.0003.
Values may be sent and summed in bfloat16 or wider, within the bound.
No kernel may reach another device: no remote copies, remote signals or barrier semaphores. Data moves between devices by JAX's collectives and lax.ppermute only.
A program may use at most 64 MiB of HBM per device.

v0:
```python
import functools
import math

import jax
import jax.numpy as jnp
import numpy as np
from jax import lax
from jax.experimental import pallas as pl
from jax.experimental.pallas import tpu as pltpu
from jax.sharding import Mesh, PartitionSpec as P

TILE = 512
BAND = 128
ROW = ("y", "z", "core")
ALL = ("y", "z", "core", "x")
HIGH = lax.Precision.HIGH


def gather_on(x, axes, n):
    return lax.all_to_all(jnp.broadcast_to(x[None], (n,) + x.shape), axes, 0, 0, tiled=True)


def sum_cols(x):
    one, two, three = (lax.ppermute(x, "x", [(i, (i + k) % 4) for i in range(4)]) for k in (1, 2, 3))
    return (x + two) + (one + three)


def phase_angles(freqs, positions):
    return 2.0 * math.pi * ((freqs[:, None] * positions[None, :]) % TILE) / TILE


def dot(a, b):
    return jnp.dot(a, b, preferred_element_type=jnp.float32)


def constant_split(x):
    x = np.asarray(x, np.float32)
    hi = x.astype(jnp.bfloat16)
    return hi, (x - hi.astype(np.float32)).astype(jnp.bfloat16)


VMEM = pl.BlockSpec(memory_space=pltpu.VMEM)
SMEM = pl.BlockSpec(memory_space=pltpu.SMEM)
HERE = pl.BlockSpec(memory_space=pltpu.HBM)


def homes(*arrays):
    return [pltpu.with_memory_space_constraint(jnp.asarray(x), pltpu.HBM) for x in arrays]


def fetch(sources, targets, sems):
    copies = [pltpu.make_async_copy(a, b, sems.at[i]) for i, (a, b) in enumerate(zip(sources, targets, strict=True))]
    for copy in copies:
        copy.start()
    return copies


def params(mib):
    return pltpu.CompilerParams(vmem_limit_bytes=mib * 1024 * 1024)


FREQ = np.arange(BAND) - BAND // 2


def analysis_table():
    ang = phase_angles(np.arange(65), np.arange(TILE))
    table = np.zeros((TILE, 2 * BAND))
    table[:, :64], table[:, 64:BAND] = np.cos(ang[:64]).T, np.sin(ang[1:]).T
    table[:, BAND : BAND + 4] = np.cos(ang[64])[:, None]
    return np.concatenate(constant_split(table), 0)


def row_transform_tables():
    tables = []
    for y in range(4):
        for core in range(2):
            slabs = [128 * ((y - k) % 4) + 8 * (core ^ other) for other in range(2) for k in range(4)]
            n = (np.array(slabs)[:, None, None] + 16 * np.arange(8)[:, None] + np.arange(8)).reshape(-1)
            ang = phase_angles(FREQ, n)
            tables.append(np.concatenate(constant_split(np.concatenate([np.cos(ang), np.sin(ang)], 0)), 0))
    return np.stack(tables)


def expand_table(tiles, norm):
    table = np.zeros((tiles + 1, 2, BAND, 2, BAND))
    for g in range(BAND):
        q = g - 64
        m = abs(q)
        if m < 64:
            table[0, 0, m, 0, g] = 1.0
            table[0, 1, m, 1, g] = -1.0
        else:
            for t in range(tiles):
                table[1 + t, 0, t, 0, g] = 1.0
                table[1 + t, 1, t, 1, g] = -1.0
        if m:
            sign = -1.0 if q > 0 else 1.0
            table[0, 1, 63 + m, 0, g] = sign
            table[0, 0, 63 + m, 1, g] = sign
    return (table.reshape(tiles + 1, 2 * BAND, 2 * BAND) * norm).astype(jnp.bfloat16)


def synthesis_table(norm):
    ang = phase_angles(FREQ, np.arange(TILE))
    c, s = np.cos(ang), np.sin(ang)
    return np.concatenate([np.concatenate([c, s], 1), np.concatenate([-s, c], 1)], 0) * norm


def line_tables(groups, height):
    at = np.arange(groups)[:, None] * height + np.array(FIELD_ROWS)[None, :]
    ang = phase_angles(at.reshape(-1), FREQ)
    return np.concatenate([np.cos(ang), np.sin(ang)], 1).reshape(groups, 16, 2 * BAND).astype(np.float32)


FIELD_ROWS = list(range(8)) + [-4, -3, -2, -1, 8, 9, 10, 11]
HIDDEN_ROWS = list(range(-1, 9)) + [-3, -2, 9, 10]
SLOPE_ROWS = list(range(8)) + [-2, -1, 8, 9] + [None] * 4
WIDE = 17 * 128


def halves(x):
    hi = x.astype(jnp.bfloat16)
    return hi, (x - hi.astype(jnp.float32)).astype(jnp.bfloat16)


def pick(out_rows, in_rows, sign):
    hit = lambda a, b, dy: float(a is not None and b is not None and b - a == sign * (dy - 1))
    return np.array([[[hit(a, b, dy) for b in in_rows] for a in out_rows] for dy in range(3)])


INNER = HIDDEN_ROWS[:10]
CHANNELS = 64


def choose_tables():
    choose = np.zeros((3, 48, 7, 256))
    for dy in range(3):
        for dx in range(3):
            for slot in range(16):
                lane = 16 * dx + slot
                for part, section in ((0, 0), (1, 1), (0, 2)):
                    choose[part, 3 * dy + dx, dy, 48 * section + lane] = 1.0
                    choose[part, 16 + 3 * dy + dx, 4 + dy, 48 * section + lane] = 1.0
    for part in range(3):
        choose[part, 32, 3, 144 + part] = 1.0
    return choose.reshape(144, 7 * 256).astype(jnp.bfloat16)


def lane_masks():
    fore = pick(HIDDEN_ROWS, FIELD_ROWS, 1).transpose(1, 0, 2)
    back = pick(INNER, SLOPE_ROWS, -1).transpose(1, 0, 2)
    masks = np.zeros((80, 256), np.float32)
    masks[:42, :144] = np.tile(fore, (1, 1, 9)).reshape(42, 144)
    masks[42:72, :144] = np.tile(back, (1, 1, 9)).reshape(30, 144)
    return masks


def row_masks():
    fore = np.repeat(pick(SLOPE_ROWS, HIDDEN_ROWS, 1), CHANNELS, 2)
    back = np.repeat(pick(list(range(8)), INNER, -1), CHANNELS, 2)
    return fore.astype(np.float32), back.astype(np.float32)


def tables_kernel(
    first_taps_any, second_taps_any, bias_any, choose_any, lane_masks_any, fore_any, aft_any,
    first_ref, second_ref, second_back_ref, first_back_ref,
    first_taps_ref, second_taps_ref, bias_ref, choose_ref, lane_masks_ref, fore_ref, aft_ref, wide_ref, sems, *, rows
):
    sources = (first_taps_any, second_taps_any, bias_any, choose_any, lane_masks_any, fore_any, aft_any)
    targets = (first_taps_ref, second_taps_ref, bias_ref, choose_ref, lane_masks_ref, fore_ref, aft_ref)
    for copy in fetch(sources, targets, sems):
        copy.wait()
    row0 = lax.axis_index(ROW) * 8
    wide_ref[...] = jnp.zeros_like(wide_ref)
    wide_ref[0:9, 0:CHANNELS] = first_taps_ref[...]
    wide_ref[16:25, 0:CHANNELS] = second_taps_ref[...]
    wide_ref[32:33, 0:CHANNELS] = bias_ref[...]
    tall = wide_ref[...].T[:CHANNELS, :48]
    hi = tall.astype(jnp.bfloat16)
    rest = tall - hi.astype(jnp.float32)
    mid = rest.astype(jnp.bfloat16)
    low = (rest - mid.astype(jnp.float32)).astype(jnp.bfloat16)
    parts = dot(jnp.concatenate([hi, mid, low], 1), choose_ref[...])
    for h, n in enumerate(HIDDEN_ROWS):
        here = row0 + n
        valid = jnp.where((here >= 0) & (here < rows), 1.0, 0.0)
        block = parts[:, 768:1024]
        for dy in range(3):
            block = block + parts[:, 256 * dy : 256 * dy + 256] * lane_masks_ref[3 * h + dy : 3 * h + dy + 1]
        first_ref[64 * h : 64 * h + 64] = (block * valid)[:, :160].astype(jnp.bfloat16)
        if h < 10:
            block = 0.0
            for dy in range(3):
                at = 1024 + 256 * dy
                block = block + parts[:, at : at + 256] * lane_masks_ref[42 + 3 * h + dy : 43 + 3 * h + dy]
            second_back_ref[64 * h : 64 * h + 64] = (block * valid)[:, :144].astype(jnp.bfloat16)
    for taps_ref, mask_ref, out_ref, height in ((second_taps_ref, fore_ref, second_ref, 16), (first_taps_ref, aft_ref, first_back_ref, 8)):
        lanes = out_ref.shape[1]
        taps = taps_ref[...]
        taps = jnp.concatenate([taps] * (lanes // CHANNELS), 1)
        taps_hi = taps.astype(jnp.bfloat16).astype(jnp.float32)
        for at, part in ((0, taps_hi), (out_ref.shape[0] // 2, taps - taps_hi)):
            blocks = []
            for dx in range(3):
                block = 0.0
                for dy in range(3):
                    block = block + part[3 * dy + dx : 3 * dy + dx + 1] * mask_ref[dy]
                blocks.append(block)
            if height == 8:
                blocks.append(jnp.zeros((8, lanes), jnp.float32))
            whole = jnp.concatenate(blocks, 0)
            out_ref[at : at + whole.shape[0]] = whole.astype(jnp.bfloat16)


def resist_tables(first_taps, first_bias, second_taps, rows):
    args = (first_taps, second_taps, first_bias.reshape(1, -1), choose_tables(), lane_masks(), *row_masks())
    return pl.pallas_call(
        functools.partial(tables_kernel, rows=rows),
        out_shape=[
            jax.ShapeDtypeStruct((14 * CHANNELS, 160), jnp.bfloat16),
            jax.ShapeDtypeStruct((96, 14 * CHANNELS), jnp.bfloat16),
            jax.ShapeDtypeStruct((10 * CHANNELS, 144), jnp.bfloat16),
            jax.ShapeDtypeStruct((64, 10 * CHANNELS), jnp.bfloat16),
        ],
        in_specs=[HERE] * 7,
        out_specs=[VMEM] * 4,
        scratch_shapes=[pltpu.VMEM(a.shape, a.dtype) for a in args]
        + [pltpu.VMEM((BAND, BAND), jnp.float32), pltpu.SemaphoreType.DMA((7,))],
        compiler_params=params(12),
        name="tables",
    )(*homes(*args))


def resist_kernel(
    field_ref, target_ref, left_ref, right_ref, first_ref, second_ref, second_back_ref, first_back_ref, offset_ref,
    weights_any, fields_any, back_any,
    resist_ref, out_ref, weights_ref, fields_ref, back_ref,
    views_ref, keep_ref, mixed_ref, spread_ref, summed_ref, all_ref, sems, *, rows, cols
):
    copies = fetch((weights_any, fields_any, back_any), (weights_ref, fields_ref, back_ref), sems)
    row0 = lax.axis_index(ROW) * resist_ref.shape[0]
    col0 = lax.axis_index("x") * resist_ref.shape[1]
    width = resist_ref.shape[1]
    inner = keep_ref.shape[0]

    def columns(shape):
        lane = lax.broadcasted_iota(jnp.int32, shape, 1)
        m = jnp.where(lane < width + 64, lane, lane - WIDE)
        return m, (col0 + m >= 0) & (col0 + m < cols)

    chunks = [(i * 256, 256) for i in range(8)] + [(2048, 128)]
    m, in_grid = columns((16, WIDE))
    keep_col = (in_grid & (m >= -3) & (m < width + 3)).astype(jnp.float32)
    lane = lax.broadcasted_iota(jnp.int32, (16, BAND), 1)
    gap = [jnp.where(lane < 64, right_ref[i : i + 16], left_ref[i : i + 16]) for i in (0, 16)]
    field = jnp.concatenate([field_ref[...], gap[0]], 1)
    target = jnp.concatenate([target_ref[...], gap[1]], 1)
    for dx in range(3):
        moved = (field if dx == 1 else pltpu.roll(field, (1 - dx) % WIDE, 1)) * keep_col
        hi, lo = halves(moved)
        views_ref[16 * dx : 16 * dx + 16] = hi
        views_ref[48 + 16 * dx : 64 + 16 * dx] = hi
        views_ref[96 + 16 * dx : 112 + 16 * dx] = lo
    views_ref[144:160] = keep_col.astype(jnp.bfloat16)

    for at, size in chunks:
        here = slice(at, at + size)
        hidden = jnp.tanh(jnp.dot(first_ref[...], views_ref[:, here], preferred_element_type=jnp.float32))
        keep_ref[:, here] = 1.0 - hidden[:inner] * hidden[:inner]
        hi, lo = halves(hidden)
        both = jnp.dot(second_ref[...], hi, preferred_element_type=jnp.float32)
        small = jnp.dot(second_ref[0:48], lo, preferred_element_type=jnp.float32)
        mixed_ref[:, here] = both[:48] + both[48:] + small

    logits = offset_ref[0] + mixed_ref[16:32] + pltpu.roll(mixed_ref[0:16], 1, 1) + pltpu.roll(mixed_ref[32:48], WIDE - 1, 1)
    resist = 1.0 / (1.0 + jnp.exp(-logits))
    resist_ref[...] = resist[:8, :width]
    slot = lax.broadcasted_iota(jnp.int32, (16, WIDE), 0)
    n = jnp.where(slot < 8, slot, jnp.where(slot < 10, slot - 10, slot - 2))
    use = in_grid & (m >= -2) & (m < width + 2) & (slot < 12) & (row0 + n >= 0) & (row0 + n < rows)
    slope = jnp.where(use, (resist - target) * (TILE / cols), 0.0)
    grid_col = in_grid.astype(jnp.float32)
    for dx in range(3):
        moved = (slope if dx == 1 else pltpu.roll(slope, (dx - 1) % WIDE, 1)) * grid_col
        hi, lo = halves(moved)
        spread_ref[16 * dx : 16 * dx + 16] = hi
        spread_ref[48 + 16 * dx : 64 + 16 * dx] = hi
        spread_ref[96 + 16 * dx : 112 + 16 * dx] = lo

    for at, size in chunks:
        here = slice(at, at + size)
        hidden_grad = jnp.dot(second_back_ref[...], spread_ref[:, here], preferred_element_type=jnp.float32)
        hi, lo = halves(hidden_grad * keep_ref[:, here])
        both = jnp.dot(first_back_ref[...], hi, preferred_element_type=jnp.float32)
        small = jnp.dot(first_back_ref[0:32], lo, preferred_element_type=jnp.float32)
        summed_ref[:, here] = both[:32] + both[32:] + small
    grad = summed_ref[8:16] + pltpu.roll(summed_ref[0:8], WIDE - 1, 1) + pltpu.roll(summed_ref[16:24], 1, 1)
    for copy in copies:
        copy.wait()
    grad = jnp.concatenate([grad[:, t * TILE : (t + 1) * TILE] for t in range(4)], 0)
    grad = jnp.concatenate([grad, grad], 1) * 2.0
    half = back_ref.shape[0] // 2
    for i in range(3):
        piece = jnp.concatenate([fields_ref[8 * i + j] * (grad * weights_ref[8 * i + j]) for j in range(8)], 0)
        hi, lo = halves(piece)
        sides = (((1,), (1,)), ((), ()))
        both = lax.dot_general(back_ref[...], hi, sides, preferred_element_type=jnp.float32)
        small = lax.dot_general(back_ref[0:half], lo, sides, preferred_element_type=jnp.float32)
        all_ref[:, 256 * i : 256 * i + 256] = both[:half] + both[half:] + small
    low = lax.broadcasted_iota(jnp.int32, (8, 384), 0) < 4
    for d in range(32):
        first, second = all_ref[8 * d : 8 * d + 8, 0:384], all_ref[8 * d : 8 * d + 8, 384:768]
        out_ref[2 * d] = jnp.where(low, first, pltpu.roll(second, 4, 0))
        out_ref[2 * d + 1] = jnp.where(low, pltpu.roll(first, 4, 0), second)


def resist_block(field, target, left, right, tables, second_bias, weights, fields, back, dims):
    rows, cols = dims
    inner, width = tables[2].shape[0], field.shape[1]
    return pl.pallas_call(
        functools.partial(resist_kernel, rows=rows, cols=cols),
        out_shape=[jax.ShapeDtypeStruct((8, width), jnp.float32), jax.ShapeDtypeStruct((64, 8, 384), jnp.float32)],
        in_specs=[VMEM] * 8 + [SMEM] + [HERE] * 3,
        out_specs=[VMEM] * 2,
        scratch_shapes=[
            pltpu.SMEM(weights.shape, jnp.float32),
            pltpu.VMEM(fields.shape, jnp.float32),
            pltpu.VMEM(back.shape, jnp.bfloat16),
            pltpu.VMEM((160, WIDE), jnp.bfloat16),
            pltpu.VMEM((inner, WIDE), jnp.float32),
            pltpu.VMEM((48, WIDE), jnp.float32),
            pltpu.VMEM((144, WIDE), jnp.bfloat16),
            pltpu.VMEM((32, WIDE), jnp.float32),
            pltpu.VMEM((256, 768), jnp.float32),
            pltpu.SemaphoreType.DMA((3,)),
        ],
        compiler_params=params(28),
        name="resist",
    )(field, target, left, right, *tables, second_bias, *homes(weights, fields, back))


def analyse_kernel(layout_any, table_any, out_ref, layout_ref, table_ref, sems):
    for copy in fetch((layout_any, table_any), (layout_ref, table_ref), sems):
        copy.wait()
    x = layout_ref[...].astype(jnp.float32)
    x = jnp.concatenate([x[:, t * TILE : (t + 1) * TILE] for t in range(4)], 0).astype(jnp.bfloat16)
    sums = dot(x, table_ref[0:TILE]) + dot(x, table_ref[TILE:])
    lane = lax.broadcasted_iota(jnp.int32, (8, BAND), 1)
    last = jnp.zeros((8, BAND), jnp.float32)
    for t in range(4):
        last = jnp.where(lane == t, sums[8 * t : 8 * t + 8, BAND:], last)
    packed = jnp.concatenate([sums[:, :BAND], last], 0)
    for i in range(out_ref.shape[0]):
        out_ref[i] = packed


def fields_kernel(*refs, rows):
    slab_any, refs = refs[:8], refs[8:]
    (
        rows_any, expand_any, line_any, synth_any, real_any, imag_any, weights_any, target_any, above_any, below_any,
        spec_ref, fields_any, intensity_ref, wanted_ref, first_edge_ref, last_edge_ref, *refs
    ) = refs
    slabs, refs = refs[:8], refs[8:]
    (
        rows_ref, expand_ref, line_ref, synth_ref, real_ref, imag_ref, weights_ref, target_ref, above_ref, below_ref,
        fields_ref, seen_ref, line_hi_ref, line_lo_ref, sum_ref, sems, out_sems
    ) = refs
    at = 2 * lax.axis_index("y") + lax.axis_index("core")
    r = lax.axis_index(ROW)
    sources = (*slab_any, rows_any.at[at], expand_any, line_any.at[r], synth_any, real_any, imag_any, weights_any, target_any, above_any, below_any)
    targets = (*slabs, rows_ref, expand_ref, line_ref, synth_ref, real_ref, imag_ref, weights_ref, target_ref, above_ref, below_ref)
    copies = fetch(sources, targets, sems)
    row0 = r * 8
    kernels = real_ref.shape[0]
    for p, slab in enumerate(slabs):
        copies[p].wait()
        for t in range(5):
            hi, lo = halves(slab[:, 8 * t : 8 * t + 8, :].reshape(64, BAND))
            seen_ref[64 * p : 64 * p + 64, t * BAND : (t + 1) * BAND] = hi
            seen_ref[rows + 64 * p : rows + 64 * p + 64, t * BAND : (t + 1) * BAND] = lo
    copies[8].wait()
    table_hi = rows_ref[0 : 2 * BAND]
    u = dot(table_hi, seen_ref[0:rows]) + dot(rows_ref[2 * BAND :], seen_ref[0:rows]) + dot(table_hi, seen_ref[rows:])

    def pair(t):
        both = u[:, t * BAND : (t + 1) * BAND]
        return halves(jnp.concatenate([both[:BAND], both[BAND:]], 1))

    copies[9].wait()
    last_hi, last_lo = pair(4)
    for t in range(4):
        hi, lo = pair(t)
        spec_ref[t] = (
            dot(hi, expand_ref[0]) + dot(lo, expand_ref[0]) + dot(last_hi, expand_ref[1 + t]) + dot(last_lo, expand_ref[1 + t])
        )

    for copy in copies[10:]:
        copy.wait()
    phase = line_ref[...]
    c, s = phase[:, :BAND], phase[:, BAND:]
    table = jnp.concatenate([jnp.concatenate([c, -s], 1), jnp.concatenate([s, c], 1)], 0)
    lines_hi, lines_lo = halves(table)
    lines_both = jnp.concatenate([lines_hi, lines_lo], 0)
    sum_ref[...] = jnp.zeros_like(sum_ref)

    def lines(k, slot, j):
        kr, ki = real_ref[k], imag_ref[k]
        pieces = []
        for p in range(2):
            columns = []
            for t in (2 * p, 2 * p + 1):
                sr, si = spec_ref[t, :, :BAND], spec_ref[t, :, BAND:]
                columns.append(jnp.concatenate([kr * sr - ki * si, kr * si + ki * sr], 0))
            hi, lo = halves(jnp.concatenate(columns, 1))
            both = dot(lines_both, hi)
            out = both[:32] + both[32:] + dot(lines_hi, lo)
            for t in range(2):
                pieces.append(jnp.concatenate([out[:16, t * BAND : (t + 1) * BAND], out[16:, t * BAND : (t + 1) * BAND]], 1))
        hi, lo = halves(jnp.concatenate(pieces, 0))
        line_hi_ref[slot, 64 * j : 64 * j + 64] = hi
        line_lo_ref[slot, 64 * j : 64 * j + 64] = lo

    def waves(k0, slot, q):
        here = slice(q * 256, q * 256 + 256)
        synth_hi = synth_ref[0 : 2 * BAND, here]
        line_hi = line_hi_ref[slot]
        f = dot(line_hi, synth_hi) + dot(line_lo_ref[slot], synth_hi) + dot(line_hi, synth_ref[2 * BAND :, here])
        total = sum_ref[:, here]
        for j in range(4):
            part = f[64 * j : 64 * j + 64]
            total = total + weights_ref[k0 + j] * (part * part)
            fields_ref[k0 + j, :, here] = jnp.concatenate([part[16 * t : 16 * t + 8] for t in range(4)], 0)
        sum_ref[:, here] = total

    sent = []
    for j in range(4):
        lines(j, 0, j)
    for i in range(kernels // 4):
        for j in range(4):
            waves(4 * i, i % 2, j)
            if 4 * i + 4 < kernels:
                lines(4 * i + 4 + j, (i + 1) % 2, j)
        sent.append(pltpu.make_async_copy(fields_ref.at[4 * i : 4 * i + 4], fields_any.at[4 * i : 4 * i + 4], out_sems.at[i]))
        sent[-1].start()
    slot = lax.broadcasted_iota(jnp.int32, (16, TILE), 0)
    n = row0 + jnp.where(slot < 8, slot, jnp.where(slot < 12, slot - 12, slot - 4))
    inside = (n >= 0) & (n < rows)
    for t in range(4):
        both = sum_ref[16 * t : 16 * t + 16]
        intensity_ref[:, t * TILE : (t + 1) * TILE] = jnp.where(inside, both[:, :TILE] + both[:, TILE:], 0.0)
    wanted_ref[0:8] = target_ref[...].astype(jnp.float32)
    above, below = above_ref[...].astype(jnp.float32), below_ref[...].astype(jnp.float32)
    wanted_ref[8:16] = jnp.concatenate([above[6:8], below[0:2], jnp.zeros((4, above.shape[1]), jnp.float32)], 0)
    width = intensity_ref.shape[1]
    for i, ref in ((0, intensity_ref), (16, wanted_ref)):
        first_edge_ref[i : i + 16] = ref[:, 0:BAND]
        last_edge_ref[i : i + 16] = ref[:, width - BAND :]
    for copy in sent:
        copy.wait()


def on_device(
    layout, target, kernel_real, kernel_imaginary, weights, first_taps, first_bias, second_taps, second_bias
):
    height, width = layout.shape
    tiles = width // TILE
    kernels = kernel_real.shape[0]
    rows, cols = height * 64, width * 4
    r = lax.axis_index(ROW)
    norm = 1.0 / math.sqrt(rows * TILE)

    above = lax.ppermute(target, ROW, [(i, i + 1) for i in range(63)])
    below = lax.ppermute(target, ROW, [(i + 1, i) for i in range(63)])
    tables = resist_tables(first_taps, first_bias, second_taps, rows)

    packed = pl.pallas_call(
        analyse_kernel,
        out_shape=jax.ShapeDtypeStruct((8, 40, BAND), jnp.float32),
        in_specs=[HERE] * 2,
        out_specs=VMEM,
        scratch_shapes=[
            pltpu.VMEM(layout.shape, jnp.bfloat16),
            pltpu.VMEM((2 * TILE, 2 * BAND), jnp.bfloat16),
            pltpu.SemaphoreType.DMA((2,)),
        ],
        compiler_params=params(8),
        name="analyse",
    )(*homes(layout, analysis_table()))
    gathered = lax.all_to_all(packed, "z", 0, 0, tiled=True)
    gathered, above, below, *tables = lax.optimization_barrier((gathered, above, below, *tables))
    slabs = [gathered] + [lax.ppermute(gathered, "y", [(i, (i + k) % 4) for i in range(4)]) for k in (1, 2, 3)]
    slabs = slabs + [lax.ppermute(slab, "core", [(0, 1), (1, 0)]) for slab in slabs]

    synth = synthesis_table(norm)
    spec, fields, intensity, wanted, first_edge, last_edge = pl.pallas_call(
        functools.partial(fields_kernel, rows=rows),
        out_shape=[
            jax.ShapeDtypeStruct((tiles, BAND, 2 * BAND), jnp.float32),
            pltpu.HBM((kernels, tiles * height, 2 * TILE), jnp.float32),
            jax.ShapeDtypeStruct((16, width), jnp.float32),
            jax.ShapeDtypeStruct((16, width), jnp.float32),
            jax.ShapeDtypeStruct((32, BAND), jnp.float32),
            jax.ShapeDtypeStruct((32, BAND), jnp.float32),
        ],
        in_specs=[HERE] * 18,
        out_specs=[VMEM, HERE] + [VMEM] * 4,
        scratch_shapes=[pltpu.VMEM((8, 40, BAND), jnp.float32)] * 8
        + [
            pltpu.VMEM((4 * BAND, rows), jnp.bfloat16),
            pltpu.VMEM((tiles + 1, 2 * BAND, 2 * BAND), jnp.bfloat16),
            pltpu.VMEM((16, 2 * BAND), jnp.float32),
            pltpu.VMEM((4 * BAND, 2 * TILE), jnp.bfloat16),
            pltpu.VMEM(kernel_real.shape, jnp.float32),
            pltpu.VMEM(kernel_real.shape, jnp.float32),
            pltpu.SMEM(weights.shape, jnp.float32),
            pltpu.VMEM(target.shape, jnp.bfloat16),
            pltpu.VMEM(target.shape, jnp.bfloat16),
            pltpu.VMEM(target.shape, jnp.bfloat16),
            pltpu.VMEM((kernels, tiles * height, 2 * TILE), jnp.float32),
            pltpu.VMEM((2 * rows, 5 * BAND), jnp.bfloat16),
            pltpu.VMEM((2, 256, 2 * BAND), jnp.bfloat16),
            pltpu.VMEM((2, 256, 2 * BAND), jnp.bfloat16),
            pltpu.VMEM((64, 2 * TILE), jnp.float32),
            pltpu.SemaphoreType.DMA((18,)),
            pltpu.SemaphoreType.DMA((kernels // 4,)),
        ],
        compiler_params=params(28),
        name="fields",
    )(
        *homes(
            *slabs, row_transform_tables(), expand_table(tiles, norm), line_tables(64, height),
            np.concatenate(constant_split(synth), 0), kernel_real, kernel_imaginary, weights, target, above, below,
        )
    )
    left = lax.ppermute(last_edge, "x", [(i, i + 1) for i in range(3)])
    right = lax.ppermute(first_edge, "x", [(i + 1, i) for i in range(3)])
    back = synth.reshape(2, 64, 2, 2 * TILE).transpose(1, 2, 0, 3).reshape(256, 2 * TILE)
    back = np.concatenate(constant_split(back), 0)
    resist, send = resist_block(
        intensity, wanted, left, right, tables, second_bias, weights, fields, back, (rows, cols)
    )

    got = lax.all_to_all(send, ROW, 0, 0, tiled=True)
    wide = phase_angles(height * np.arange(64), FREQ)
    w = np.stack([np.concatenate([np.cos(wide), -np.sin(wide)], 1), np.concatenate([np.sin(wide), np.cos(wide)], 1)], 0)
    y = jnp.einsum(
        "shgil,isx->ghlx", got.reshape(64, 2, 2, 2, -1), w.astype(np.float32), precision=HIGH, preferred_element_type=jnp.float32
    )
    y = y.reshape(2, kernels, tiles, height, 2, BAND)
    near = phase_angles(np.arange(height), FREQ)
    nc, ns = np.cos(near).astype(np.float32), np.sin(near).astype(np.float32)
    z_re = jnp.sum(y[..., 0, :] * nc + y[..., 1, :] * ns, 3)
    z_im = jnp.sum(y[..., 1, :] * nc - y[..., 0, :] * ns, 3)
    s_re = lax.dynamic_slice_in_dim(spec, 2 * r, 2, 2).transpose(2, 0, 1)[:, None]
    s_im = lax.dynamic_slice_in_dim(spec, BAND + 2 * r, 2, 2).transpose(2, 0, 1)[:, None]
    mine = jnp.stack([jnp.sum(z_re * s_re + z_im * s_im, 2), jnp.sum(z_im * s_re - z_re * s_im, 2)])
    whole = sum_cols(mine)
    squares = jnp.broadcast_to(jnp.sum(whole * whole), (1, 128))
    total = jnp.sum(gather_on(squares, ROW, 64)[:, 0, 0])
    entries = 2 * kernels * BAND * BAND
    return resist, whole.transpose(0, 2, 3, 1) * lax.rsqrt(total / entries + 1e-06)


def solution(mesh):
    devices = mesh.devices.reshape(4, 8, 2, 4)
    fine = Mesh(devices, ALL)
    grid = P(ROW, "x")
    in_specs = (grid, grid, P(), P(), P(), P(), P(), P(), P())
    out_specs = (grid, P(None, None, None, ROW))
    return jax.shard_map(on_device, mesh=fine, in_specs=in_specs, out_specs=out_specs, check_vma=False)
```

profile of v0, /device:TPU:1, one launch (start us, length us, event | category | flops | bytes accessed | tf_op | source)
XLA Modules:
  0.0 126.9 jit_solution(6963373755983031512)
XLA Ops:
  0.6 1.9 %analyse.1 = f32[8,40,128]{2,1,0:T(8,128)} custom-call(bf16[8,2048]{1,0:T(8,128)(2,1)} %layout_any.1, bf16[1024,256]{1,0:T(8,128)(2,1)} %constant.64.clone.table_any), custom_call_target="tpu_custom_call" | custom-call | tf_op jit(solution)/shard_map/analyse/pallas_call | solution.py:476
  2.6 9.0 %all-to-all-start = ((f32[8,40,128]{2,1,0:T(8,128)}), f32[8,40,128]{2,1,0:T(8,128)S(1)}, u32[]{:S(2)}, u32[]{:S(2)}) async-start(f32[8,40,128]{2,1,0:T(8,128)} %analyse.1), calls=%async_computation | async-start | bytes 327680 | tf_op jit(solution)/shard_map/all_to_all | solution.py:489
  11.6 4.5 %collective-permute-start = (bf16[8,2048]{1,0:T(8,128)(2,1)}, bf16[8,2048]{1,0:T(8,128)(2,1)S(1)}, u32[]{:S(2)}, u32[]{:S(2)}) collective-permute-start(bf16[8,2048]{1,0:T(8,128)(2,1)} %refs_15_.1), channel_id=1, source_target_pairs={{0,4},{4,8},{8,12},{12,16},{16,20},{20,24},{24,28},{28,32},{32,36}... | collective-permute-start | bytes 98312 | tf_op jit(solution)/shard_map/ppermute | solution.py:472
  16.1 1.9 %collective-permute-start.1 = (bf16[8,2048]{1,0:T(8,128)(2,1)}, bf16[8,2048]{1,0:T(8,128)(2,1)S(1)}, u32[]{:S(2)}, u32[]{:S(2)}) collective-permute-start(bf16[8,2048]{1,0:T(8,128)(2,1)} %refs_15_.1), channel_id=1, source_target_pairs={{4,0},{8,4},{12,8},{16,12},{20,16},{24,20},{28,24},{32,28},{36,32}... | collective-permute-start | bytes 98312 | tf_op jit(solution)/shard_map/ppermute | solution.py:473
  18.0 2.1 %tables.1 = (bf16[896,160]{1,0:T(8,128)(2,1)S(1)}, bf16[96,896]{1,0:T(8,128)(2,1)S(1)}, bf16[640,144]{1,0:T(8,128)(2,1)S(1)}, bf16[64,640]{1,0:T(8,128)(2,1)S(1)}) custom-call(f32[9,64]{1,0:T(8,128)} %first_taps_any.1, f32[9,64]{1,0:T(8,128)} %second_taps_any.1, f32[1,64]{1,0:T(1,128)} %bitcast.41, bf16[144,1792]{1,0:T(8,128)(2,1)} %constant.60.clone.choose_any, ...), custom_call_target="tpu_custom_call" | custom-call | tf_op jit(solution)/shard_map/tables/pallas_call | solution.py:217
  20.1 0.0 collective-permute-done.refs_16_
  20.1 0.0 copy-start.9
  20.1 1.7 %collective-permute-done.1.refs_17_ = bf16[8,2048]{1,0:T(8,128)(2,1)S(1)} collective-permute-done((bf16[8,2048]{1,0:T(8,128)(2,1)}, bf16[8,2048]{1,0:T(8,128)(2,1)S(1)}, u32[]{:S(2)}, u32[]{:S(2)}) %collective-permute-start.1) | collective-permute-done | bytes 32800 | tf_op jit(solution)/shard_map/ppermute | solution.py:473
  21.8 0.0 all-to-all-done.refs_0_
  21.8 1.4 %collective-permute-start.2 = (f32[8,40,128]{2,1,0:T(8,128)S(1)}, f32[8,40,128]{2,1,0:T(8,128)S(1)}, u32[]{:S(2)}, u32[]{:S(2)}) collective-permute-start(f32[8,40,128]{2,1,0:T(8,128)S(1)} %all-to-all-done.refs_0_), channel_id=1, source_target_pairs={{0,64},{64,128},{128,192},{192,0},{1,65},{65,129},{129,193},{193,1... | collective-permute-start | bytes 491528 | tf_op jit(solution)/shard_map/ppermute | solution.py:491
  23.2 2.6 %collective-permute-start.3 = (f32[8,40,128]{2,1,0:T(8,128)S(1)}, f32[8,40,128]{2,1,0:T(8,128)S(1)}, u32[]{:S(2)}, u32[]{:S(2)}) collective-permute-start(f32[8,40,128]{2,1,0:T(8,128)S(1)} %all-to-all-done.refs_0_), channel_id=1, source_target_pairs={{0,128},{64,192},{128,0},{192,64},{1,129},{65,193},{129,1},{193,65... | collective-permute-start | bytes 491528 | tf_op jit(solution)/shard_map/ppermute | solution.py:491
  25.8 1.1 collective-permute-start.4
  26.9 1.4 %collective-permute-start.5 = (f32[8,40,128]{2,1,0:T(8,128)S(1)}, f32[8,40,128]{2,1,0:T(8,128)S(1)}, u32[]{:S(2)}, u32[]{:S(2)}) collective-permute-start(f32[8,40,128]{2,1,0:T(8,128)S(1)} %all-to-all-done.refs_0_), channel_id=1, source_target_pairs={{0,4},{4,0},{1,5},{5,1},{2,6},{6,2},{3,7},{7,3},{8,12},{12,8},{9,1... | collective-permute-start | bytes 491528 | tf_op jit(solution)/shard_map/ppermute | solution.py:492
  28.3 0.2 collective-permute-done.2.refs_1_
  28.5 1.3 %collective-permute-start.6 = (f32[8,40,128]{2,1,0:T(8,128)S(1)}, f32[8,40,128]{2,1,0:T(8,128)S(1)}, u32[]{:S(2)}, u32[]{:S(2)}) collective-permute-start(f32[8,40,128]{2,1,0:T(8,128)S(1)} %collective-permute-done.2.refs_1_), channel_id=1, source_target_pairs={{0,4},{4,0},{1,5},{5,1},{2,6},{6,2},{3,7},{7,3},{8,12},{12,8},{9,1... | collective-permute-start | bytes 491528 | tf_op jit(solution)/shard_map/ppermute | solution.py:492
  29.8 3.3 %collective-permute-done.3.refs_2_ = f32[8,40,128]{2,1,0:T(8,128)S(1)} collective-permute-done((f32[8,40,128]{2,1,0:T(8,128)S(1)}, f32[8,40,128]{2,1,0:T(8,128)S(1)}, u32[]{:S(2)}, u32[]{:S(2)}) %collective-permute-start.3) | collective-permute-done | bytes 163872 | tf_op jit(solution)/shard_map/ppermute | solution.py:491
  33.1 1.4 %collective-permute-start.7 = (f32[8,40,128]{2,1,0:T(8,128)S(1)}, f32[8,40,128]{2,1,0:T(8,128)S(1)}, u32[]{:S(2)}, u32[]{:S(2)}) collective-permute-start(f32[8,40,128]{2,1,0:T(8,128)S(1)} %collective-permute-done.3.refs_2_), channel_id=1, source_target_pairs={{0,4},{4,0},{1,5},{5,1},{2,6},{6,2},{3,7},{7,3},{8,12},{12,8},{9,1... | collective-permute-start | bytes 491528 | tf_op jit(solution)/shard_map/ppermute | solution.py:492
  34.5 0.0 collective-permute-done.4.refs_3_
  34.5 0.3 collective-permute-start.8
  34.8 0.0 collective-permute-done.5.refs_4_
  34.8 0.0 collective-permute-done.6.refs_5_
  34.8 0.0 copy-start.5
  34.8 0.7 collective-permute-done.7.refs_6_
  35.5 0.4 collective-permute-done.8.refs_7_
  35.9 0.0 copy-done
  35.9 0.0 copy-done.1
  35.9 0.0 copy-done.2
  35.9 0.0 copy-done.3
  35.9 0.0 copy-done.4
  36.0 0.0 copy-done.5
  36.0 0.2 copy-done.6
  36.2 0.7 copy-done.7
  36.9 10.2 %fields.1 = (f32[4,128,256]{2,1,0:T(8,128)S(1)}, f32[24,32,1024]{2,1,0:T(8,128)}, f32[16,2048]{1,0:T(8,128)S(1)}, f32[16,2048]{1,0:T(8,128)S(1)}, f32[32,128]{1,0:T(8,128)S(1)}, /*index=5*/f32[32,128]{1,0:T(8,128)S(1)}) custom-call(f32[8,40,128]{2,1,0:T(8,128)} %copy-done, f32[8,40,128]{2,1,0:T(8,128)} %copy-done.1, f32[8,40,128]{2,1,0:T(8,128)} %copy-done.2, ...), custom_call_target="tpu_custom_call" | custom-call | tf_op jit(solution)/shard_map/fields/pallas_call | solution.py:495
  47.1 1.3 %collective-permute-start.10 = (f32[32,128]{1,0:T(8,128)S(1)}, f32[32,128]{1,0:T(8,128)S(1)}, u32[]{:S(2)}, u32[]{:S(2)}) collective-permute-start(f32[32,128]{1,0:T(8,128)S(1)} %get-tuple-element.31), channel_id=1, source_target_pairs={{1,0},{2,1},{3,2},{5,4},{6,5},{7,6},{9,8},{10,9},{11,10},{13,12},{... | collective-permute-start | bytes 49160 | tf_op jit(solution)/shard_map/ppermute | solution.py:536
  48.4 4.2 %collective-permute-start.9 = (f32[32,128]{1,0:T(8,128)S(1)}, f32[32,128]{1,0:T(8,128)S(1)}, u32[]{:S(2)}, u32[]{:S(2)}) collective-permute-start(f32[32,128]{1,0:T(8,128)S(1)} %get-tuple-element.30), channel_id=1, source_target_pairs={{0,1},{1,2},{2,3},{4,5},{5,6},{6,7},{8,9},{9,10},{10,11},{12,13},{... | collective-permute-start | bytes 49160 | tf_op jit(solution)/shard_map/ppermute | solution.py:535
  53.2 0.0 collective-permute-done.10.right_ref
  53.2 0.0 collective-permute-done.9.left_ref
  53.3 11.5 %resist.1 = (f32[8,2048]{1,0:T(8,128)}, f32[64,8,384]{2,1,0:T(8,128)}) custom-call(f32[16,2048]{1,0:T(8,128)S(1)} %get-tuple-element.28.field_ref, f32[16,2048]{1,0:T(8,128)S(1)} %get-tuple-element.29.target_ref, f32[32,128]{1,0:T(8,128)S(1)} %collective-permute-done.9.left_ref, f32[32,128]{1,0:T(8,128)S(1)} %collective-permute-done.10.right_ref, ...), custom_call_target="tpu_custom_call" | custom-call | tf_op jit(solution)/shard_map/resist/pallas_call | solution.py:320
  64.8 8.9 %all-to-all-start.1 = ((f32[64,8,384]{2,1,0:T(8,128)}), f32[64,8,384]{2,1,0:T(8,128)S(1)}, u32[]{:S(2)}, u32[]{:S(2)}) async-start(f32[64,8,384]{2,1,0:T(8,128)} %get-tuple-element.38), calls=%async_computation.1 | async-start | bytes 1572864 | tf_op jit(solution)/shard_map/all_to_all | solution.py:543
  73.7 0.0 copy-start.8
  73.7 0.2 dynamic-slice_bitcast_fusion.1
  73.9 0.1 copy.42
  74.0 0.1 copy.43
  74.1 22.5 %all-to-all-done.1 = f32[64,8,384]{2,1,0:T(8,128)S(1)} async-done(((f32[64,8,384]{2,1,0:T(8,128)}), f32[64,8,384]{2,1,0:T(8,128)S(1)}, u32[]{:S(2)}, u32[]{:S(2)}) %all-to-all-start.1) | async-done | bytes 786464 | tf_op jit(solution)/shard_map/all_to_all | solution.py:543
  96.7 0.2 copy.50
  96.8 0.8 convolution_bitcast_fusion
  97.7 0.0 copy-start.11
  97.7 0.0 copy-start.12
  97.7 0.1 copy.40
  97.8 0.6 copy-done.11
  98.3 0.0 copy-done.12
  98.4 0.6 subtract_reduce_fusion
  99.0 0.1 add_reduce_fusion.1
  99.1 3.6 %collective-permute-start.11 = (f32[2,2,24,128]{3,2,1,0:T(8,128)S(1)}, f32[2,2,24,128]{3,2,1,0:T(8,128)S(1)}, u32[]{:S(2)}, u32[]{:S(2)}) collective-permute-start(f32[2,2,24,128]{3,2,1,0:T(8,128)S(1)} %pad_maximum_fusion), channel_id=1, source_target_pairs={{0,2},{1,3},{2,0},{3,1},{4,6},{5,7},{6,4},{7,5},{8,10},{9,11},{10,... | collective-permute-start | bytes 147464 | tf_op jit(solution)/shard_map/ppermute | solution.py:24
  102.8 0.6 collective-permute-start.12
  103.4 2.1 %collective-permute-start.13 = (f32[2,2,24,128]{3,2,1,0:T(8,128)S(1)}, f32[2,2,24,128]{3,2,1,0:T(8,128)S(1)}, u32[]{:S(2)}, u32[]{:S(2)}) collective-permute-start(f32[2,2,24,128]{3,2,1,0:T(8,128)S(1)} %pad_maximum_fusion), channel_id=1, source_target_pairs={{0,3},{1,0},{2,1},{3,2},{4,7},{5,4},{6,5},{7,6},{8,11},{9,8},{10,9... | collective-permute-start | bytes 147464 | tf_op jit(solution)/shard_map/ppermute | solution.py:24
  105.4 0.0 collective-permute-done.11
  105.4 1.5 %collective-permute-done.12 = f32[2,2,24,128]{3,2,1,0:T(8,128)S(1)} collective-permute-done((f32[2,2,24,128]{3,2,1,0:T(8,128)S(1)}, f32[2,2,24,128]{3,2,1,0:T(8,128)S(1)}, u32[]{:S(2)}, u32[]{:S(2)}) %collective-permute-start.12) | collective-permute-done | bytes 49184 | tf_op jit(solution)/shard_map/ppermute | solution.py:24
  106.9 0.0 collective-permute-done.13
  106.9 0.6 multiply_reduce_fusion
  107.5 0.7 broadcast_in_dim_broadcast_in_dim_broadcast_in_dim.3
  108.2 16.7 %all_to_all.15 = f32[64,1,128]{2,1,0:T(1,128)S(1)} all-to-all(f32[64,1,128]{2,1,0:T(1,128)S(1)} %broadcast_in_dim_broadcast_in_dim_broadcast_in_dim.3), channel_id=1, replica_groups=mesh['y'=4,'z'=8,'core'=2,'x'=4] {'y','z','core'}, dimensions={0} | all-to-all | bytes 65536 | tf_op jit(solution)/shard_map/all_to_all | solution.py:20
  124.9 0.7 slice_reduce_fusion
  126.3 0.6 copy.47
  (13 shorter events, 0.0 us)
Async XLA Ops:
  2.6 19.3 %all-to-all-start = ((f32[8,40,128]{2,1,0:T(8,128)}), f32[8,40,128]{2,1,0:T(8,128)S(1)}, u32[]{:S(2)}, u32[]{:S(2)}) async-start(f32[8,40,128]{2,1,0:T(8,128)} %analyse.1), calls=%async_computation | async-start | bytes 327680 | tf_op jit(solution)/shard_map/all_to_all | solution.py:489
  11.6 8.5 %collective-permute-start = (bf16[8,2048]{1,0:T(8,128)(2,1)}, bf16[8,2048]{1,0:T(8,128)(2,1)S(1)}, u32[]{:S(2)}, u32[]{:S(2)}) collective-permute-start(bf16[8,2048]{1,0:T(8,128)(2,1)} %refs_15_.1), channel_id=1, source_target_pairs={{0,4},{4,8},{8,12},{12,16},{16,20},{20,24},{24,28},{28,32},{32,36}... | collective-permute-start | bytes 98312 | tf_op jit(solution)/shard_map/ppermute | solution.py:472
  16.1 5.7 %collective-permute-start.1 = (bf16[8,2048]{1,0:T(8,128)(2,1)}, bf16[8,2048]{1,0:T(8,128)(2,1)S(1)}, u32[]{:S(2)}, u32[]{:S(2)}) collective-permute-start(bf16[8,2048]{1,0:T(8,128)(2,1)} %refs_15_.1), channel_id=1, source_target_pairs={{4,0},{8,4},{12,8},{16,12},{20,16},{24,20},{28,24},{32,28},{36,32}... | collective-permute-start | bytes 98312 | tf_op jit(solution)/shard_map/ppermute | solution.py:473
  20.1 15.8 %copy-start.9 = (bf16[8,2048]{1,0:T(8,128)(2,1)}, bf16[8,2048]{1,0:T(8,128)(2,1)S(1)}, u32[]{:S(2)}) copy-start(bf16[8,2048]{1,0:T(8,128)(2,1)S(1)} %collective-permute-done.refs_16_) | copy-start | bytes 98308
  21.8 14.1 %copy-start.10 = (bf16[8,2048]{1,0:T(8,128)(2,1)}, bf16[8,2048]{1,0:T(8,128)(2,1)S(1)}, u32[]{:S(2)}) copy-start(bf16[8,2048]{1,0:T(8,128)(2,1)S(1)} %collective-permute-done.1.refs_17_) | copy-start | bytes 98308
  21.8 14.1 %copy-start = (f32[8,40,128]{2,1,0:T(8,128)}, f32[8,40,128]{2,1,0:T(8,128)S(1)}, u32[]{:S(2)}) copy-start(f32[8,40,128]{2,1,0:T(8,128)S(1)} %all-to-all-done.refs_0_) | copy-start | bytes 491524
  21.8 6.6 %collective-permute-start.2 = (f32[8,40,128]{2,1,0:T(8,128)S(1)}, f32[8,40,128]{2,1,0:T(8,128)S(1)}, u32[]{:S(2)}, u32[]{:S(2)}) collective-permute-start(f32[8,40,128]{2,1,0:T(8,128)S(1)} %all-to-all-done.refs_0_), channel_id=1, source_target_pairs={{0,64},{64,128},{128,192},{192,0},{1,65},{65,129},{129,193},{193,1... | collective-permute-start | bytes 491528 | tf_op jit(solution)/shard_map/ppermute | solution.py:491
  23.2 9.9 %collective-permute-start.3 = (f32[8,40,128]{2,1,0:T(8,128)S(1)}, f32[8,40,128]{2,1,0:T(8,128)S(1)}, u32[]{:S(2)}, u32[]{:S(2)}) collective-permute-start(f32[8,40,128]{2,1,0:T(8,128)S(1)} %all-to-all-done.refs_0_), channel_id=1, source_target_pairs={{0,128},{64,192},{128,0},{192,64},{1,129},{65,193},{129,1},{193,65... | collective-permute-start | bytes 491528 | tf_op jit(solution)/shard_map/ppermute | solution.py:491
  25.8 8.7 %collective-permute-start.4 = (f32[8,40,128]{2,1,0:T(8,128)S(1)}, f32[8,40,128]{2,1,0:T(8,128)S(1)}, u32[]{:S(2)}, u32[]{:S(2)}) collective-permute-start(f32[8,40,128]{2,1,0:T(8,128)S(1)} %all-to-all-done.refs_0_), channel_id=1, source_target_pairs={{0,192},{64,0},{128,64},{192,128},{1,193},{65,1},{129,65},{193,129... | collective-permute-start | bytes 491528 | tf_op jit(solution)/shard_map/ppermute | solution.py:491
  26.9 7.9 %collective-permute-start.5 = (f32[8,40,128]{2,1,0:T(8,128)S(1)}, f32[8,40,128]{2,1,0:T(8,128)S(1)}, u32[]{:S(2)}, u32[]{:S(2)}) collective-permute-start(f32[8,40,128]{2,1,0:T(8,128)S(1)} %all-to-all-done.refs_0_), channel_id=1, source_target_pairs={{0,4},{4,0},{1,5},{5,1},{2,6},{6,2},{3,7},{7,3},{8,12},{12,8},{9,1... | collective-permute-start | bytes 491528 | tf_op jit(solution)/shard_map/ppermute | solution.py:492
  28.5 7.4 %copy-start.1 = (f32[8,40,128]{2,1,0:T(8,128)}, f32[8,40,128]{2,1,0:T(8,128)S(1)}, u32[]{:S(2)}) copy-start(f32[8,40,128]{2,1,0:T(8,128)S(1)} %collective-permute-done.2.refs_1_) | copy-start | bytes 491524
  28.5 6.3 %collective-permute-start.6 = (f32[8,40,128]{2,1,0:T(8,128)S(1)}, f32[8,40,128]{2,1,0:T(8,128)S(1)}, u32[]{:S(2)}, u32[]{:S(2)}) collective-permute-start(f32[8,40,128]{2,1,0:T(8,128)S(1)} %collective-permute-done.2.refs_1_), channel_id=1, source_target_pairs={{0,4},{4,0},{1,5},{5,1},{2,6},{6,2},{3,7},{7,3},{8,12},{12,8},{9,1... | collective-permute-start | bytes 491528 | tf_op jit(solution)/shard_map/ppermute | solution.py:492
  33.1 2.8 %copy-start.2 = (f32[8,40,128]{2,1,0:T(8,128)}, f32[8,40,128]{2,1,0:T(8,128)S(1)}, u32[]{:S(2)}) copy-start(f32[8,40,128]{2,1,0:T(8,128)S(1)} %collective-permute-done.3.refs_2_) | copy-start | bytes 491524
  33.1 2.4 %collective-permute-start.7 = (f32[8,40,128]{2,1,0:T(8,128)S(1)}, f32[8,40,128]{2,1,0:T(8,128)S(1)}, u32[]{:S(2)}, u32[]{:S(2)}) collective-permute-start(f32[8,40,128]{2,1,0:T(8,128)S(1)} %collective-permute-done.3.refs_2_), channel_id=1, source_target_pairs={{0,4},{4,0},{1,5},{5,1},{2,6},{6,2},{3,7},{7,3},{8,12},{12,8},{9,1... | collective-permute-start | bytes 491528 | tf_op jit(solution)/shard_map/ppermute | solution.py:492
  34.5 1.4 %copy-start.3 = (f32[8,40,128]{2,1,0:T(8,128)}, f32[8,40,128]{2,1,0:T(8,128)S(1)}, u32[]{:S(2)}) copy-start(f32[8,40,128]{2,1,0:T(8,128)S(1)} %collective-permute-done.4.refs_3_) | copy-start | bytes 491524
  34.5 1.4 %collective-permute-start.8 = (f32[8,40,128]{2,1,0:T(8,128)S(1)}, f32[8,40,128]{2,1,0:T(8,128)S(1)}, u32[]{:S(2)}, u32[]{:S(2)}) collective-permute-start(f32[8,40,128]{2,1,0:T(8,128)S(1)} %collective-permute-done.4.refs_3_), channel_id=1, source_target_pairs={{0,4},{4,0},{1,5},{5,1},{2,6},{6,2},{3,7},{7,3},{8,12},{12,8},{9,1... | collective-permute-start | bytes 491528 | tf_op jit(solution)/shard_map/ppermute | solution.py:492
  34.8 1.2 copy-start.4
  34.8 1.2 copy-start.5
  35.5 0.7 copy-start.6
  36.2 0.7 copy-start.7
  47.1 6.2 %collective-permute-start.10 = (f32[32,128]{1,0:T(8,128)S(1)}, f32[32,128]{1,0:T(8,128)S(1)}, u32[]{:S(2)}, u32[]{:S(2)}) collective-permute-start(f32[32,128]{1,0:T(8,128)S(1)} %get-tuple-element.31), channel_id=1, source_target_pairs={{1,0},{2,1},{3,2},{5,4},{6,5},{7,6},{9,8},{10,9},{11,10},{13,12},{... | collective-permute-start | bytes 49160 | tf_op jit(solution)/shard_map/ppermute | solution.py:536
  48.4 4.9 %collective-permute-start.9 = (f32[32,128]{1,0:T(8,128)S(1)}, f32[32,128]{1,0:T(8,128)S(1)}, u32[]{:S(2)}, u32[]{:S(2)}) collective-permute-start(f32[32,128]{1,0:T(8,128)S(1)} %get-tuple-element.30), channel_id=1, source_target_pairs={{0,1},{1,2},{2,3},{4,5},{5,6},{6,7},{8,9},{9,10},{10,11},{12,13},{... | collective-permute-start | bytes 49160 | tf_op jit(solution)/shard_map/ppermute | solution.py:535
  64.8 31.9 %all-to-all-start.1 = ((f32[64,8,384]{2,1,0:T(8,128)}), f32[64,8,384]{2,1,0:T(8,128)S(1)}, u32[]{:S(2)}, u32[]{:S(2)}) async-start(f32[64,8,384]{2,1,0:T(8,128)} %get-tuple-element.38), calls=%async_computation.1 | async-start | bytes 1572864 | tf_op jit(solution)/shard_map/all_to_all | solution.py:543
  73.7 23.1 %copy-start.8 = (f32[2,64,256,1,1]{2,1,0,4,3:T(8,128)S(1)}, f32[2,64,256,1,1]{2,1,0,4,3:T(8,128)}, u32[]{:S(2)}) copy-start(f32[2,64,256,1,1]{2,1,0,4,3:T(8,128)} %constant.75) | copy-start | bytes 393220
  97.7 0.7 copy-start.11
  97.7 0.7 copy-start.12
  99.1 6.3 %collective-permute-start.11 = (f32[2,2,24,128]{3,2,1,0:T(8,128)S(1)}, f32[2,2,24,128]{3,2,1,0:T(8,128)S(1)}, u32[]{:S(2)}, u32[]{:S(2)}) collective-permute-start(f32[2,2,24,128]{3,2,1,0:T(8,128)S(1)} %pad_maximum_fusion), channel_id=1, source_target_pairs={{0,2},{1,3},{2,0},{3,1},{4,6},{5,7},{6,4},{7,5},{8,10},{9,11},{10,... | collective-permute-start | bytes 147464 | tf_op jit(solution)/shard_map/ppermute | solution.py:24
  102.8 4.2 %collective-permute-start.12 = (f32[2,2,24,128]{3,2,1,0:T(8,128)S(1)}, f32[2,2,24,128]{3,2,1,0:T(8,128)S(1)}, u32[]{:S(2)}, u32[]{:S(2)}) collective-permute-start(f32[2,2,24,128]{3,2,1,0:T(8,128)S(1)} %pad_maximum_fusion), channel_id=1, source_target_pairs={{0,1},{1,2},{2,3},{3,0},{4,5},{5,6},{6,7},{7,4},{8,9},{9,10},{10,1... | collective-permute-start | bytes 147464 | tf_op jit(solution)/shard_map/ppermute | solution.py:24
  103.4 3.5 %collective-permute-start.13 = (f32[2,2,24,128]{3,2,1,0:T(8,128)S(1)}, f32[2,2,24,128]{3,2,1,0:T(8,128)S(1)}, u32[]{:S(2)}, u32[]{:S(2)}) collective-permute-start(f32[2,2,24,128]{3,2,1,0:T(8,128)S(1)} %pad_maximum_fusion), channel_id=1, source_target_pairs={{0,3},{1,0},{2,1},{3,2},{4,7},{5,4},{6,5},{7,6},{8,11},{9,8},{10,9... | collective-permute-start | bytes 147464 | tf_op jit(solution)/shard_map/ppermute | solution.py:24
where the time goes:
time: 127 us
  starting transfers between devices  45.6 us (36%)
  waiting for transfers between devices  30.3 us (24%)
  Pallas kernels  25.7 us (20%)
  blocking collectives  16.7 us (13%)
  local copies, waits for them, and re-layouts  3.54 us (3%)
  between operations  2.24 us (2%)
  other arithmetic  2.04 us (2%)
    all_to_all x1, waiting for transfers between devices, on_device(): got = lax.all_to_all(send, ROW, 0, 0, tiled=True)  22.5 us
    all_to_all x1, blocking collectives, gather_on(): lax.all_to_all(jnp.broadcast_to(x[None], (n,) + x.shape), axes, 0, 0, til...  16.7 us
    pallas_call x1, Pallas kernels, resist_block(): pl.pallas_call(functools.partial(resist_kernel, rows=rows, cols=cols), ou...  11.5 us
    pallas_call x1, Pallas kernels, on_device(): pl.pallas_call(functools.partial(fields_kernel, rows=rows), out_shape=[ja...  10.2 us
    all_to_all x1, starting transfers between devices, on_device(): gathered = lax.all_to_all(packed, 'z', 0, 0, tiled=True)  9.03 us
    all_to_all x1, starting transfers between devices, on_device(): got = lax.all_to_all(send, ROW, 0, 0, tiled=True)  8.89 us
    ppermute x3, starting transfers between devices, sum_cols(): lax.ppermute(x, 'x', [(i, (i + k) % 4) for i in range(4)])  6.31 us
    ppermute x3, starting transfers between devices, on_device(): lax.ppermute(gathered, 'y', [(i, (i + k) % 4) for i in range(4)])  5.06 us
  transfers between devices with their start and end apart: 16, of which 7 were waited for; matrix products, arithmetic and copies ran while one was open for 0% of the time, Pallas kernels for 2%

commit v1 on v0

--- a/solution.py
+++ b/solution.py
@@ -13,16 +13,6 @@
 BAND = 128
 ROW = ("y", "z", "core")
 ALL = ("y", "z", "core", "x")
-HIGH = lax.Precision.HIGH
-
-
-def gather_on(x, axes, n):
-    return lax.all_to_all(jnp.broadcast_to(x[None], (n,) + x.shape), axes, 0, 0, tiled=True)
-
-
-def sum_cols(x):
-    one, two, three = (lax.ppermute(x, "x", [(i, (i + k) % 4) for i in range(4)]) for k in (1, 2, 3))
-    return (x + two) + (one + three)
 
 
 def phase_angles(freqs, positions):
@@ -42,6 +32,10 @@
 VMEM = pl.BlockSpec(memory_space=pltpu.VMEM)
 SMEM = pl.BlockSpec(memory_space=pltpu.SMEM)
 HERE = pl.BlockSpec(memory_space=pltpu.HBM)
+
+
+def near(*arrays):
+    return [pltpu.with_memory_space_constraint(jnp.asarray(x), pltpu.VMEM) for x in arrays]
 
 
 def homes(*arrays):
@@ -81,23 +75,19 @@
     return np.stack(tables)
 
 
-def expand_table(tiles, norm):
-    table = np.zeros((tiles + 1, 2, BAND, 2, BAND))
+def expand_table(norm):
+    table = np.zeros((2, BAND, 2, BAND))
     for g in range(BAND):
         q = g - 64
         m = abs(q)
         if m < 64:
-            table[0, 0, m, 0, g] = 1.0
-            table[0, 1, m, 1, g] = -1.0
-        else:
-            for t in range(tiles):
-                table[1 + t, 0, t, 0, g] = 1.0
-                table[1 + t, 1, t, 1, g] = -1.0
+            table[0, m, 0, g] = 1.0
+            table[1, m, 1, g] = -1.0
         if m:
             sign = -1.0 if q > 0 else 1.0
-            table[0, 1, 63 + m, 0, g] = sign
-            table[0, 0, 63 + m, 1, g] = sign
-    return (table.reshape(tiles + 1, 2 * BAND, 2 * BAND) * norm).astype(jnp.bfloat16)
+            table[1, 63 + m, 0, g] = sign
+            table[0, 63 + m, 1, g] = sign
+    return (table.reshape(2 * BAND, 2 * BAND) * norm).astype(jnp.bfloat16)
 
 
 def synthesis_table(norm):
@@ -233,11 +223,11 @@
 
 def resist_kernel(
     field_ref, target_ref, left_ref, right_ref, first_ref, second_ref, second_back_ref, first_back_ref, offset_ref,
-    weights_any, fields_any, back_any,
-    resist_ref, out_ref, weights_ref, fields_ref, back_ref,
+    fields_ref, weights_any, back_any,
+    resist_ref, out_ref, weights_ref, back_ref,
     views_ref, keep_ref, mixed_ref, spread_ref, summed_ref, all_ref, sems, *, rows, cols
 ):
-    copies = fetch((weights_any, fields_any, back_any), (weights_ref, fields_ref, back_ref), sems)
+    copies = fetch((weights_any, back_any), (weights_ref, back_ref), sems)
     row0 = lax.axis_index(ROW) * resist_ref.shape[0]
     col0 = lax.axis_index("x") * resist_ref.shape[1]
     width = resist_ref.shape[1]
@@ -310,8 +300,10 @@
     low = lax.broadcasted_iota(jnp.int32, (8, 384), 0) < 4
     for d in range(32):
         first, second = all_ref[8 * d : 8 * d + 8, 0:384], all_ref[8 * d : 8 * d + 8, 384:768]
-        out_ref[2 * d] = jnp.where(low, first, pltpu.roll(second, 4, 0))
-        out_ref[2 * d + 1] = jnp.where(low, pltpu.roll(first, 4, 0), second)
+        even, odd = jnp.where(low, first, pltpu.roll(second, 4, 0)), jnp.where(low, pltpu.roll(first, 4, 0), second)
+        for b in range(3):
+            out_ref[2 * d, 8 * b : 8 * b + 8] = even[:, BAND * b : BAND * (b + 1)]
+            out_ref[2 * d + 1, 8 * b : 8 * b + 8] = odd[:, BAND * b : BAND * (b + 1)]
 
 
 def resist_block(field, target, left, right, tables, second_bias, weights, fields, back, dims):
@@ -319,12 +311,11 @@
     inner, width = tables[2].shape[0], field.shape[1]
     return pl.pallas_call(
         functools.partial(resist_kernel, rows=rows, cols=cols),
-        out_shape=[jax.ShapeDtypeStruct((8, width), jnp.float32), jax.ShapeDtypeStruct((64, 8, 384), jnp.float32)],
-        in_specs=[VMEM] * 8 + [SMEM] + [HERE] * 3,
+        out_shape=[jax.ShapeDtypeStruct((8, width), jnp.float32), jax.ShapeDtypeStruct((64, 24, BAND), jnp.float32)],
+        in_specs=[VMEM] * 8 + [SMEM, VMEM] + [HERE] * 2,
         out_specs=[VMEM] * 2,
         scratch_shapes=[
             pltpu.SMEM(weights.shape, jnp.float32),
-            pltpu.VMEM(fields.shape, jnp.float32),
             pltpu.VMEM(back.shape, jnp.bfloat16),
             pltpu.VMEM((160, WIDE), jnp.bfloat16),
             pltpu.VMEM((inner, WIDE), jnp.float32),
@@ -332,11 +323,11 @@
             pltpu.VMEM((144, WIDE), jnp.bfloat16),
             pltpu.VMEM((32, WIDE), jnp.float32),
             pltpu.VMEM((256, 768), jnp.float32),
-            pltpu.SemaphoreType.DMA((3,)),
+            pltpu.SemaphoreType.DMA((2,)),
         ],
         compiler_params=params(28),
         name="resist",
-    )(field, target, left, right, *tables, second_bias, *homes(weights, fields, back))
+    )(field, target, left, right, *tables, second_bias, *near(fields), *homes(weights, back))
 
 
 def analyse_kernel(layout_any, table_any, out_ref, layout_ref, table_ref, sems):
@@ -354,31 +345,32 @@
         out_ref[i] = packed
 
 
-def fields_kernel(*refs, rows):
-    slab_any, refs = refs[:8], refs[8:]
-    (
-        rows_any, expand_any, line_any, synth_any, real_any, imag_any, weights_any, target_any, above_any, below_any,
-        spec_ref, fields_any, intensity_ref, wanted_ref, first_edge_ref, last_edge_ref, *refs
-    ) = refs
+def fields_kernel(*refs, rows, norm):
     slabs, refs = refs[:8], refs[8:]
     (
-        rows_ref, expand_ref, line_ref, synth_ref, real_ref, imag_ref, weights_ref, target_ref, above_ref, below_ref,
-        fields_ref, seen_ref, line_hi_ref, line_lo_ref, sum_ref, sems, out_sems
+        target_ref, above_ref, below_ref, rows_any, expand_any, line_any, weights_any, synth_any, real_any, imag_any,
+        cols_ref, fields_ref, intensity_ref, wanted_ref, first_edge_ref, last_edge_ref, *refs
+    ) = refs
+    (
+        rows_ref, expand_ref, line_ref, weights_ref, synth_ref, real_ref, imag_ref,
+        spec_ref, seen_ref, line_hi_ref, line_lo_ref, sum_ref, sems
     ) = refs
     at = 2 * lax.axis_index("y") + lax.axis_index("core")
     r = lax.axis_index(ROW)
-    sources = (*slab_any, rows_any.at[at], expand_any, line_any.at[r], synth_any, real_any, imag_any, weights_any, target_any, above_any, below_any)
-    targets = (*slabs, rows_ref, expand_ref, line_ref, synth_ref, real_ref, imag_ref, weights_ref, target_ref, above_ref, below_ref)
+    sources = [rows_any.at[at], expand_any, line_any.at[r], weights_any, synth_any]
+    targets = [rows_ref, expand_ref, line_ref, weights_ref, synth_ref]
+    for i in range(0, real_ref.shape[0], 4):
+        sources += [real_any.at[i : i + 4], imag_any.at[i : i + 4]]
+        targets += [real_ref.at[i : i + 4], imag_ref.at[i : i + 4]]
     copies = fetch(sources, targets, sems)
     row0 = r * 8
     kernels = real_ref.shape[0]
     for p, slab in enumerate(slabs):
-        copies[p].wait()
         for t in range(5):
             hi, lo = halves(slab[:, 8 * t : 8 * t + 8, :].reshape(64, BAND))
             seen_ref[64 * p : 64 * p + 64, t * BAND : (t + 1) * BAND] = hi
             seen_ref[rows + 64 * p : rows + 64 * p + 64, t * BAND : (t + 1) * BAND] = lo
-    copies[8].wait()
+    copies[0].wait()
     table_hi = rows_ref[0 : 2 * BAND]
     u = dot(table_hi, seen_ref[0:rows]) + dot(rows_ref[2 * BAND :], seen_ref[0:rows]) + dot(table_hi, seen_ref[rows:])
 
@@ -386,16 +378,16 @@
         both = u[:, t * BAND : (t + 1) * BAND]
         return halves(jnp.concatenate([both[:BAND], both[BAND:]], 1))
 
-    copies[9].wait()
-    last_hi, last_lo = pair(4)
+    copies[1].wait()
+    lane = lax.broadcasted_iota(jnp.int32, (BAND, 2 * BAND), 1)
+    last = u[:, 4 * BAND :] * norm
     for t in range(4):
         hi, lo = pair(t)
-        spec_ref[t] = (
-            dot(hi, expand_ref[0]) + dot(lo, expand_ref[0]) + dot(last_hi, expand_ref[1 + t]) + dot(last_lo, expand_ref[1 + t])
-        )
-
-    for copy in copies[10:]:
-        copy.wait()
+        moved = pltpu.roll(last, (BAND - t) % BAND, 1)
+        moved = jnp.concatenate([moved[:BAND], -moved[BAND:]], 1)
+        spec_ref[t] = dot(hi, expand_ref[...]) + dot(lo, expand_ref[...]) + jnp.where((lane == 0) | (lane == BAND), moved, 0.0)
+
+    copies[2].wait()
     phase = line_ref[...]
     c, s = phase[:, :BAND], phase[:, BAND:]
     table = jnp.concatenate([jnp.concatenate([c, -s], 1), jnp.concatenate([s, c], 1)], 0)
@@ -432,16 +424,27 @@
             fields_ref[k0 + j, :, here] = jnp.concatenate([part[16 * t : 16 * t + 8] for t in range(4)], 0)
         sum_ref[:, here] = total
 
-    sent = []
+    for copy in copies[5:7]:
+        copy.wait()
     for j in range(4):
         lines(j, 0, j)
+    for copy in copies[3:5]:
+        copy.wait()
     for i in range(kernels // 4):
+        for copy in copies[7 + 2 * i : 9 + 2 * i]:
+            copy.wait()
         for j in range(4):
             waves(4 * i, i % 2, j)
             if 4 * i + 4 < kernels:
                 lines(4 * i + 4 + j, (i + 1) % 2, j)
-        sent.append(pltpu.make_async_copy(fields_ref.at[4 * i : 4 * i + 4], fields_any.at[4 * i : 4 * i + 4], out_sems.at[i]))
-        sent[-1].start()
+    row = lax.broadcasted_iota(jnp.int32, (16, 2 * BAND), 0)
+    lane = lax.broadcasted_iota(jnp.int32, (16, 2 * BAND), 1)
+    chosen = ((row < 4) & (lane == 2 * r + row % 2 + BAND * (row // 2))).astype(jnp.bfloat16)
+    for t in range(4):
+        hi, lo = halves(spec_ref[t])
+        sides = (((1,), (1,)), ((), ()))
+        picked = lax.dot_general(chosen, hi, sides, preferred_element_type=jnp.float32)
+        cols_ref[t] = (picked + lax.dot_general(chosen, lo, sides, preferred_element_type=jnp.float32))[:8]
     slot = lax.broadcasted_iota(jnp.int32, (16, TILE), 0)
     n = row0 + jnp.where(slot < 8, slot, jnp.where(slot < 12, slot - 12, slot - 4))
     inside = (n >= 0) & (n < rows)
@@ -455,8 +458,97 @@
     for i, ref in ((0, intensity_ref), (16, wanted_ref)):
         first_edge_ref[i : i + 16] = ref[:, 0:BAND]
         last_edge_ref[i : i + 16] = ref[:, width - BAND :]
-    for copy in sent:
+
+
+def adjoint_tables():
+    wide = phase_angles(8 * np.arange(64), FREQ)
+    c, s = np.cos(wide), np.sin(wide)
+    w = np.concatenate([np.concatenate([c, -s], 1), np.concatenate([s, c], 1)], 0)
+    near_rows = phase_angles(np.arange(8), FREQ)
+    return np.concatenate(constant_split(w), 0), np.concatenate([np.cos(near_rows), np.sin(near_rows)], 0).astype(np.float32)
+
+
+def adjoint_kernel(got_ref, columns_ref, table_any, turn_any, out_ref, table_ref, turn_ref, sems):
+    for copy in fetch((table_any, turn_any), (table_ref, turn_ref), sems):
         copy.wait()
+    table_hi, table_lo = table_ref[0:BAND], table_ref[BAND:]
+    c, s = turn_ref[0:8], turn_ref[8:16]
+    for g in range(2):
+        turned = []
+        for t in range(4):
+            re, im = columns_ref[t, g : g + 1], columns_ref[t, 2 + g : 3 + g]
+            turned.append((c * re - s * im, s * re + c * im))
+        a, b = (jnp.concatenate([x[i] for x in turned], 0)[None] for i in range(2))
+        for h in range(2):
+            at = 4 * h + 2 * g
+            x = [[got_ref[pl.ds(8 * b + at + i, 64, stride=24), :] for b in range(3)] for i in range(2)]
+            x = jnp.concatenate([jnp.concatenate(part, 1) for part in x], 0)
+            hi, lo = halves(x)
+            sides = (((0,), (0,)), ((), ()))
+            y = lax.dot_general(hi, table_hi, sides, preferred_element_type=jnp.float32)
+            y = y + lax.dot_general(lo, table_hi, sides, preferred_element_type=jnp.float32)
+            y = y + lax.dot_general(hi, table_lo, sides, preferred_element_type=jnp.float32)
+            y = y.reshape(12, 32, 2 * BAND)
+            re, im = y[:, :, :BAND], y[:, :, BAND:]
+            out_ref[0, g, 12 * h : 12 * h + 12] = jnp.sum(re * a + im * b, 1)
+            out_ref[1, g, 12 * h : 12 * h + 12] = jnp.sum(im * a - re * b, 1)
+
+
+def total_kernel(x_ref, one_ref, two_ref, three_ref, whole_ref, square_ref):
+    whole = (x_ref[...] + two_ref[...]) + (one_ref[...] + three_ref[...])
+    whole_ref[...] = whole
+    flat = jnp.sum(whole * whole, (0, 1, 2))[None]
+    square_ref[...] = jnp.broadcast_to(flat[None], square_ref.shape)
+
+
+def scale_kernel(whole_ref, squares_ref, out_ref, *, entries):
+    total = jnp.sum(jnp.sum(squares_ref[...], 0), 1, keepdims=True)
+    factor = lax.rsqrt(total / entries + 1e-06)
+    for i in range(2):
+        for g in range(2):
+            out_ref[i, :, g, :] = whole_ref[i, g] * factor
+
+
+def fields_block(slabs, synth, kernel_real, kernel_imaginary, weights, target, above, below, norm):
+    kernels = kernel_real.shape[0]
+    height, width = target.shape
+    tiles, rows = width // TILE, 64 * height
+    return pl.pallas_call(
+        functools.partial(fields_kernel, rows=rows, norm=norm),
+        out_shape=[
+            jax.ShapeDtypeStruct((tiles, 8, BAND), jnp.float32),
+            pltpu.VMEM((kernels, tiles * height, 2 * TILE), jnp.float32),
+            jax.ShapeDtypeStruct((16, width), jnp.float32),
+            jax.ShapeDtypeStruct((16, width), jnp.float32),
+            jax.ShapeDtypeStruct((32, BAND), jnp.float32),
+            jax.ShapeDtypeStruct((32, BAND), jnp.float32),
+        ],
+        in_specs=[VMEM] * 11 + [HERE] * 7,
+        out_specs=[VMEM] * 6,
+        scratch_shapes=[
+            pltpu.VMEM((4 * BAND, rows), jnp.bfloat16),
+            pltpu.VMEM((2 * BAND, 2 * BAND), jnp.bfloat16),
+            pltpu.VMEM((16, 2 * BAND), jnp.float32),
+            pltpu.SMEM(weights.shape, jnp.float32),
+            pltpu.VMEM((4 * BAND, 2 * TILE), jnp.bfloat16),
+            pltpu.VMEM(kernel_real.shape, jnp.float32),
+            pltpu.VMEM(kernel_real.shape, jnp.float32),
+            pltpu.VMEM((tiles, BAND, 2 * BAND), jnp.float32),
+            pltpu.VMEM((2 * rows, 5 * BAND), jnp.bfloat16),
+            pltpu.VMEM((2, 256, 2 * BAND), jnp.bfloat16),
+            pltpu.VMEM((2, 256, 2 * BAND), jnp.bfloat16),
+            pltpu.VMEM((64, 2 * TILE), jnp.float32),
+            pltpu.SemaphoreType.DMA((5 + kernels // 2,)),
+        ],
+        compiler_params=params(28),
+        name="fields",
+    )(
+        *near(*slabs, target, above, below),
+        *homes(
+            row_transform_tables(), expand_table(norm), line_tables(64, height), weights,
+            np.concatenate(constant_split(synth), 0), kernel_real, kernel_imaginary,
+        ),
+    )
 
 
 def on_device(
@@ -471,7 +563,6 @@
 
     above = lax.ppermute(target, ROW, [(i, i + 1) for i in range(63)])
     below = lax.ppermute(target, ROW, [(i + 1, i) for i in range(63)])
-    tables = resist_tables(first_taps, first_bias, second_taps, rows)
 
     packed = pl.pallas_call(
         analyse_kernel,
@@ -487,50 +578,14 @@
         name="analyse",
     )(*homes(layout, analysis_table()))
     gathered = lax.all_to_all(packed, "z", 0, 0, tiled=True)
+    tables = resist_tables(first_taps, first_bias, second_taps, rows)
     gathered, above, below, *tables = lax.optimization_barrier((gathered, above, below, *tables))
     slabs = [gathered] + [lax.ppermute(gathered, "y", [(i, (i + k) % 4) for i in range(4)]) for k in (1, 2, 3)]
     slabs = slabs + [lax.ppermute(slab, "core", [(0, 1), (1, 0)]) for slab in slabs]
 
     synth = synthesis_table(norm)
-    spec, fields, intensity, wanted, first_edge, last_edge = pl.pallas_call(
-        functools.partial(fields_kernel, rows=rows),
-        out_shape=[
-            jax.ShapeDtypeStruct((tiles, BAND, 2 * BAND), jnp.float32),
-            pltpu.HBM((kernels, tiles * height, 2 * TILE), jnp.float32),
-            jax.ShapeDtypeStruct((16, width), jnp.float32),
-            jax.ShapeDtypeStruct((16, width), jnp.float32),
-            jax.ShapeDtypeStruct((32, BAND), jnp.float32),
-            jax.ShapeDtypeStruct((32, BAND), jnp.float32),
-        ],
-        in_specs=[HERE] * 18,
-        out_specs=[VMEM, HERE] + [VMEM] * 4,
-        scratch_shapes=[pltpu.VMEM((8, 40, BAND), jnp.float32)] * 8
-        + [
-            pltpu.VMEM((4 * BAND, rows), jnp.bfloat16),
-            pltpu.VMEM((tiles + 1, 2 * BAND, 2 * BAND), jnp.bfloat16),
-            pltpu.VMEM((16, 2 * BAND), jnp.float32),
-            pltpu.VMEM((4 * BAND, 2 * TILE), jnp.bfloat16),
-            pltpu.VMEM(kernel_real.shape, jnp.float32),
-            pltpu.VMEM(kernel_real.shape, jnp.float32),
-            pltpu.SMEM(weights.shape, jnp.float32),
-            pltpu.VMEM(target.shape, jnp.bfloat16),
-            pltpu.VMEM(target.shape, jnp.bfloat16),
-            pltpu.VMEM(target.shape, jnp.bfloat16),
-            pltpu.VMEM((kernels, tiles * height, 2 * TILE), jnp.float32),
-            pltpu.VMEM((2 * rows, 5 * BAND), jnp.bfloat16),
-            pltpu.VMEM((2, 256, 2 * BAND), jnp.bfloat16),
-            pltpu.VMEM((2, 256, 2 * BAND), jnp.bfloat16),
-            pltpu.VMEM((64, 2 * TILE), jnp.float32),
-            pltpu.SemaphoreType.DMA((18,)),
-            pltpu.SemaphoreType.DMA((kernels // 4,)),
-        ],
-        compiler_params=params(28),
-        name="fields",
-    )(
-        *homes(
-            *slabs, row_transform_tables(), expand_table(tiles, norm), line_tables(64, height),
-            np.concatenate(constant_split(synth), 0), kernel_real, kernel_imaginary, weights, target, above, below,
-        )
+    columns, fields, intensity, wanted, first_edge, last_edge = fields_block(
+        slabs, synth, kernel_real, kernel_imaginary, weights, target, above, below, norm
     )
     left = lax.ppermute(last_edge, "x", [(i, i + 1) for i in range(3)])
     right = lax.ppermute(first_edge, "x", [(i + 1, i) for i in range(3)])
@@ -541,24 +596,39 @@
     )
 
     got = lax.all_to_all(send, ROW, 0, 0, tiled=True)
-    wide = phase_angles(height * np.arange(64), FREQ)
-    w = np.stack([np.concatenate([np.cos(wide), -np.sin(wide)], 1), np.concatenate([np.sin(wide), np.cos(wide)], 1)], 0)
-    y = jnp.einsum(
-        "shgil,isx->ghlx", got.reshape(64, 2, 2, 2, -1), w.astype(np.float32), precision=HIGH, preferred_element_type=jnp.float32
-    )
-    y = y.reshape(2, kernels, tiles, height, 2, BAND)
-    near = phase_angles(np.arange(height), FREQ)
-    nc, ns = np.cos(near).astype(np.float32), np.sin(near).astype(np.float32)
-    z_re = jnp.sum(y[..., 0, :] * nc + y[..., 1, :] * ns, 3)
-    z_im = jnp.sum(y[..., 1, :] * nc - y[..., 0, :] * ns, 3)
-    s_re = lax.dynamic_slice_in_dim(spec, 2 * r, 2, 2).transpose(2, 0, 1)[:, None]
-    s_im = lax.dynamic_slice_in_dim(spec, BAND + 2 * r, 2, 2).transpose(2, 0, 1)[:, None]
-    mine = jnp.stack([jnp.sum(z_re * s_re + z_im * s_im, 2), jnp.sum(z_im * s_re - z_re * s_im, 2)])
-    whole = sum_cols(mine)
-    squares = jnp.broadcast_to(jnp.sum(whole * whole), (1, 128))
-    total = jnp.sum(gather_on(squares, ROW, 64)[:, 0, 0])
-    entries = 2 * kernels * BAND * BAND
-    return resist, whole.transpose(0, 2, 3, 1) * lax.rsqrt(total / entries + 1e-06)
+    table, turn = adjoint_tables()
+    mine = pl.pallas_call(
+        adjoint_kernel,
+        out_shape=jax.ShapeDtypeStruct((2, 2, kernels, BAND), jnp.float32),
+        in_specs=[VMEM] * 2 + [HERE] * 2,
+        out_specs=VMEM,
+        scratch_shapes=[
+            pltpu.VMEM(table.shape, jnp.bfloat16),
+            pltpu.VMEM(turn.shape, jnp.float32),
+            pltpu.SemaphoreType.DMA((2,)),
+        ],
+        compiler_params=params(12),
+        name="adjoint",
+    )(*near(got.reshape(64 * 24, BAND), columns), *homes(table, turn))
+    others = [lax.ppermute(mine, "x", [(i, (i + k) % 4) for i in range(4)]) for k in (1, 2, 3)]
+    whole, squares = pl.pallas_call(
+        total_kernel,
+        out_shape=[jax.ShapeDtypeStruct(mine.shape, jnp.float32), jax.ShapeDtypeStruct((64, 1, BAND), jnp.float32)],
+        in_specs=[VMEM] * 4,
+        out_specs=[VMEM] * 2,
+        compiler_params=params(8),
+        name="total",
+    )(mine, *others)
+    squares = lax.all_to_all(squares, ROW, 0, 0, tiled=True)
+    grads = pl.pallas_call(
+        functools.partial(scale_kernel, entries=2 * kernels * BAND * BAND),
+        out_shape=jax.ShapeDtypeStruct((2, kernels, 2, BAND), jnp.float32),
+        in_specs=[VMEM] * 2,
+        out_specs=VMEM,
+        compiler_params=params(8),
+        name="scale",
+    )(whole, squares)
+    return resist, grads.transpose(0, 1, 3, 2)
 
 
 def solution(mesh):

time: 127 us -> 121 us (0.953)
  blocking collectives: 16.7 us -> 48.6 us
  waiting for transfers between devices: 30.3 us -> 8.72 us
  starting transfers between devices: 45.6 us -> 36 us
  local copies, waits for them, and re-layouts: 3.54 us -> 0.76 us
  other arithmetic: 2.04 us -> 0 us
    all_to_all x1 -> x2, blocking collectives: 16.7 us -> 48.6 us  [the longest x1 31.9 us: on_device(): got = lax.all_to_all(send, ROW, 0, 0, tiled=True)]
    all_to_all x1 -> x0, waiting for transfers between devices: 22.5 us -> none  [on_device(): got = lax.all_to_all(send, ROW, 0, 0, tiled=True)]
    all_to_all x1 -> x0, starting transfers between devices: 8.89 us -> none  [on_device(): got = lax.all_to_all(send, ROW, 0, 0, tiled=True)]
    reduce_sum x4 -> x0, other arithmetic: 2.03 us -> none  [the longest x1 0.67 us: on_device(): total = jnp.sum(gather_on(squares, ROW, 64)[:, 0, 0])]
    pallas_call x1, Pallas kernels: 11.5 us -> 9.72 us  [resist_block(): pl.pallas_call(functools.partial(resist_kernel, rows=rows, cols=cols), ou...]
    unnamed x27 -> x2, local copies, waits for them, and re-layouts: 2.19 us -> 0.76 us
    pallas_call x1 -> x4, Pallas kernels: 10.2 us -> 11.2 us  [the longest x1 8.53 us: fields_block(): pl.pallas_call(functools.partial(fields_kernel, rows=rows, norm=norm), ou...]
  transfers between devices with their start and end apart: 16 -> 15, of which waited for: 7 -> 6; matrix products, arithmetic and copies ran while one was open for 0% -> 0% of each run, Pallas kernels for 2% -> 2%
where the time goes in v1:
time: 121 us; the launch traced here: 120 us
  blocking collectives  48.6 us (40%)
  starting transfers between devices  36 us (30%)
  Pallas kernels  24.9 us (21%)
  waiting for transfers between devices  8.72 us (7%)
  between operations  1.4 us (1%)
    all_to_all x1, blocking collectives, on_device(): got = lax.all_to_all(send, ROW, 0, 0, tiled=True)  31.9 us
    all_to_all x1, blocking collectives, on_device(): squares = lax.all_to_all(squares, ROW, 0, 0, tiled=True)  16.7 us
    pallas_call x1, Pallas kernels, resist_block(): pl.pallas_call(functools.partial(resist_kernel, rows=rows, cols=cols), ou...  9.72 us
    all_to_all x1, starting transfers between devices, on_device(): gathered = lax.all_to_all(packed, 'z', 0, 0, tiled=True)  9.03 us
    pallas_call x1, Pallas kernels, fields_block(): pl.pallas_call(functools.partial(fields_kernel, rows=rows, norm=norm), ou...  8.53 us
    ppermute x3, starting transfers between devices, on_device(): lax.ppermute(mine, 'x', [(i, (i + k) % 4) for i in range(4)])  5.69 us
    ppermute x3, starting transfers between devices, on_device(): lax.ppermute(gathered, 'y', [(i, (i + k) % 4) for i in range(4)])  4.99 us
    ppermute x1, starting transfers between devices, on_device(): above = lax.ppermute(target, ROW, [(i, i + 1) for i in range(63)])  4.48 us
  transfers between devices with their start and end apart: 15, of which 6 were waited for; matrix products, arithmetic and copies ran while one was open for 0% of the time, Pallas kernels for 2%

profile of v1, /device:TPU:1, one launch (start us, length us, event | category | flops | bytes accessed | tf_op | source)
XLA Modules:
  0.0 120.3 jit_solution(366623116876314440)
XLA Ops:
  0.6 1.9 %analyse.1 = f32[8,40,128]{2,1,0:T(8,128)} custom-call(bf16[8,2048]{1,0:T(8,128)(2,1)} %layout_any.1, bf16[1024,256]{1,0:T(8,128)(2,1)} %constant.24.clone.table_any), custom_call_target="tpu_custom_call" | custom-call | tf_op jit(solution)/shard_map/analyse/pallas_call | solution.py:567
  2.6 9.0 %all-to-all-start = ((f32[8,40,128]{2,1,0:T(8,128)}), f32[8,40,128]{2,1,0:T(8,128)S(1)}, u32[]{:S(2)}, u32[]{:S(2)}) async-start(f32[8,40,128]{2,1,0:T(8,128)} %analyse.1), calls=%async_computation | async-start | bytes 327680 | tf_op jit(solution)/shard_map/all_to_all | solution.py:580
  11.6 4.5 %collective-permute-start = (bf16[8,2048]{1,0:T(8,128)(2,1)}, bf16[8,2048]{1,0:T(8,128)(2,1)S(1)}, u32[]{:S(2)}, u32[]{:S(2)}) collective-permute-start(bf16[8,2048]{1,0:T(8,128)(2,1)} %refs_8_.1), channel_id=1, source_target_pairs={{0,4},{4,8},{8,12},{12,16},{16,20},{20,24},{24,28},{28,32},{32,36}... | collective-permute-start | bytes 98312 | tf_op jit(solution)/shard_map/ppermute | solution.py:564
  16.1 1.9 %collective-permute-start.1 = (bf16[8,2048]{1,0:T(8,128)(2,1)}, bf16[8,2048]{1,0:T(8,128)(2,1)S(1)}, u32[]{:S(2)}, u32[]{:S(2)}) collective-permute-start(bf16[8,2048]{1,0:T(8,128)(2,1)} %refs_8_.1), channel_id=1, source_target_pairs={{4,0},{8,4},{12,8},{16,12},{20,16},{24,20},{28,24},{32,28},{36,32}... | collective-permute-start | bytes 98312 | tf_op jit(solution)/shard_map/ppermute | solution.py:565
  18.0 2.1 %tables.1 = (bf16[896,160]{1,0:T(8,128)(2,1)S(1)}, bf16[96,896]{1,0:T(8,128)(2,1)S(1)}, bf16[640,144]{1,0:T(8,128)(2,1)S(1)}, bf16[64,640]{1,0:T(8,128)(2,1)S(1)}) custom-call(f32[9,64]{1,0:T(8,128)} %first_taps_any.1, f32[9,64]{1,0:T(8,128)} %second_taps_any.1, f32[1,64]{1,0:T(1,128)} %bitcast.5, bf16[144,1792]{1,0:T(8,128)(2,1)} %constant.25.clone.choose_any, ...), custom_call_target="tpu_custom_call" | custom-call | tf_op jit(solution)/shard_map/tables/pallas_call | solution.py:207
  20.1 0.0 collective-permute-done.refs_9_
  20.1 1.7 %collective-permute-done.1.refs_10_ = bf16[8,2048]{1,0:T(8,128)(2,1)S(1)} collective-permute-done((bf16[8,2048]{1,0:T(8,128)(2,1)}, bf16[8,2048]{1,0:T(8,128)(2,1)S(1)}, u32[]{:S(2)}, u32[]{:S(2)}) %collective-permute-start.1) | collective-permute-done | bytes 32800 | tf_op jit(solution)/shard_map/ppermute | solution.py:565
  21.8 0.0 all-to-all-done.refs_0_
  21.8 1.3 %collective-permute-start.2 = (f32[8,40,128]{2,1,0:T(8,128)S(1)}, f32[8,40,128]{2,1,0:T(8,128)S(1)}, u32[]{:S(2)}, u32[]{:S(2)}) collective-permute-start(f32[8,40,128]{2,1,0:T(8,128)S(1)} %all-to-all-done.refs_0_), channel_id=1, source_target_pairs={{0,64},{64,128},{128,192},{192,0},{1,65},{65,129},{129,193},{193,1... | collective-permute-start | bytes 491528 | tf_op jit(solution)/shard_map/ppermute | solution.py:583
  23.1 2.6 %collective-permute-start.3 = (f32[8,40,128]{2,1,0:T(8,128)S(1)}, f32[8,40,128]{2,1,0:T(8,128)S(1)}, u32[]{:S(2)}, u32[]{:S(2)}) collective-permute-start(f32[8,40,128]{2,1,0:T(8,128)S(1)} %all-to-all-done.refs_0_), channel_id=1, source_target_pairs={{0,128},{64,192},{128,0},{192,64},{1,129},{65,193},{129,1},{193,65... | collective-permute-start | bytes 491528 | tf_op jit(solution)/shard_map/ppermute | solution.py:583
  25.8 1.1 collective-permute-start.4
  26.8 1.5 %collective-permute-start.5 = (f32[8,40,128]{2,1,0:T(8,128)S(1)}, f32[8,40,128]{2,1,0:T(8,128)S(1)}, u32[]{:S(2)}, u32[]{:S(2)}) collective-permute-start(f32[8,40,128]{2,1,0:T(8,128)S(1)} %all-to-all-done.refs_0_), channel_id=1, source_target_pairs={{0,4},{4,0},{1,5},{5,1},{2,6},{6,2},{3,7},{7,3},{8,12},{12,8},{9,1... | collective-permute-start | bytes 491528 | tf_op jit(solution)/shard_map/ppermute | solution.py:584
  28.3 0.0 collective-permute-done.2.refs_1_
  28.3 1.4 %collective-permute-start.6 = (f32[8,40,128]{2,1,0:T(8,128)S(1)}, f32[8,40,128]{2,1,0:T(8,128)S(1)}, u32[]{:S(2)}, u32[]{:S(2)}) collective-permute-start(f32[8,40,128]{2,1,0:T(8,128)S(1)} %collective-permute-done.2.refs_1_), channel_id=1, source_target_pairs={{0,4},{4,0},{1,5},{5,1},{2,6},{6,2},{3,7},{7,3},{8,12},{12,8},{9,1... | collective-permute-start | bytes 491528 | tf_op jit(solution)/shard_map/ppermute | solution.py:584
  29.7 3.2 %collective-permute-done.3.refs_2_ = f32[8,40,128]{2,1,0:T(8,128)S(1)} collective-permute-done((f32[8,40,128]{2,1,0:T(8,128)S(1)}, f32[8,40,128]{2,1,0:T(8,128)S(1)}, u32[]{:S(2)}, u32[]{:S(2)}) %collective-permute-start.3) | collective-permute-done | bytes 163872 | tf_op jit(solution)/shard_map/ppermute | solution.py:583
  32.9 1.5 %collective-permute-start.7 = (f32[8,40,128]{2,1,0:T(8,128)S(1)}, f32[8,40,128]{2,1,0:T(8,128)S(1)}, u32[]{:S(2)}, u32[]{:S(2)}) collective-permute-start(f32[8,40,128]{2,1,0:T(8,128)S(1)} %collective-permute-done.3.refs_2_), channel_id=1, source_target_pairs={{0,4},{4,0},{1,5},{5,1},{2,6},{6,2},{3,7},{7,3},{8,12},{12,8},{9,1... | collective-permute-start | bytes 491528 | tf_op jit(solution)/shard_map/ppermute | solution.py:584
  34.4 0.0 collective-permute-done.4.refs_3_
  34.4 0.0 collective-permute-start.8
  34.4 0.0 collective-permute-done.5.refs_4_
  34.4 0.0 collective-permute-done.6.refs_5_
  34.4 1.0 collective-permute-done.7.refs_6_
  35.5 0.4 collective-permute-done.8.refs_7_
  35.8 0.0 copy-start
  35.8 0.8 copy-done
  36.6 8.5 %fields.1 = (f32[4,8,128]{2,1,0:T(8,128)S(1)}, f32[24,32,1024]{2,1,0:T(8,128)S(1)}, f32[16,2048]{1,0:T(8,128)S(1)}, f32[16,2048]{1,0:T(8,128)S(1)}, f32[32,128]{1,0:T(8,128)S(1)}, /*index=5*/f32[32,128]{1,0:T(8,128)S(1)}) custom-call(f32[8,40,128]{2,1,0:T(8,128)S(1)} %all-to-all-done.refs_0_, f32[8,40,128]{2,1,0:T(8,128)S(1)} %collective-permute-done.2.refs_1_, ...), custom_call_target="tpu_custom_call" | custom-call | tf_op jit(solution)/shard_map/fields/pallas_call | solution.py:516
  45.1 1.3 %collective-permute-start.10 = (f32[32,128]{1,0:T(8,128)S(1)}, f32[32,128]{1,0:T(8,128)S(1)}, u32[]{:S(2)}, u32[]{:S(2)}) collective-permute-start(f32[32,128]{1,0:T(8,128)S(1)} %get-tuple-element.33), channel_id=1, source_target_pairs={{1,0},{2,1},{3,2},{5,4},{6,5},{7,6},{9,8},{10,9},{11,10},{13,12},{... | collective-permute-start | bytes 49160 | tf_op jit(solution)/shard_map/ppermute | solution.py:591
  46.4 4.2 %collective-permute-start.9 = (f32[32,128]{1,0:T(8,128)S(1)}, f32[32,128]{1,0:T(8,128)S(1)}, u32[]{:S(2)}, u32[]{:S(2)}) collective-permute-start(f32[32,128]{1,0:T(8,128)S(1)} %get-tuple-element.32), channel_id=1, source_target_pairs={{0,1},{1,2},{2,3},{4,5},{5,6},{6,7},{8,9},{9,10},{10,11},{12,13},{... | collective-permute-start | bytes 49160 | tf_op jit(solution)/shard_map/ppermute | solution.py:590
  51.3 0.0 collective-permute-done.10.right_ref
  51.3 0.0 collective-permute-done.9.left_ref
  51.3 9.7 %resist.1 = (f32[8,2048]{1,0:T(8,128)}, f32[64,24,128]{2,1,0:T(8,128)S(1)}) custom-call(f32[16,2048]{1,0:T(8,128)S(1)} %get-tuple-element.30.field_ref, f32[16,2048]{1,0:T(8,128)S(1)} %get-tuple-element.31.target_ref, f32[32,128]{1,0:T(8,128)S(1)} %collective-permute-done.9.left_ref, f32[32,128]{1,0:T(8,128)S(1)} %collective-permute-done.10.right_ref, ...), custom_call_target="tpu_custom_call" | custom-call | tf_op jit(solution)/shard_map/resist/pallas_call | solution.py:312
  61.0 31.9 %all_to_all.15 = f32[64,24,128]{2,1,0:T(8,128)S(1)} all-to-all(f32[64,24,128]{2,1,0:T(8,128)S(1)} %get-tuple-element.40), channel_id=1, replica_groups=mesh['y'=4,'z'=8,'core'=2,'x'=4] {'y','z','core'}, dimensions={0} | all-to-all | bytes 1572864 | tf_op jit(solution)/shard_map/all_to_all | solution.py:598
  92.9 1.8 %adjoint.1.x_ref = f32[2,2,24,128]{3,2,1,0:T(8,128)S(1)} custom-call(f32[1536,128]{1,0:T(8,128)S(1)} %bitcast.3, f32[4,8,128]{2,1,0:T(8,128)S(1)} %get-tuple-element.41.columns_ref, bf16[256,256]{1,0:T(8,128)(2,1)} %constant.34.clone.table_any, f32[16,128]{1,0:T(8,128)} %constant.35.clone.turn_any), custom_call_target="tpu_custom_call" | custom-call | tf_op jit(solution)/shard_map/adjoint/pallas_call | solution.py:600
  94.7 2.1 %collective-permute-start.11 = (f32[2,2,24,128]{3,2,1,0:T(8,128)S(1)}, f32[2,2,24,128]{3,2,1,0:T(8,128)S(1)}, u32[]{:S(2)}, u32[]{:S(2)}) collective-permute-start(f32[2,2,24,128]{3,2,1,0:T(8,128)S(1)} %adjoint.1.x_ref), channel_id=1, source_target_pairs={{0,1},{1,2},{2,3},{3,0},{4,5},{5,6},{6,7},{7,4},{8,9},{9,10},{10,1... | collective-permute-start | bytes 147464 | tf_op jit(solution)/shard_map/ppermute | solution.py:613
  96.8 2.7 %collective-permute-start.12 = (f32[2,2,24,128]{3,2,1,0:T(8,128)S(1)}, f32[2,2,24,128]{3,2,1,0:T(8,128)S(1)}, u32[]{:S(2)}, u32[]{:S(2)}) collective-permute-start(f32[2,2,24,128]{3,2,1,0:T(8,128)S(1)} %adjoint.1.x_ref), channel_id=1, source_target_pairs={{0,2},{1,3},{2,0},{3,1},{4,6},{5,7},{6,4},{7,5},{8,10},{9,11},{10,... | collective-permute-start | bytes 147464 | tf_op jit(solution)/shard_map/ppermute | solution.py:613
  99.5 0.9 collective-permute-start.13
  100.4 0.0 collective-permute-done.11.one_ref
  100.4 1.4 %collective-permute-done.12.two_ref = f32[2,2,24,128]{3,2,1,0:T(8,128)S(1)} collective-permute-done((f32[2,2,24,128]{3,2,1,0:T(8,128)S(1)}, f32[2,2,24,128]{3,2,1,0:T(8,128)S(1)}, u32[]{:S(2)}, u32[]{:S(2)}) %collective-permute-start.12) | collective-permute-done | bytes 49184 | tf_op jit(solution)/shard_map/ppermute | solution.py:613
  101.8 1.0 collective-permute-done.13.three_ref
  102.8 16.7 %all_to_all.16.squares_ref = f32[64,1,128]{2,1,0:T(1,128)S(1)} all-to-all(f32[64,1,128]{2,1,0:T(1,128)S(1)} %get-tuple-element.43), channel_id=1, replica_groups=mesh['y'=4,'z'=8,'core'=2,'x'=4] {'y','z','core'}, dimensions={0} | all-to-all | bytes 65536 | tf_op jit(solution)/shard_map/all_to_all | solution.py:622
  119.5 0.8 scale.1
  (1 shorter events, 0.0 us)
Async XLA Ops:
  2.6 19.3 %all-to-all-start = ((f32[8,40,128]{2,1,0:T(8,128)}), f32[8,40,128]{2,1,0:T(8,128)S(1)}, u32[]{:S(2)}, u32[]{:S(2)}) async-start(f32[8,40,128]{2,1,0:T(8,128)} %analyse.1), calls=%async_computation | async-start | bytes 327680 | tf_op jit(solution)/shard_map/all_to_all | solution.py:580
  11.6 8.5 %collective-permute-start = (bf16[8,2048]{1,0:T(8,128)(2,1)}, bf16[8,2048]{1,0:T(8,128)(2,1)S(1)}, u32[]{:S(2)}, u32[]{:S(2)}) collective-permute-start(bf16[8,2048]{1,0:T(8,128)(2,1)} %refs_8_.1), channel_id=1, source_target_pairs={{0,4},{4,8},{8,12},{12,16},{16,20},{20,24},{24,28},{28,32},{32,36}... | collective-permute-start | bytes 98312 | tf_op jit(solution)/shard_map/ppermute | solution.py:564
  16.1 5.7 %collective-permute-start.1 = (bf16[8,2048]{1,0:T(8,128)(2,1)}, bf16[8,2048]{1,0:T(8,128)(2,1)S(1)}, u32[]{:S(2)}, u32[]{:S(2)}) collective-permute-start(bf16[8,2048]{1,0:T(8,128)(2,1)} %refs_8_.1), channel_id=1, source_target_pairs={{4,0},{8,4},{12,8},{16,12},{20,16},{24,20},{28,24},{32,28},{36,32}... | collective-permute-start | bytes 98312 | tf_op jit(solution)/shard_map/ppermute | solution.py:565
  21.8 6.5 %collective-permute-start.2 = (f32[8,40,128]{2,1,0:T(8,128)S(1)}, f32[8,40,128]{2,1,0:T(8,128)S(1)}, u32[]{:S(2)}, u32[]{:S(2)}) collective-permute-start(f32[8,40,128]{2,1,0:T(8,128)S(1)} %all-to-all-done.refs_0_), channel_id=1, source_target_pairs={{0,64},{64,128},{128,192},{192,0},{1,65},{65,129},{129,193},{193,1... | collective-permute-start | bytes 491528 | tf_op jit(solution)/shard_map/ppermute | solution.py:583
  23.1 9.8 %collective-permute-start.3 = (f32[8,40,128]{2,1,0:T(8,128)S(1)}, f32[8,40,128]{2,1,0:T(8,128)S(1)}, u32[]{:S(2)}, u32[]{:S(2)}) collective-permute-start(f32[8,40,128]{2,1,0:T(8,128)S(1)} %all-to-all-done.refs_0_), channel_id=1, source_target_pairs={{0,128},{64,192},{128,0},{192,64},{1,129},{65,193},{129,1},{193,65... | collective-permute-start | bytes 491528 | tf_op jit(solution)/shard_map/ppermute | solution.py:583
  25.8 8.7 %collective-permute-start.4 = (f32[8,40,128]{2,1,0:T(8,128)S(1)}, f32[8,40,128]{2,1,0:T(8,128)S(1)}, u32[]{:S(2)}, u32[]{:S(2)}) collective-permute-start(f32[8,40,128]{2,1,0:T(8,128)S(1)} %all-to-all-done.refs_0_), channel_id=1, source_target_pairs={{0,192},{64,0},{128,64},{192,128},{1,193},{65,1},{129,65},{193,129... | collective-permute-start | bytes 491528 | tf_op jit(solution)/shard_map/ppermute | solution.py:583
  26.8 7.6 %collective-permute-start.5 = (f32[8,40,128]{2,1,0:T(8,128)S(1)}, f32[8,40,128]{2,1,0:T(8,128)S(1)}, u32[]{:S(2)}, u32[]{:S(2)}) collective-permute-start(f32[8,40,128]{2,1,0:T(8,128)S(1)} %all-to-all-done.refs_0_), channel_id=1, source_target_pairs={{0,4},{4,0},{1,5},{5,1},{2,6},{6,2},{3,7},{7,3},{8,12},{12,8},{9,1... | collective-permute-start | bytes 491528 | tf_op jit(solution)/shard_map/ppermute | solution.py:584
  28.3 6.1 %collective-permute-start.6 = (f32[8,40,128]{2,1,0:T(8,128)S(1)}, f32[8,40,128]{2,1,0:T(8,128)S(1)}, u32[]{:S(2)}, u32[]{:S(2)}) collective-permute-start(f32[8,40,128]{2,1,0:T(8,128)S(1)} %collective-permute-done.2.refs_1_), channel_id=1, source_target_pairs={{0,4},{4,0},{1,5},{5,1},{2,6},{6,2},{3,7},{7,3},{8,12},{12,8},{9,1... | collective-permute-start | bytes 491528 | tf_op jit(solution)/shard_map/ppermute | solution.py:584
  32.9 2.5 %collective-permute-start.7 = (f32[8,40,128]{2,1,0:T(8,128)S(1)}, f32[8,40,128]{2,1,0:T(8,128)S(1)}, u32[]{:S(2)}, u32[]{:S(2)}) collective-permute-start(f32[8,40,128]{2,1,0:T(8,128)S(1)} %collective-permute-done.3.refs_2_), channel_id=1, source_target_pairs={{0,4},{4,0},{1,5},{5,1},{2,6},{6,2},{3,7},{7,3},{8,12},{12,8},{9,1... | collective-permute-start | bytes 491528 | tf_op jit(solution)/shard_map/ppermute | solution.py:584
  34.4 1.4 %collective-permute-start.8 = (f32[8,40,128]{2,1,0:T(8,128)S(1)}, f32[8,40,128]{2,1,0:T(8,128)S(1)}, u32[]{:S(2)}, u32[]{:S(2)}) collective-permute-start(f32[8,40,128]{2,1,0:T(8,128)S(1)} %collective-permute-done.4.refs_3_), channel_id=1, source_target_pairs={{0,4},{4,0},{1,5},{5,1},{2,6},{6,2},{3,7},{7,3},{8,12},{12,8},{9,1... | collective-permute-start | bytes 491528 | tf_op jit(solution)/shard_map/ppermute | solution.py:584
  35.8 0.8 copy-start
  45.1 6.2 %collective-permute-start.10 = (f32[32,128]{1,0:T(8,128)S(1)}, f32[32,128]{1,0:T(8,128)S(1)}, u32[]{:S(2)}, u32[]{:S(2)}) collective-permute-start(f32[32,128]{1,0:T(8,128)S(1)} %get-tuple-element.33), channel_id=1, source_target_pairs={{1,0},{2,1},{3,2},{5,4},{6,5},{7,6},{9,8},{10,9},{11,10},{13,12},{... | collective-permute-start | bytes 49160 | tf_op jit(solution)/shard_map/ppermute | solution.py:591
  46.4 4.9 %collective-permute-start.9 = (f32[32,128]{1,0:T(8,128)S(1)}, f32[32,128]{1,0:T(8,128)S(1)}, u32[]{:S(2)}, u32[]{:S(2)}) collective-permute-start(f32[32,128]{1,0:T(8,128)S(1)} %get-tuple-element.32), channel_id=1, source_target_pairs={{0,1},{1,2},{2,3},{4,5},{5,6},{6,7},{8,9},{9,10},{10,11},{12,13},{... | collective-permute-start | bytes 49160 | tf_op jit(solution)/shard_map/ppermute | solution.py:590
  94.7 5.7 %collective-permute-start.11 = (f32[2,2,24,128]{3,2,1,0:T(8,128)S(1)}, f32[2,2,24,128]{3,2,1,0:T(8,128)S(1)}, u32[]{:S(2)}, u32[]{:S(2)}) collective-permute-start(f32[2,2,24,128]{3,2,1,0:T(8,128)S(1)} %adjoint.1.x_ref), channel_id=1, source_target_pairs={{0,1},{1,2},{2,3},{3,0},{4,5},{5,6},{6,7},{7,4},{8,9},{9,10},{10,1... | collective-permute-start | bytes 147464 | tf_op jit(solution)/shard_map/ppermute | solution.py:613
  96.8 5.0 %collective-permute-start.12 = (f32[2,2,24,128]{3,2,1,0:T(8,128)S(1)}, f32[2,2,24,128]{3,2,1,0:T(8,128)S(1)}, u32[]{:S(2)}, u32[]{:S(2)}) collective-permute-start(f32[2,2,24,128]{3,2,1,0:T(8,128)S(1)} %adjoint.1.x_ref), channel_id=1, source_target_pairs={{0,2},{1,3},{2,0},{3,1},{4,6},{5,7},{6,4},{7,5},{8,10},{9,11},{10,... | collective-permute-start | bytes 147464 | tf_op jit(solution)/shard_map/ppermute | solution.py:613
  99.5 3.2 %collective-permute-start.13 = (f32[2,2,24,128]{3,2,1,0:T(8,128)S(1)}, f32[2,2,24,128]{3,2,1,0:T(8,128)S(1)}, u32[]{:S(2)}, u32[]{:S(2)}) collective-permute-start(f32[2,2,24,128]{3,2,1,0:T(8,128)S(1)} %adjoint.1.x_ref), channel_id=1, source_target_pairs={{0,3},{1,0},{2,1},{3,2},{4,7},{5,4},{6,5},{7,6},{8,11},{9,8},{10,9... | collective-permute-start | bytes 147464 | tf_op jit(solution)/shard_map/ppermute | solution.py:613

commit v2 on v1

--- a/solution.py
+++ b/solution.py
@@ -224,7 +224,7 @@
 def resist_kernel(
     field_ref, target_ref, left_ref, right_ref, first_ref, second_ref, second_back_ref, first_back_ref, offset_ref,
     fields_ref, weights_any, back_any,
-    resist_ref, out_ref, weights_ref, back_ref,
+    resist_any, out_ref, resist_ref, weights_ref, back_ref,
     views_ref, keep_ref, mixed_ref, spread_ref, summed_ref, all_ref, sems, *, rows, cols
 ):
     copies = fetch((weights_any, back_any), (weights_ref, back_ref), sems)
@@ -238,7 +238,10 @@
         m = jnp.where(lane < width + 64, lane, lane - WIDE)
         return m, (col0 + m >= 0) & (col0 + m < cols)
 
-    chunks = [(i * 256, 256) for i in range(8)] + [(2048, 128)]
+    def sweep(step, times, size):
+        lax.fori_loop(0, width // size, lambda i, c: (step(pl.ds(pl.multiple_of(i * size, size), size)), c)[1], 0, unroll=times)
+        step(slice(width, WIDE))
+
     m, in_grid = columns((16, WIDE))
     keep_col = (in_grid & (m >= -3) & (m < width + 3)).astype(jnp.float32)
     lane = lax.broadcasted_iota(jnp.int32, (16, BAND), 1)
@@ -253,8 +256,7 @@
         views_ref[96 + 16 * dx : 112 + 16 * dx] = lo
     views_ref[144:160] = keep_col.astype(jnp.bfloat16)
 
-    for at, size in chunks:
-        here = slice(at, at + size)
+    def forward(here):
         hidden = jnp.tanh(jnp.dot(first_ref[...], views_ref[:, here], preferred_element_type=jnp.float32))
         keep_ref[:, here] = 1.0 - hidden[:inner] * hidden[:inner]
         hi, lo = halves(hidden)
@@ -262,9 +264,12 @@
         small = jnp.dot(second_ref[0:48], lo, preferred_element_type=jnp.float32)
         mixed_ref[:, here] = both[:48] + both[48:] + small
 
+    sweep(forward, 4, 256)
     logits = offset_ref[0] + mixed_ref[16:32] + pltpu.roll(mixed_ref[0:16], 1, 1) + pltpu.roll(mixed_ref[32:48], WIDE - 1, 1)
     resist = 1.0 / (1.0 + jnp.exp(-logits))
     resist_ref[...] = resist[:8, :width]
+    sent = pltpu.make_async_copy(resist_ref, resist_any, sems.at[2])
+    sent.start()
     slot = lax.broadcasted_iota(jnp.int32, (16, WIDE), 0)
     n = jnp.where(slot < 8, slot, jnp.where(slot < 10, slot - 10, slot - 2))
     use = in_grid & (m >= -2) & (m < width + 2) & (slot < 12) & (row0 + n >= 0) & (row0 + n < rows)
@@ -277,13 +282,14 @@
         spread_ref[48 + 16 * dx : 64 + 16 * dx] = hi
         spread_ref[96 + 16 * dx : 112 + 16 * dx] = lo
 
-    for at, size in chunks:
-        here = slice(at, at + size)
+    def backward(here):
         hidden_grad = jnp.dot(second_back_ref[...], spread_ref[:, here], preferred_element_type=jnp.float32)
         hi, lo = halves(hidden_grad * keep_ref[:, here])
         both = jnp.dot(first_back_ref[...], hi, preferred_element_type=jnp.float32)
         small = jnp.dot(first_back_ref[0:32], lo, preferred_element_type=jnp.float32)
         summed_ref[:, here] = both[:32] + both[32:] + small
+
+    sweep(backward, 1, 1024)
     grad = summed_ref[8:16] + pltpu.roll(summed_ref[0:8], WIDE - 1, 1) + pltpu.roll(summed_ref[16:24], 1, 1)
     for copy in copies:
         copy.wait()
@@ -304,6 +310,7 @@
         for b in range(3):
             out_ref[2 * d, 8 * b : 8 * b + 8] = even[:, BAND * b : BAND * (b + 1)]
             out_ref[2 * d + 1, 8 * b : 8 * b + 8] = odd[:, BAND * b : BAND * (b + 1)]
+    sent.wait()
 
 
 def resist_block(field, target, left, right, tables, second_bias, weights, fields, back, dims):
@@ -311,10 +318,11 @@
     inner, width = tables[2].shape[0], field.shape[1]
     return pl.pallas_call(
         functools.partial(resist_kernel, rows=rows, cols=cols),
-        out_shape=[jax.ShapeDtypeStruct((8, width), jnp.float32), jax.ShapeDtypeStruct((64, 24, BAND), jnp.float32)],
+        out_shape=[pltpu.HBM((8, width), jnp.float32), pltpu.VMEM((64, 24, BAND), jnp.float32)],
         in_specs=[VMEM] * 8 + [SMEM, VMEM] + [HERE] * 2,
-        out_specs=[VMEM] * 2,
+        out_specs=[HERE, VMEM],
         scratch_shapes=[
+            pltpu.VMEM((8, width), jnp.float32),
             pltpu.SMEM(weights.shape, jnp.float32),
             pltpu.VMEM(back.shape, jnp.bfloat16),
             pltpu.VMEM((160, WIDE), jnp.bfloat16),
@@ -323,7 +331,7 @@
             pltpu.VMEM((144, WIDE), jnp.bfloat16),
             pltpu.VMEM((32, WIDE), jnp.float32),
             pltpu.VMEM((256, 768), jnp.float32),
-            pltpu.SemaphoreType.DMA((2,)),
+            pltpu.SemaphoreType.DMA((3,)),
         ],
         compiler_params=params(28),
         name="resist",
@@ -348,17 +356,16 @@
 def fields_kernel(*refs, rows, norm):
     slabs, refs = refs[:8], refs[8:]
     (
-        target_ref, above_ref, below_ref, rows_any, expand_any, line_any, weights_any, synth_any, real_any, imag_any,
+        above_ref, below_ref, rows_ref, expand_any, line_any, weights_any, synth_any, target_any, real_any, imag_any,
         cols_ref, fields_ref, intensity_ref, wanted_ref, first_edge_ref, last_edge_ref, *refs
     ) = refs
     (
-        rows_ref, expand_ref, line_ref, weights_ref, synth_ref, real_ref, imag_ref,
+        expand_ref, line_ref, weights_ref, synth_ref, target_ref, real_ref, imag_ref,
         spec_ref, seen_ref, line_hi_ref, line_lo_ref, sum_ref, sems
     ) = refs
-    at = 2 * lax.axis_index("y") + lax.axis_index("core")
     r = lax.axis_index(ROW)
-    sources = [rows_any.at[at], expand_any, line_any.at[r], weights_any, synth_any]
-    targets = [rows_ref, expand_ref, line_ref, weights_ref, synth_ref]
+    sources = [expand_any, line_any.at[r], weights_any, synth_any, target_any]
+    targets = [expand_ref, line_ref, weights_ref, synth_ref, target_ref]
     for i in range(0, real_ref.shape[0], 4):
         sources += [real_any.at[i : i + 4], imag_any.at[i : i + 4]]
         targets += [real_ref.at[i : i + 4], imag_ref.at[i : i + 4]]
@@ -370,7 +377,6 @@
             hi, lo = halves(slab[:, 8 * t : 8 * t + 8, :].reshape(64, BAND))
             seen_ref[64 * p : 64 * p + 64, t * BAND : (t + 1) * BAND] = hi
             seen_ref[rows + 64 * p : rows + 64 * p + 64, t * BAND : (t + 1) * BAND] = lo
-    copies[0].wait()
     table_hi = rows_ref[0 : 2 * BAND]
     u = dot(table_hi, seen_ref[0:rows]) + dot(rows_ref[2 * BAND :], seen_ref[0:rows]) + dot(table_hi, seen_ref[rows:])
 
@@ -378,7 +384,7 @@
         both = u[:, t * BAND : (t + 1) * BAND]
         return halves(jnp.concatenate([both[:BAND], both[BAND:]], 1))
 
-    copies[1].wait()
+    copies[0].wait()
     lane = lax.broadcasted_iota(jnp.int32, (BAND, 2 * BAND), 1)
     last = u[:, 4 * BAND :] * norm
     for t in range(4):
@@ -387,7 +393,7 @@
         moved = jnp.concatenate([moved[:BAND], -moved[BAND:]], 1)
         spec_ref[t] = dot(hi, expand_ref[...]) + dot(lo, expand_ref[...]) + jnp.where((lane == 0) | (lane == BAND), moved, 0.0)
 
-    copies[2].wait()
+    copies[1].wait()
     phase = line_ref[...]
     c, s = phase[:, :BAND], phase[:, BAND:]
     table = jnp.concatenate([jnp.concatenate([c, -s], 1), jnp.concatenate([s, c], 1)], 0)
@@ -428,15 +434,25 @@
         copy.wait()
     for j in range(4):
         lines(j, 0, j)
-    for copy in copies[3:5]:
+    for copy in copies[2:5]:
         copy.wait()
-    for i in range(kernels // 4):
-        for copy in copies[7 + 2 * i : 9 + 2 * i]:
-            copy.wait()
+    for copy in copies[7:]:
+        copy.wait()
+
+    def group(i, slot, more):
         for j in range(4):
-            waves(4 * i, i % 2, j)
-            if 4 * i + 4 < kernels:
-                lines(4 * i + 4 + j, (i + 1) % 2, j)
+            waves(4 * i, slot, j)
+            if more:
+                lines(4 * i + 4 + j, 1 - slot, j)
+
+    def both(m, carry):
+        group(2 * m, 0, True)
+        group(2 * m + 1, 1, True)
+        return carry
+
+    lax.fori_loop(0, 2, both, 0)
+    group(4, 0, True)
+    group(5, 1, False)
     row = lax.broadcasted_iota(jnp.int32, (16, 2 * BAND), 0)
     lane = lax.broadcasted_iota(jnp.int32, (16, 2 * BAND), 1)
     chosen = ((row < 4) & (lane == 2 * r + row % 2 + BAND * (row // 2))).astype(jnp.bfloat16)
@@ -509,7 +525,7 @@
             out_ref[i, :, g, :] = whole_ref[i, g] * factor
 
 
-def fields_block(slabs, synth, kernel_real, kernel_imaginary, weights, target, above, below, norm):
+def fields_block(slabs, row_table, synth, kernel_real, kernel_imaginary, weights, target, above, below, norm):
     kernels = kernel_real.shape[0]
     height, width = target.shape
     tiles, rows = width // TILE, 64 * height
@@ -526,11 +542,11 @@
         in_specs=[VMEM] * 11 + [HERE] * 7,
         out_specs=[VMEM] * 6,
         scratch_shapes=[
-            pltpu.VMEM((4 * BAND, rows), jnp.bfloat16),
             pltpu.VMEM((2 * BAND, 2 * BAND), jnp.bfloat16),
             pltpu.VMEM((16, 2 * BAND), jnp.float32),
             pltpu.SMEM(weights.shape, jnp.float32),
             pltpu.VMEM((4 * BAND, 2 * TILE), jnp.bfloat16),
+            pltpu.VMEM(target.shape, jnp.bfloat16),
             pltpu.VMEM(kernel_real.shape, jnp.float32),
             pltpu.VMEM(kernel_real.shape, jnp.float32),
             pltpu.VMEM((tiles, BAND, 2 * BAND), jnp.float32),
@@ -543,10 +559,10 @@
         compiler_params=params(28),
         name="fields",
     )(
-        *near(*slabs, target, above, below),
+        *near(*slabs, above, below, row_table),
         *homes(
-            row_transform_tables(), expand_table(norm), line_tables(64, height), weights,
-            np.concatenate(constant_split(synth), 0), kernel_real, kernel_imaginary,
+            expand_table(norm), line_tables(64, height), weights,
+            np.concatenate(constant_split(synth), 0), target, kernel_real, kernel_imaginary,
         ),
     )
 
@@ -579,13 +595,15 @@
     )(*homes(layout, analysis_table()))
     gathered = lax.all_to_all(packed, "z", 0, 0, tiled=True)
     tables = resist_tables(first_taps, first_bias, second_taps, rows)
-    gathered, above, below, *tables = lax.optimization_barrier((gathered, above, below, *tables))
+    at = 2 * lax.axis_index("y") + lax.axis_index("core")
+    row_table = lax.dynamic_index_in_dim(row_transform_tables(), at, 0, keepdims=False)
+    gathered, above, below, row_table, *tables = lax.optimization_barrier((gathered, above, below, row_table, *tables))
     slabs = [gathered] + [lax.ppermute(gathered, "y", [(i, (i + k) % 4) for i in range(4)]) for k in (1, 2, 3)]
     slabs = slabs + [lax.ppermute(slab, "core", [(0, 1), (1, 0)]) for slab in slabs]
 
     synth = synthesis_table(norm)
     columns, fields, intensity, wanted, first_edge, last_edge = fields_block(
-        slabs, synth, kernel_real, kernel_imaginary, weights, target, above, below, norm
+        slabs, row_table, synth, kernel_real, kernel_imaginary, weights, target, above, below, norm
     )
     left = lax.ppermute(last_edge, "x", [(i, i + 1) for i in range(3)])
     right = lax.ppermute(first_edge, "x", [(i + 1, i) for i in range(3)])

time: 121 us -> 118 us (0.975)
  waiting for transfers between devices: 8.72 us -> 5.04 us
  starting transfers between devices: 36 us -> 38.6 us
  Pallas kernels: 24.9 us -> 22.3 us
    ppermute x3, waiting for transfers between devices: 3.21 us -> 0.61 us  [on_device(): lax.ppermute(gathered, 'y', [(i, (i + k) % 4) for i in range(4)])]
    ppermute x4, starting transfers between devices: 4.38 us -> 6.98 us  [on_device(): lax.ppermute(slab, 'core', [(0, 1), (1, 0)])]
    pallas_call x1, Pallas kernels: 9.72 us -> 7.51 us  [resist_block(): pl.pallas_call(functools.partial(resist_kernel, rows=rows, cols=cols), ou...]
  transfers between devices with their start and end apart: 15 -> 15, of which waited for: 6 -> 6; matrix products, arithmetic and copies ran while one was open for 0% -> 1% of each run, Pallas kernels for 2% -> 2%
where the time goes in v2:
time: 118 us; the launch traced here: 117 us
  blocking collectives  48.7 us (41%)
  starting transfers between devices  38.6 us (33%)
  Pallas kernels  22.3 us (19%)
  waiting for transfers between devices  5.04 us (4%)
  between operations  1.4 us (1%)
    all_to_all x1, blocking collectives, on_device(): got = lax.all_to_all(send, ROW, 0, 0, tiled=True)  32 us
    all_to_all x1, blocking collectives, on_device(): squares = lax.all_to_all(squares, ROW, 0, 0, tiled=True)  16.7 us
    all_to_all x1, starting transfers between devices, on_device(): gathered = lax.all_to_all(packed, 'z', 0, 0, tiled=True)  9.03 us
    pallas_call x1, Pallas kernels, fields_block(): pl.pallas_call(functools.partial(fields_kernel, rows=rows, norm=norm), ou...  8.17 us
    pallas_call x1, Pallas kernels, resist_block(): pl.pallas_call(functools.partial(resist_kernel, rows=rows, cols=cols), ou...  7.51 us
    ppermute x4, starting transfers between devices, on_device(): lax.ppermute(slab, 'core', [(0, 1), (1, 0)])  6.98 us
    ppermute x3, starting transfers between devices, on_device(): lax.ppermute(mine, 'x', [(i, (i + k) % 4) for i in range(4)])  5.7 us
    ppermute x3, starting transfers between devices, on_device(): lax.ppermute(gathered, 'y', [(i, (i + k) % 4) for i in range(4)])  4.99 us
  transfers between devices with their start and end apart: 15, of which 6 were waited for; matrix products, arithmetic and copies ran while one was open for 1% of the time, Pallas kernels for 2%

profile of v2, /device:TPU:1, one launch (start us, length us, event | category | flops | bytes accessed | tf_op | source)
XLA Modules:
  0.0 117.0 jit_solution(10465209663989526518)
XLA Ops:
  0.6 1.9 %analyse.1 = f32[8,40,128]{2,1,0:T(8,128)} custom-call(bf16[8,2048]{1,0:T(8,128)(2,1)} %layout_any.1, bf16[1024,256]{1,0:T(8,128)(2,1)} %constant.43.clone.table_any), custom_call_target="tpu_custom_call" | custom-call | tf_op jit(solution)/shard_map/analyse/pallas_call | solution.py:583
  2.6 9.0 %all-to-all-start = ((f32[8,40,128]{2,1,0:T(8,128)}), f32[8,40,128]{2,1,0:T(8,128)S(1)}, u32[]{:S(2)}, u32[]{:S(2)}) async-start(f32[8,40,128]{2,1,0:T(8,128)} %analyse.1), calls=%async_computation | async-start | bytes 327680 | tf_op jit(solution)/shard_map/all_to_all | solution.py:596
  11.6 4.5 %collective-permute-start = (bf16[8,2048]{1,0:T(8,128)(2,1)}, bf16[8,2048]{1,0:T(8,128)(2,1)S(1)}, u32[]{:S(2)}, u32[]{:S(2)}) collective-permute-start(bf16[8,2048]{1,0:T(8,128)(2,1)} %refs_15_.1), channel_id=1, source_target_pairs={{0,4},{4,8},{8,12},{12,16},{16,20},{20,24},{24,28},{28,32},{32,36}... | collective-permute-start | bytes 98312 | tf_op jit(solution)/shard_map/ppermute | solution.py:580
  16.1 1.9 %collective-permute-start.1 = (bf16[8,2048]{1,0:T(8,128)(2,1)}, bf16[8,2048]{1,0:T(8,128)(2,1)S(1)}, u32[]{:S(2)}, u32[]{:S(2)}) collective-permute-start(bf16[8,2048]{1,0:T(8,128)(2,1)} %refs_15_.1), channel_id=1, source_target_pairs={{4,0},{8,4},{12,8},{16,12},{20,16},{24,20},{28,24},{32,28},{36,32}... | collective-permute-start | bytes 98312 | tf_op jit(solution)/shard_map/ppermute | solution.py:581
  18.0 1.1 dynamic-slice_bitcast_fusion.refs_10_
  19.1 2.1 %tables.1 = (bf16[896,160]{1,0:T(8,128)(2,1)S(1)}, bf16[96,896]{1,0:T(8,128)(2,1)S(1)}, bf16[640,144]{1,0:T(8,128)(2,1)S(1)}, bf16[64,640]{1,0:T(8,128)(2,1)S(1)}) custom-call(f32[9,64]{1,0:T(8,128)} %first_taps_any.1, f32[9,64]{1,0:T(8,128)} %second_taps_any.1, f32[1,64]{1,0:T(1,128)} %bitcast.7, bf16[144,1792]{1,0:T(8,128)(2,1)} %constant.44.clone.choose_any, ...), custom_call_target="tpu_custom_call" | custom-call | tf_op jit(solution)/shard_map/tables/pallas_call | solution.py:207
  21.2 0.0 collective-permute-done.refs_8_
  21.2 0.6 collective-permute-done.1.refs_9_
  21.8 0.0 all-to-all-done.refs_0_
  21.8 1.3 %collective-permute-start.2 = (f32[8,40,128]{2,1,0:T(8,128)S(1)}, f32[8,40,128]{2,1,0:T(8,128)S(1)}, u32[]{:S(2)}, u32[]{:S(2)}) collective-permute-start(f32[8,40,128]{2,1,0:T(8,128)S(1)} %all-to-all-done.refs_0_), channel_id=1, source_target_pairs={{0,64},{64,128},{128,192},{192,0},{1,65},{65,129},{129,193},{193,1... | collective-permute-start | bytes 491528 | tf_op jit(solution)/shard_map/ppermute | solution.py:601
  23.1 2.6 %collective-permute-start.3 = (f32[8,40,128]{2,1,0:T(8,128)S(1)}, f32[8,40,128]{2,1,0:T(8,128)S(1)}, u32[]{:S(2)}, u32[]{:S(2)}) collective-permute-start(f32[8,40,128]{2,1,0:T(8,128)S(1)} %all-to-all-done.refs_0_), channel_id=1, source_target_pairs={{0,128},{64,192},{128,0},{192,64},{1,129},{65,193},{129,1},{193,65... | collective-permute-start | bytes 491528 | tf_op jit(solution)/shard_map/ppermute | solution.py:601
  25.8 1.1 collective-permute-start.4
  26.8 2.5 %collective-permute-start.5 = (f32[8,40,128]{2,1,0:T(8,128)S(1)}, f32[8,40,128]{2,1,0:T(8,128)S(1)}, u32[]{:S(2)}, u32[]{:S(2)}) collective-permute-start(f32[8,40,128]{2,1,0:T(8,128)S(1)} %all-to-all-done.refs_0_), channel_id=1, source_target_pairs={{0,4},{4,0},{1,5},{5,1},{2,6},{6,2},{3,7},{7,3},{8,12},{12,8},{9,1... | collective-permute-start | bytes 491528 | tf_op jit(solution)/shard_map/ppermute | solution.py:602
  29.3 0.0 collective-permute-done.2.refs_1_
  29.3 1.6 %collective-permute-start.6 = (f32[8,40,128]{2,1,0:T(8,128)S(1)}, f32[8,40,128]{2,1,0:T(8,128)S(1)}, u32[]{:S(2)}, u32[]{:S(2)}) collective-permute-start(f32[8,40,128]{2,1,0:T(8,128)S(1)} %collective-permute-done.2.refs_1_), channel_id=1, source_target_pairs={{0,4},{4,0},{1,5},{5,1},{2,6},{6,2},{3,7},{7,3},{8,12},{12,8},{9,1... | collective-permute-start | bytes 491528 | tf_op jit(solution)/shard_map/ppermute | solution.py:602
  30.9 0.6 collective-permute-done.3.refs_2_
  31.5 2.9 %collective-permute-start.7 = (f32[8,40,128]{2,1,0:T(8,128)S(1)}, f32[8,40,128]{2,1,0:T(8,128)S(1)}, u32[]{:S(2)}, u32[]{:S(2)}) collective-permute-start(f32[8,40,128]{2,1,0:T(8,128)S(1)} %collective-permute-done.3.refs_2_), channel_id=1, source_target_pairs={{0,4},{4,0},{1,5},{5,1},{2,6},{6,2},{3,7},{7,3},{8,12},{12,8},{9,1... | collective-permute-start | bytes 491528 | tf_op jit(solution)/shard_map/ppermute | solution.py:602
  34.4 0.0 collective-permute-done.4.refs_3_
  34.4 0.0 collective-permute-start.8
  34.4 0.0 collective-permute-done.5.refs_4_
  34.4 0.0 collective-permute-done.6.refs_5_
  34.4 1.0 collective-permute-done.7.refs_6_
  35.4 0.4 collective-permute-done.8.refs_7_
  35.8 8.2 %fields.1 = (f32[4,8,128]{2,1,0:T(8,128)S(1)}, f32[24,32,1024]{2,1,0:T(8,128)S(1)}, f32[16,2048]{1,0:T(8,128)S(1)}, f32[16,2048]{1,0:T(8,128)S(1)}, f32[32,128]{1,0:T(8,128)S(1)}, /*index=5*/f32[32,128]{1,0:T(8,128)S(1)}) custom-call(f32[8,40,128]{2,1,0:T(8,128)S(1)} %all-to-all-done.refs_0_, f32[8,40,128]{2,1,0:T(8,128)S(1)} %collective-permute-done.2.refs_1_, ...), custom_call_target="tpu_custom_call" | custom-call | tf_op jit(solution)/shard_map/fields/pallas_call | solution.py:532
  44.0 1.3 %collective-permute-start.10 = (f32[32,128]{1,0:T(8,128)S(1)}, f32[32,128]{1,0:T(8,128)S(1)}, u32[]{:S(2)}, u32[]{:S(2)}) collective-permute-start(f32[32,128]{1,0:T(8,128)S(1)} %get-tuple-element.35), channel_id=1, source_target_pairs={{1,0},{2,1},{3,2},{5,4},{6,5},{7,6},{9,8},{10,9},{11,10},{13,12},{... | collective-permute-start | bytes 49160 | tf_op jit(solution)/shard_map/ppermute | solution.py:609
  45.3 4.2 %collective-permute-start.9 = (f32[32,128]{1,0:T(8,128)S(1)}, f32[32,128]{1,0:T(8,128)S(1)}, u32[]{:S(2)}, u32[]{:S(2)}) collective-permute-start(f32[32,128]{1,0:T(8,128)S(1)} %get-tuple-element.34), channel_id=1, source_target_pairs={{0,1},{1,2},{2,3},{4,5},{5,6},{6,7},{8,9},{9,10},{10,11},{12,13},{... | collective-permute-start | bytes 49160 | tf_op jit(solution)/shard_map/ppermute | solution.py:608
  50.1 0.0 collective-permute-done.10.right_ref
  50.1 0.0 collective-permute-done.9.left_ref
  50.1 7.5 %resist.1 = (f32[8,2048]{1,0:T(8,128)}, f32[64,24,128]{2,1,0:T(8,128)S(1)}) custom-call(f32[16,2048]{1,0:T(8,128)S(1)} %get-tuple-element.32.field_ref, f32[16,2048]{1,0:T(8,128)S(1)} %get-tuple-element.33.target_ref, f32[32,128]{1,0:T(8,128)S(1)} %collective-permute-done.9.left_ref, f32[32,128]{1,0:T(8,128)S(1)} %collective-permute-done.10.right_ref, ...), custom_call_target="tpu_custom_call" | custom-call | tf_op jit(solution)/shard_map/resist/pallas_call | solution.py:319
  57.7 32.0 %all_to_all.15 = f32[64,24,128]{2,1,0:T(8,128)S(1)} all-to-all(f32[64,24,128]{2,1,0:T(8,128)S(1)} %get-tuple-element.42), channel_id=1, replica_groups=mesh['y'=4,'z'=8,'core'=2,'x'=4] {'y','z','core'}, dimensions={0} | all-to-all | bytes 1572864 | tf_op jit(solution)/shard_map/all_to_all | solution.py:616
  89.6 1.8 %adjoint.1.x_ref = f32[2,2,24,128]{3,2,1,0:T(8,128)S(1)} custom-call(f32[1536,128]{1,0:T(8,128)S(1)} %bitcast.5, f32[4,8,128]{2,1,0:T(8,128)S(1)} %get-tuple-element.43.columns_ref, bf16[256,256]{1,0:T(8,128)(2,1)} %constant.53.clone.table_any, f32[16,128]{1,0:T(8,128)} %constant.54.clone.turn_any), custom_call_target="tpu_custom_call" | custom-call | tf_op jit(solution)/shard_map/adjoint/pallas_call | solution.py:618
  91.4 2.1 %collective-permute-start.11 = (f32[2,2,24,128]{3,2,1,0:T(8,128)S(1)}, f32[2,2,24,128]{3,2,1,0:T(8,128)S(1)}, u32[]{:S(2)}, u32[]{:S(2)}) collective-permute-start(f32[2,2,24,128]{3,2,1,0:T(8,128)S(1)} %adjoint.1.x_ref), channel_id=1, source_target_pairs={{0,1},{1,2},{2,3},{3,0},{4,5},{5,6},{6,7},{7,4},{8,9},{9,10},{10,1... | collective-permute-start | bytes 147464 | tf_op jit(solution)/shard_map/ppermute | solution.py:631
  93.5 2.7 %collective-permute-start.12 = (f32[2,2,24,128]{3,2,1,0:T(8,128)S(1)}, f32[2,2,24,128]{3,2,1,0:T(8,128)S(1)}, u32[]{:S(2)}, u32[]{:S(2)}) collective-permute-start(f32[2,2,24,128]{3,2,1,0:T(8,128)S(1)} %adjoint.1.x_ref), channel_id=1, source_target_pairs={{0,2},{1,3},{2,0},{3,1},{4,6},{5,7},{6,4},{7,5},{8,10},{9,11},{10,... | collective-permute-start | bytes 147464 | tf_op jit(solution)/shard_map/ppermute | solution.py:631
  96.3 0.9 collective-permute-start.13
  97.1 0.0 collective-permute-done.11.one_ref
  97.1 1.4 %collective-permute-done.12.two_ref = f32[2,2,24,128]{3,2,1,0:T(8,128)S(1)} collective-permute-done((f32[2,2,24,128]{3,2,1,0:T(8,128)S(1)}, f32[2,2,24,128]{3,2,1,0:T(8,128)S(1)}, u32[]{:S(2)}, u32[]{:S(2)}) %collective-permute-start.12) | collective-permute-done | bytes 49184 | tf_op jit(solution)/shard_map/ppermute | solution.py:631
  98.5 1.0 collective-permute-done.13.three_ref
  99.5 16.7 %all_to_all.16.squares_ref = f32[64,1,128]{2,1,0:T(1,128)S(1)} all-to-all(f32[64,1,128]{2,1,0:T(1,128)S(1)} %get-tuple-element.45), channel_id=1, replica_groups=mesh['y'=4,'z'=8,'core'=2,'x'=4] {'y','z','core'}, dimensions={0} | all-to-all | bytes 65536 | tf_op jit(solution)/shard_map/all_to_all | solution.py:640
  116.2 0.8 scale.1
  (1 shorter events, 0.0 us)
Async XLA Ops:
  2.6 19.3 %all-to-all-start = ((f32[8,40,128]{2,1,0:T(8,128)}), f32[8,40,128]{2,1,0:T(8,128)S(1)}, u32[]{:S(2)}, u32[]{:S(2)}) async-start(f32[8,40,128]{2,1,0:T(8,128)} %analyse.1), calls=%async_computation | async-start | bytes 327680 | tf_op jit(solution)/shard_map/all_to_all | solution.py:596
  11.6 9.6 %collective-permute-start = (bf16[8,2048]{1,0:T(8,128)(2,1)}, bf16[8,2048]{1,0:T(8,128)(2,1)S(1)}, u32[]{:S(2)}, u32[]{:S(2)}) collective-permute-start(bf16[8,2048]{1,0:T(8,128)(2,1)} %refs_15_.1), channel_id=1, source_target_pairs={{0,4},{4,8},{8,12},{12,16},{16,20},{20,24},{24,28},{28,32},{32,36}... | collective-permute-start | bytes 98312 | tf_op jit(solution)/shard_map/ppermute | solution.py:580
  16.1 5.7 %collective-permute-start.1 = (bf16[8,2048]{1,0:T(8,128)(2,1)}, bf16[8,2048]{1,0:T(8,128)(2,1)S(1)}, u32[]{:S(2)}, u32[]{:S(2)}) collective-permute-start(bf16[8,2048]{1,0:T(8,128)(2,1)} %refs_15_.1), channel_id=1, source_target_pairs={{4,0},{8,4},{12,8},{16,12},{20,16},{24,20},{28,24},{32,28},{36,32}... | collective-permute-start | bytes 98312 | tf_op jit(solution)/shard_map/ppermute | solution.py:581
  21.8 7.5 %collective-permute-start.2 = (f32[8,40,128]{2,1,0:T(8,128)S(1)}, f32[8,40,128]{2,1,0:T(8,128)S(1)}, u32[]{:S(2)}, u32[]{:S(2)}) collective-permute-start(f32[8,40,128]{2,1,0:T(8,128)S(1)} %all-to-all-done.refs_0_), channel_id=1, source_target_pairs={{0,64},{64,128},{128,192},{192,0},{1,65},{65,129},{129,193},{193,1... | collective-permute-start | bytes 491528 | tf_op jit(solution)/shard_map/ppermute | solution.py:601
  23.1 8.4 %collective-permute-start.3 = (f32[8,40,128]{2,1,0:T(8,128)S(1)}, f32[8,40,128]{2,1,0:T(8,128)S(1)}, u32[]{:S(2)}, u32[]{:S(2)}) collective-permute-start(f32[8,40,128]{2,1,0:T(8,128)S(1)} %all-to-all-done.refs_0_), channel_id=1, source_target_pairs={{0,128},{64,192},{128,0},{192,64},{1,129},{65,193},{129,1},{193,65... | collective-permute-start | bytes 491528 | tf_op jit(solution)/shard_map/ppermute | solution.py:601
  25.8 8.7 %collective-permute-start.4 = (f32[8,40,128]{2,1,0:T(8,128)S(1)}, f32[8,40,128]{2,1,0:T(8,128)S(1)}, u32[]{:S(2)}, u32[]{:S(2)}) collective-permute-start(f32[8,40,128]{2,1,0:T(8,128)S(1)} %all-to-all-done.refs_0_), channel_id=1, source_target_pairs={{0,192},{64,0},{128,64},{192,128},{1,193},{65,1},{129,65},{193,129... | collective-permute-start | bytes 491528 | tf_op jit(solution)/shard_map/ppermute | solution.py:601
  26.8 7.6 %collective-permute-start.5 = (f32[8,40,128]{2,1,0:T(8,128)S(1)}, f32[8,40,128]{2,1,0:T(8,128)S(1)}, u32[]{:S(2)}, u32[]{:S(2)}) collective-permute-start(f32[8,40,128]{2,1,0:T(8,128)S(1)} %all-to-all-done.refs_0_), channel_id=1, source_target_pairs={{0,4},{4,0},{1,5},{5,1},{2,6},{6,2},{3,7},{7,3},{8,12},{12,8},{9,1... | collective-permute-start | bytes 491528 | tf_op jit(solution)/shard_map/ppermute | solution.py:602
  29.3 5.1 %collective-permute-start.6 = (f32[8,40,128]{2,1,0:T(8,128)S(1)}, f32[8,40,128]{2,1,0:T(8,128)S(1)}, u32[]{:S(2)}, u32[]{:S(2)}) collective-permute-start(f32[8,40,128]{2,1,0:T(8,128)S(1)} %collective-permute-done.2.refs_1_), channel_id=1, source_target_pairs={{0,4},{4,0},{1,5},{5,1},{2,6},{6,2},{3,7},{7,3},{8,12},{12,8},{9,1... | collective-permute-start | bytes 491528 | tf_op jit(solution)/shard_map/ppermute | solution.py:602
  31.5 3.9 %collective-permute-start.7 = (f32[8,40,128]{2,1,0:T(8,128)S(1)}, f32[8,40,128]{2,1,0:T(8,128)S(1)}, u32[]{:S(2)}, u32[]{:S(2)}) collective-permute-start(f32[8,40,128]{2,1,0:T(8,128)S(1)} %collective-permute-done.3.refs_2_), channel_id=1, source_target_pairs={{0,4},{4,0},{1,5},{5,1},{2,6},{6,2},{3,7},{7,3},{8,12},{12,8},{9,1... | collective-permute-start | bytes 491528 | tf_op jit(solution)/shard_map/ppermute | solution.py:602
  34.4 1.4 %collective-permute-start.8 = (f32[8,40,128]{2,1,0:T(8,128)S(1)}, f32[8,40,128]{2,1,0:T(8,128)S(1)}, u32[]{:S(2)}, u32[]{:S(2)}) collective-permute-start(f32[8,40,128]{2,1,0:T(8,128)S(1)} %collective-permute-done.4.refs_3_), channel_id=1, source_target_pairs={{0,4},{4,0},{1,5},{5,1},{2,6},{6,2},{3,7},{7,3},{8,12},{12,8},{9,1... | collective-permute-start | bytes 491528 | tf_op jit(solution)/shard_map/ppermute | solution.py:602
  44.0 6.1 %collective-permute-start.10 = (f32[32,128]{1,0:T(8,128)S(1)}, f32[32,128]{1,0:T(8,128)S(1)}, u32[]{:S(2)}, u32[]{:S(2)}) collective-permute-start(f32[32,128]{1,0:T(8,128)S(1)} %get-tuple-element.35), channel_id=1, source_target_pairs={{1,0},{2,1},{3,2},{5,4},{6,5},{7,6},{9,8},{10,9},{11,10},{13,12},{... | collective-permute-start | bytes 49160 | tf_op jit(solution)/shard_map/ppermute | solution.py:609
  45.3 4.8 %collective-permute-start.9 = (f32[32,128]{1,0:T(8,128)S(1)}, f32[32,128]{1,0:T(8,128)S(1)}, u32[]{:S(2)}, u32[]{:S(2)}) collective-permute-start(f32[32,128]{1,0:T(8,128)S(1)} %get-tuple-element.34), channel_id=1, source_target_pairs={{0,1},{1,2},{2,3},{4,5},{5,6},{6,7},{8,9},{9,10},{10,11},{12,13},{... | collective-permute-start | bytes 49160 | tf_op jit(solution)/shard_map/ppermute | solution.py:608
  91.4 5.7 %collective-permute-start.11 = (f32[2,2,24,128]{3,2,1,0:T(8,128)S(1)}, f32[2,2,24,128]{3,2,1,0:T(8,128)S(1)}, u32[]{:S(2)}, u32[]{:S(2)}) collective-permute-start(f32[2,2,24,128]{3,2,1,0:T(8,128)S(1)} %adjoint.1.x_ref), channel_id=1, source_target_pairs={{0,1},{1,2},{2,3},{3,0},{4,5},{5,6},{6,7},{7,4},{8,9},{9,10},{10,1... | collective-permute-start | bytes 147464 | tf_op jit(solution)/shard_map/ppermute | solution.py:631
  93.5 5.0 %collective-permute-start.12 = (f32[2,2,24,128]{3,2,1,0:T(8,128)S(1)}, f32[2,2,24,128]{3,2,1,0:T(8,128)S(1)}, u32[]{:S(2)}, u32[]{:S(2)}) collective-permute-start(f32[2,2,24,128]{3,2,1,0:T(8,128)S(1)} %adjoint.1.x_ref), channel_id=1, source_target_pairs={{0,2},{1,3},{2,0},{3,1},{4,6},{5,7},{6,4},{7,5},{8,10},{9,11},{10,... | collective-permute-start | bytes 147464 | tf_op jit(solution)/shard_map/ppermute | solution.py:631
  96.3 3.2 %collective-permute-start.13 = (f32[2,2,24,128]{3,2,1,0:T(8,128)S(1)}, f32[2,2,24,128]{3,2,1,0:T(8,128)S(1)}, u32[]{:S(2)}, u32[]{:S(2)}) collective-permute-start(f32[2,2,24,128]{3,2,1,0:T(8,128)S(1)} %adjoint.1.x_ref), channel_id=1, source_target_pairs={{0,3},{1,0},{2,1},{3,2},{4,7},{5,4},{6,5},{7,6},{8,11},{9,8},{10,9... | collective-permute-start | bytes 147464 | tf_op jit(solution)/shard_map/ppermute | solution.py:631

commit v3 on v2

--- a/solution.py
+++ b/solution.py
@@ -221,9 +221,41 @@
     )(*homes(*args))
 
 
+SIDE = 256
+
+
+def hide(first_ref, second_ref, views_ref, here, inner):
+    hidden = jnp.tanh(dot(first_ref[...], views_ref[:, here]))
+    hi, lo = halves(hidden)
+    both = dot(second_ref[...], hi)
+    return both[:48] + both[48:] + dot(second_ref[0:48], lo), 1.0 - hidden[:inner] * hidden[:inner]
+
+
+def place_views(views_ref, dx, moved):
+    hi, lo = halves(moved)
+    views_ref[16 * dx : 16 * dx + 16] = hi
+    views_ref[48 + 16 * dx : 64 + 16 * dx] = hi
+    views_ref[96 + 16 * dx : 112 + 16 * dx] = lo
+
+
+def middle_kernel(field_ref, first_ref, second_ref, mixed_ref, keep_ref, views_ref):
+    width = field_ref.shape[1]
+    for dx in range(3):
+        place_views(views_ref, dx, field_ref[...] if dx == 1 else pltpu.roll(field_ref[...], (1 - dx) % width, 1))
+    views_ref[144:160] = jnp.ones((16, width), jnp.bfloat16)
+
+    def step(i, carry):
+        at = pl.multiple_of(i * 256, 256)
+        there = pl.ds(pl.multiple_of(at + SIDE, 256), 256)
+        mixed_ref[:, pl.ds(at, 256)], keep_ref[:, pl.ds(at, 256)] = hide(first_ref, second_ref, views_ref, there, keep_ref.shape[0])
+        return carry
+
+    lax.fori_loop(0, (width - 2 * SIDE) // 256, step, 0, unroll=3)
+
+
 def resist_kernel(
     field_ref, target_ref, left_ref, right_ref, first_ref, second_ref, second_back_ref, first_back_ref, offset_ref,
-    fields_ref, weights_any, back_any,
+    fields_ref, mixed_mid_ref, keep_mid_ref, weights_any, back_any,
     resist_any, out_ref, resist_ref, weights_ref, back_ref,
     views_ref, keep_ref, mixed_ref, spread_ref, summed_ref, all_ref, sems, *, rows, cols
 ):
@@ -238,33 +270,22 @@
         m = jnp.where(lane < width + 64, lane, lane - WIDE)
         return m, (col0 + m >= 0) & (col0 + m < cols)
 
-    def sweep(step, times, size):
-        lax.fori_loop(0, width // size, lambda i, c: (step(pl.ds(pl.multiple_of(i * size, size), size)), c)[1], 0, unroll=times)
-        step(slice(width, WIDE))
-
     m, in_grid = columns((16, WIDE))
     keep_col = (in_grid & (m >= -3) & (m < width + 3)).astype(jnp.float32)
     lane = lax.broadcasted_iota(jnp.int32, (16, BAND), 1)
     gap = [jnp.where(lane < 64, right_ref[i : i + 16], left_ref[i : i + 16]) for i in (0, 16)]
-    field = jnp.concatenate([field_ref[...], gap[0]], 1)
+    field = jnp.concatenate([field_ref[...], jnp.where(in_grid[:, width:], gap[0], 0.0)], 1)
     target = jnp.concatenate([target_ref[...], gap[1]], 1)
     for dx in range(3):
-        moved = (field if dx == 1 else pltpu.roll(field, (1 - dx) % WIDE, 1)) * keep_col
-        hi, lo = halves(moved)
-        views_ref[16 * dx : 16 * dx + 16] = hi
-        views_ref[48 + 16 * dx : 64 + 16 * dx] = hi
-        views_ref[96 + 16 * dx : 112 + 16 * dx] = lo
+        place_views(views_ref, dx, (field if dx == 1 else pltpu.roll(field, (1 - dx) % WIDE, 1)) * keep_col)
     views_ref[144:160] = keep_col.astype(jnp.bfloat16)
 
-    def forward(here):
-        hidden = jnp.tanh(jnp.dot(first_ref[...], views_ref[:, here], preferred_element_type=jnp.float32))
-        keep_ref[:, here] = 1.0 - hidden[:inner] * hidden[:inner]
-        hi, lo = halves(hidden)
-        both = jnp.dot(second_ref[...], hi, preferred_element_type=jnp.float32)
-        small = jnp.dot(second_ref[0:48], lo, preferred_element_type=jnp.float32)
-        mixed_ref[:, here] = both[:48] + both[48:] + small
-
-    sweep(forward, 4, 256)
+    edges = (slice(0, SIDE), slice(width - SIDE, width), slice(width, WIDE))
+    kept = (slice(0, SIDE), slice(SIDE, 2 * SIDE), slice(2 * SIDE, 2 * SIDE + BAND))
+    mixed_ref[:, SIDE : width - SIDE] = mixed_mid_ref[...]
+    for here, place in zip(edges, kept, strict=True):
+        mixed_ref[:, here], keep_ref[:, place] = hide(first_ref, second_ref, views_ref, here, inner)
+
     logits = offset_ref[0] + mixed_ref[16:32] + pltpu.roll(mixed_ref[0:16], 1, 1) + pltpu.roll(mixed_ref[32:48], WIDE - 1, 1)
     resist = 1.0 / (1.0 + jnp.exp(-logits))
     resist_ref[...] = resist[:8, :width]
@@ -276,20 +297,22 @@
     slope = jnp.where(use, (resist - target) * (TILE / cols), 0.0)
     grid_col = in_grid.astype(jnp.float32)
     for dx in range(3):
-        moved = (slope if dx == 1 else pltpu.roll(slope, (dx - 1) % WIDE, 1)) * grid_col
-        hi, lo = halves(moved)
-        spread_ref[16 * dx : 16 * dx + 16] = hi
-        spread_ref[48 + 16 * dx : 64 + 16 * dx] = hi
-        spread_ref[96 + 16 * dx : 112 + 16 * dx] = lo
-
-    def backward(here):
-        hidden_grad = jnp.dot(second_back_ref[...], spread_ref[:, here], preferred_element_type=jnp.float32)
-        hi, lo = halves(hidden_grad * keep_ref[:, here])
-        both = jnp.dot(first_back_ref[...], hi, preferred_element_type=jnp.float32)
-        small = jnp.dot(first_back_ref[0:32], lo, preferred_element_type=jnp.float32)
-        summed_ref[:, here] = both[:32] + both[32:] + small
-
-    sweep(backward, 1, 1024)
+        place_views(spread_ref, dx, (slope if dx == 1 else pltpu.roll(slope, (dx - 1) % WIDE, 1)) * grid_col)
+
+    def backward(here, kept):
+        hidden_grad = dot(second_back_ref[...], spread_ref[:, here])
+        hi, lo = halves(hidden_grad * kept)
+        both = dot(first_back_ref[...], hi)
+        summed_ref[:, here] = both[:32] + both[32:] + dot(first_back_ref[0:32], lo)
+
+    def middle(i, carry):
+        at = pl.multiple_of(i * 768, 256)
+        backward(pl.ds(pl.multiple_of(SIDE + at, 256), 768), keep_mid_ref[:, pl.ds(at, 768)])
+        return carry
+
+    lax.fori_loop(0, keep_mid_ref.shape[1] // 768, middle, 0)
+    for here, place in zip(edges, kept, strict=True):
+        backward(here, keep_ref[:, place])
     grad = summed_ref[8:16] + pltpu.roll(summed_ref[0:8], WIDE - 1, 1) + pltpu.roll(summed_ref[16:24], 1, 1)
     for copy in copies:
         copy.wait()
@@ -313,20 +336,33 @@
     sent.wait()
 
 
-def resist_block(field, target, left, right, tables, second_bias, weights, fields, back, dims):
+def middle_block(field, tables):
+    inner, width = tables[2].shape[0], field.shape[1]
+    return pl.pallas_call(
+        middle_kernel,
+        out_shape=[pltpu.VMEM((48, width - 2 * SIDE), jnp.float32), pltpu.VMEM((inner, width - 2 * SIDE), jnp.float32)],
+        in_specs=[VMEM] * 3,
+        out_specs=[VMEM] * 2,
+        scratch_shapes=[pltpu.VMEM((160, width), jnp.bfloat16)],
+        compiler_params=params(16),
+        name="middle",
+    )(*near(field, tables[0], tables[1]))
+
+
+def resist_block(field, target, left, right, tables, second_bias, weights, fields, middle, back, dims):
     rows, cols = dims
     inner, width = tables[2].shape[0], field.shape[1]
     return pl.pallas_call(
         functools.partial(resist_kernel, rows=rows, cols=cols),
         out_shape=[pltpu.HBM((8, width), jnp.float32), pltpu.VMEM((64, 24, BAND), jnp.float32)],
-        in_specs=[VMEM] * 8 + [SMEM, VMEM] + [HERE] * 2,
+        in_specs=[VMEM] * 8 + [SMEM] + [VMEM] * 3 + [HERE] * 2,
         out_specs=[HERE, VMEM],
         scratch_shapes=[
             pltpu.VMEM((8, width), jnp.float32),
             pltpu.SMEM(weights.shape, jnp.float32),
             pltpu.VMEM(back.shape, jnp.bfloat16),
             pltpu.VMEM((160, WIDE), jnp.bfloat16),
-            pltpu.VMEM((inner, WIDE), jnp.float32),
+            pltpu.VMEM((inner, 2 * SIDE + BAND), jnp.float32),
             pltpu.VMEM((48, WIDE), jnp.float32),
             pltpu.VMEM((144, WIDE), jnp.bfloat16),
             pltpu.VMEM((32, WIDE), jnp.float32),
@@ -335,7 +371,7 @@
         ],
         compiler_params=params(28),
         name="resist",
-    )(field, target, left, right, *tables, second_bias, *near(fields), *homes(weights, back))
+    )(field, target, left, right, *tables, second_bias, *near(fields, *middle), *homes(weights, back))
 
 
 def analyse_kernel(layout_any, table_any, out_ref, layout_ref, table_ref, sems):
@@ -356,7 +392,7 @@
 def fields_kernel(*refs, rows, norm):
     slabs, refs = refs[:8], refs[8:]
     (
-        above_ref, below_ref, rows_ref, expand_any, line_any, weights_any, synth_any, target_any, real_any, imag_any,
+        near_rows_ref, far_rows_ref, rows_ref, expand_any, line_any, weights_any, synth_any, target_any, real_any, imag_any,
         cols_ref, fields_ref, intensity_ref, wanted_ref, first_edge_ref, last_edge_ref, *refs
     ) = refs
     (
@@ -468,7 +504,9 @@
         both = sum_ref[16 * t : 16 * t + 16]
         intensity_ref[:, t * TILE : (t + 1) * TILE] = jnp.where(inside, both[:, :TILE] + both[:, TILE:], 0.0)
     wanted_ref[0:8] = target_ref[...].astype(jnp.float32)
-    above, below = above_ref[...].astype(jnp.float32), below_ref[...].astype(jnp.float32)
+    one, other = near_rows_ref[...].astype(jnp.float32), far_rows_ref[...].astype(jnp.float32)
+    even = r % 2 == 0
+    above, below = jnp.where(even, other, one), jnp.where(even, one, other)
     wanted_ref[8:16] = jnp.concatenate([above[6:8], below[0:2], jnp.zeros((4, above.shape[1]), jnp.float32)], 0)
     width = intensity_ref.shape[1]
     for i, ref in ((0, intensity_ref), (16, wanted_ref)):
@@ -525,7 +563,7 @@
             out_ref[i, :, g, :] = whole_ref[i, g] * factor
 
 
-def fields_block(slabs, row_table, synth, kernel_real, kernel_imaginary, weights, target, above, below, norm):
+def fields_block(slabs, row_table, synth, kernel_real, kernel_imaginary, weights, target, near_rows, far_rows, norm):
     kernels = kernel_real.shape[0]
     height, width = target.shape
     tiles, rows = width // TILE, 64 * height
@@ -559,7 +597,7 @@
         compiler_params=params(28),
         name="fields",
     )(
-        *near(*slabs, above, below, row_table),
+        *near(*slabs, near_rows, far_rows, row_table),
         *homes(
             expand_table(norm), line_tables(64, height), weights,
             np.concatenate(constant_split(synth), 0), target, kernel_real, kernel_imaginary,
@@ -577,8 +615,8 @@
     r = lax.axis_index(ROW)
     norm = 1.0 / math.sqrt(rows * TILE)
 
-    above = lax.ppermute(target, ROW, [(i, i + 1) for i in range(63)])
-    below = lax.ppermute(target, ROW, [(i + 1, i) for i in range(63)])
+    near_rows = lax.ppermute(target, ROW, [(i, i ^ 1) for i in range(64)])
+    far_rows = lax.ppermute(target, ROW, [(i, (i - 1 if i % 2 == 0 else i + 1) % 64) for i in range(64)])
 
     packed = pl.pallas_call(
         analyse_kernel,
@@ -597,20 +635,23 @@
     tables = resist_tables(first_taps, first_bias, second_taps, rows)
     at = 2 * lax.axis_index("y") + lax.axis_index("core")
     row_table = lax.dynamic_index_in_dim(row_transform_tables(), at, 0, keepdims=False)
-    gathered, above, below, row_table, *tables = lax.optimization_barrier((gathered, above, below, row_table, *tables))
+    gathered, near_rows, far_rows, row_table, *tables = lax.optimization_barrier(
+        (gathered, near_rows, far_rows, row_table, *tables)
+    )
     slabs = [gathered] + [lax.ppermute(gathered, "y", [(i, (i + k) % 4) for i in range(4)]) for k in (1, 2, 3)]
     slabs = slabs + [lax.ppermute(slab, "core", [(0, 1), (1, 0)]) for slab in slabs]
 
     synth = synthesis_table(norm)
     columns, fields, intensity, wanted, first_edge, last_edge = fields_block(
-        slabs, row_table, synth, kernel_real, kernel_imaginary, weights, target, above, below, norm
+        slabs, row_table, synth, kernel_real, kernel_imaginary, weights, target, near_rows, far_rows, norm
     )
-    left = lax.ppermute(last_edge, "x", [(i, i + 1) for i in range(3)])
-    right = lax.ppermute(first_edge, "x", [(i + 1, i) for i in range(3)])
+    left = lax.ppermute(last_edge, "x", [(i, (i + 1) % 4) for i in range(4)])
+    right = lax.ppermute(first_edge, "x", [((i + 1) % 4, i) for i in range(4)])
     back = synth.reshape(2, 64, 2, 2 * TILE).transpose(1, 2, 0, 3).reshape(256, 2 * TILE)
     back = np.concatenate(constant_split(back), 0)
+    middle = middle_block(intensity, tables)
     resist, send = resist_block(
-        intensity, wanted, left, right, tables, second_bias, weights, fields, back, (rows, cols)
+        intensity, wanted, left, right, tables, second_bias, weights, fields, middle, back, (rows, cols)
     )
 
     got = lax.all_to_all(send, ROW, 0, 0, tiled=True)

time: 118 us -> 110 us (0.932)
  starting transfers between devices: 38.6 us -> 31.4 us
  blocking collectives: 48.7 us -> 45.2 us
  waiting for transfers between devices: 5.04 us -> 7.54 us
    ppermute x4, starting transfers between devices: 11.9 us -> 5.4 us  [the longest x1 1.63 us: on_device(): lax.ppermute(target, ROW, [(i, (i - 1 if i % 2 == 0 else i + 1) % 64) for...]
    ppermute x4, starting transfers between devices: 6.98 us -> 10.8 us  [on_device(): lax.ppermute(slab, 'core', [(0, 1), (1, 0)])]
    all_to_all x1, blocking collectives: 32 us -> 28.5 us  [on_device(): got = lax.all_to_all(send, ROW, 0, 0, tiled=True)]
    ppermute x3, starting transfers between devices: 5.7 us -> 2.47 us  [on_device(): lax.ppermute(mine, 'x', [(i, (i + k) % 4) for i in range(4)])]
    pallas_call x0 -> x1, Pallas kernels: none -> 2.45 us  [middle_block(): pl.pallas_call(middle_kernel, out_shape=[pltpu.VMEM((48, width - 2 * SIDE...]
    pallas_call x1, Pallas kernels: 7.51 us -> 5.25 us  [resist_block(): pl.pallas_call(functools.partial(resist_kernel, rows=rows, cols=cols), ou...]
    ppermute x3, waiting for transfers between devices: 2.38 us -> 4.11 us  [on_device(): lax.ppermute(mine, 'x', [(i, (i + k) % 4) for i in range(4)])]
    all_to_all x1, waiting for transfers between devices: 0.01 us -> 1.55 us  [on_device(): gathered = lax.all_to_all(packed, 'z', 0, 0, tiled=True)]
  transfers between devices with their start and end apart: 15 -> 15, of which waited for: 6 -> 6; matrix products, arithmetic and copies ran while one was open for 1% -> 1% of each run, Pallas kernels for 2% -> 4%
where the time goes in v3:
time: 110 us; the launch traced here: 109 us
  blocking collectives  45.2 us (41%)
  starting transfers between devices  31.4 us (29%)
  Pallas kernels  22.8 us (21%)
  waiting for transfers between devices  7.54 us (7%)
  between operations  1.38 us (1%)
    all_to_all x1, blocking collectives, on_device(): got = lax.all_to_all(send, ROW, 0, 0, tiled=True)  28.5 us
    all_to_all x1, blocking collectives, on_device(): squares = lax.all_to_all(squares, ROW, 0, 0, tiled=True)  16.7 us
    ppermute x4, starting transfers between devices, on_device(): lax.ppermute(slab, 'core', [(0, 1), (1, 0)])  10.8 us
    all_to_all x1, starting transfers between devices, on_device(): gathered = lax.all_to_all(packed, 'z', 0, 0, tiled=True)  9.03 us
    pallas_call x1, Pallas kernels, fields_block(): pl.pallas_call(functools.partial(fields_kernel, rows=rows, norm=norm), ou...  8.46 us
    pallas_call x1, Pallas kernels, resist_block(): pl.pallas_call(functools.partial(resist_kernel, rows=rows, cols=cols), ou...  5.25 us
    ppermute x3, waiting for transfers between devices, on_device(): lax.ppermute(mine, 'x', [(i, (i + k) % 4) for i in range(4)])  4.11 us
    ppermute x3, starting transfers between devices, on_device(): lax.ppermute(gathered, 'y', [(i, (i + k) % 4) for i in range(4)])  3.78 us
  transfers between devices with their start and end apart: 15, of which 6 were waited for; matrix products, arithmetic and copies ran while one was open for 1% of the time, Pallas kernels for 4%

profile of v3, /device:TPU:1, one launch (start us, length us, event | category | flops | bytes accessed | tf_op | source)
XLA Modules:
  0.0 109.4 jit_solution(800679947294018350)
XLA Ops:
  0.6 1.9 %analyse.1 = f32[8,40,128]{2,1,0:T(8,128)} custom-call(bf16[8,2048]{1,0:T(8,128)(2,1)} %layout_any.1, bf16[1024,256]{1,0:T(8,128)(2,1)} %constant.43.clone.table_any), custom_call_target="tpu_custom_call" | custom-call | tf_op jit(solution)/shard_map/analyse/pallas_call | solution.py:621
  2.6 9.0 %all-to-all-start = ((f32[8,40,128]{2,1,0:T(8,128)}), f32[8,40,128]{2,1,0:T(8,128)S(1)}, u32[]{:S(2)}, u32[]{:S(2)}) async-start(f32[8,40,128]{2,1,0:T(8,128)} %analyse.1), calls=%async_computation | async-start | bytes 327680 | tf_op jit(solution)/shard_map/all_to_all | solution.py:634
  11.6 1.0 collective-permute-start
  12.6 1.6 %collective-permute-start.1 = (bf16[8,2048]{1,0:T(8,128)(2,1)}, bf16[8,2048]{1,0:T(8,128)(2,1)S(1)}, u32[]{:S(2)}, u32[]{:S(2)}) collective-permute-start(bf16[8,2048]{1,0:T(8,128)(2,1)} %refs_15_.1), channel_id=1, source_target_pairs={{0,252},{4,8},{8,4},{12,16},{16,12},{20,24},{24,20},{28,32},{32,28... | collective-permute-start | bytes 98312 | tf_op jit(solution)/shard_map/ppermute | solution.py:619
  14.2 1.1 dynamic-slice_bitcast_fusion.refs_10_
  15.3 2.1 %tables.1 = (bf16[896,160]{1,0:T(8,128)(2,1)S(1)}, bf16[96,896]{1,0:T(8,128)(2,1)S(1)}, bf16[640,144]{1,0:T(8,128)(2,1)S(1)}, bf16[64,640]{1,0:T(8,128)(2,1)S(1)}) custom-call(f32[9,64]{1,0:T(8,128)} %first_taps_any.1, f32[9,64]{1,0:T(8,128)} %second_taps_any.1, f32[1,64]{1,0:T(1,128)} %bitcast.7, bf16[144,1792]{1,0:T(8,128)(2,1)} %constant.44.clone.choose_any, ...), custom_call_target="tpu_custom_call" | custom-call | tf_op jit(solution)/shard_map/tables/pallas_call | solution.py:207
  17.3 0.0 collective-permute-done.refs_8_
  17.3 0.8 collective-permute-done.1.refs_9_
  18.2 1.6 %all-to-all-done.refs_0_ = f32[8,40,128]{2,1,0:T(8,128)S(1)} async-done(((f32[8,40,128]{2,1,0:T(8,128)}), f32[8,40,128]{2,1,0:T(8,128)S(1)}, u32[]{:S(2)}, u32[]{:S(2)}) %all-to-all-start) | async-done | bytes 163872 | tf_op jit(solution)/shard_map/all_to_all | solution.py:634
  19.7 2.7 %collective-permute-start.4 = (f32[8,40,128]{2,1,0:T(8,128)S(1)}, f32[8,40,128]{2,1,0:T(8,128)S(1)}, u32[]{:S(2)}, u32[]{:S(2)}) collective-permute-start(f32[8,40,128]{2,1,0:T(8,128)S(1)} %all-to-all-done.refs_0_), channel_id=1, source_target_pairs={{0,192},{64,0},{128,64},{192,128},{1,193},{65,1},{129,65},{193,129... | collective-permute-start | bytes 491528 | tf_op jit(solution)/shard_map/ppermute | solution.py:641
  22.5 0.3 collective-permute-start.3
  22.8 0.7 collective-permute-start.2
  23.5 3.8 %collective-permute-start.5 = (f32[8,40,128]{2,1,0:T(8,128)S(1)}, f32[8,40,128]{2,1,0:T(8,128)S(1)}, u32[]{:S(2)}, u32[]{:S(2)}) collective-permute-start(f32[8,40,128]{2,1,0:T(8,128)S(1)} %all-to-all-done.refs_0_), channel_id=1, source_target_pairs={{0,4},{4,0},{1,5},{5,1},{2,6},{6,2},{3,7},{7,3},{8,12},{12,8},{9,1... | collective-permute-start | bytes 491528 | tf_op jit(solution)/shard_map/ppermute | solution.py:642
  27.3 0.0 collective-permute-done.4.refs_3_
  27.3 3.1 %collective-permute-start.8 = (f32[8,40,128]{2,1,0:T(8,128)S(1)}, f32[8,40,128]{2,1,0:T(8,128)S(1)}, u32[]{:S(2)}, u32[]{:S(2)}) collective-permute-start(f32[8,40,128]{2,1,0:T(8,128)S(1)} %collective-permute-done.4.refs_3_), channel_id=1, source_target_pairs={{0,4},{4,0},{1,5},{5,1},{2,6},{6,2},{3,7},{7,3},{8,12},{12,8},{9,1... | collective-permute-start | bytes 491528 | tf_op jit(solution)/shard_map/ppermute | solution.py:642
  30.4 0.0 collective-permute-done.3.refs_2_
  30.4 2.2 %collective-permute-start.7 = (f32[8,40,128]{2,1,0:T(8,128)S(1)}, f32[8,40,128]{2,1,0:T(8,128)S(1)}, u32[]{:S(2)}, u32[]{:S(2)}) collective-permute-start(f32[8,40,128]{2,1,0:T(8,128)S(1)} %collective-permute-done.3.refs_2_), channel_id=1, source_target_pairs={{0,4},{4,0},{1,5},{5,1},{2,6},{6,2},{3,7},{7,3},{8,12},{12,8},{9,1... | collective-permute-start | bytes 491528 | tf_op jit(solution)/shard_map/ppermute | solution.py:642
  32.6 0.0 collective-permute-done.2.refs_1_
  32.6 1.6 %collective-permute-start.6 = (f32[8,40,128]{2,1,0:T(8,128)S(1)}, f32[8,40,128]{2,1,0:T(8,128)S(1)}, u32[]{:S(2)}, u32[]{:S(2)}) collective-permute-start(f32[8,40,128]{2,1,0:T(8,128)S(1)} %collective-permute-done.2.refs_1_), channel_id=1, source_target_pairs={{0,4},{4,0},{1,5},{5,1},{2,6},{6,2},{3,7},{7,3},{8,12},{12,8},{9,1... | collective-permute-start | bytes 491528 | tf_op jit(solution)/shard_map/ppermute | solution.py:642
  34.3 0.0 collective-permute-done.5.refs_4_
  34.3 0.0 collective-permute-done.8.refs_7_
  34.3 0.0 collective-permute-done.7.refs_6_
  34.3 1.0 collective-permute-done.6.refs_5_
  35.3 8.5 %fields.1 = (f32[4,8,128]{2,1,0:T(8,128)S(1)}, f32[24,32,1024]{2,1,0:T(8,128)S(1)}, f32[16,2048]{1,0:T(8,128)S(1)}, f32[16,2048]{1,0:T(8,128)S(1)}, f32[32,128]{1,0:T(8,128)S(1)}, /*index=5*/f32[32,128]{1,0:T(8,128)S(1)}) custom-call(f32[8,40,128]{2,1,0:T(8,128)S(1)} %all-to-all-done.refs_0_, f32[8,40,128]{2,1,0:T(8,128)S(1)} %collective-permute-done.2.refs_1_, ...), custom_call_target="tpu_custom_call" | custom-call | tf_op jit(solution)/shard_map/fields/pallas_call | solution.py:570
  43.8 1.3 %collective-permute-start.9 = (f32[32,128]{1,0:T(8,128)S(1)}, f32[32,128]{1,0:T(8,128)S(1)}, u32[]{:S(2)}, u32[]{:S(2)}) collective-permute-start(f32[32,128]{1,0:T(8,128)S(1)} %get-tuple-element.36), channel_id=1, source_target_pairs={{0,1},{1,2},{2,3},{3,0},{4,5},{5,6},{6,7},{7,4},{8,9},{9,10},{10,1... | collective-permute-start | bytes 49160 | tf_op jit(solution)/shard_map/ppermute | solution.py:648
  45.1 1.5 %collective-permute-start.10 = (f32[32,128]{1,0:T(8,128)S(1)}, f32[32,128]{1,0:T(8,128)S(1)}, u32[]{:S(2)}, u32[]{:S(2)}) collective-permute-start(f32[32,128]{1,0:T(8,128)S(1)} %get-tuple-element.37), channel_id=1, source_target_pairs={{1,0},{2,1},{3,2},{0,3},{5,4},{6,5},{7,6},{4,7},{9,8},{10,9},{11,1... | collective-permute-start | bytes 49160 | tf_op jit(solution)/shard_map/ppermute | solution.py:649
  47.3 2.5 %middle.1 = (f32[48,1536]{1,0:T(8,128)S(1)}, f32[640,1536]{1,0:T(8,128)S(1)}) custom-call(f32[16,2048]{1,0:T(8,128)S(1)} %get-tuple-element.34.field_ref, bf16[896,160]{1,0:T(8,128)(2,1)S(1)} %get-tuple-element.38.first_ref, bf16[96,896]{1,0:T(8,128)(2,1)S(1)} %get-tuple-element.39.second_ref), custom_call_target="tpu_custom_call" | custom-call | tf_op jit(solution)/shard_map/middle/pallas_call | solution.py:341
  49.7 0.0 collective-permute-done.9.left_ref
  49.7 0.0 collective-permute-done.10.right_ref
  49.7 5.2 %resist.1 = (f32[8,2048]{1,0:T(8,128)}, f32[64,24,128]{2,1,0:T(8,128)S(1)}) custom-call(f32[16,2048]{1,0:T(8,128)S(1)} %get-tuple-element.34.field_ref, f32[16,2048]{1,0:T(8,128)S(1)} %get-tuple-element.35.target_ref, f32[32,128]{1,0:T(8,128)S(1)} %collective-permute-done.9.left_ref, f32[32,128]{1,0:T(8,128)S(1)} %collective-permute-done.10.right_ref, ...), custom_call_target="tpu_custom_call" | custom-call | tf_op jit(solution)/shard_map/resist/pallas_call | solution.py:355
  55.0 28.5 %all_to_all.15 = f32[64,24,128]{2,1,0:T(8,128)S(1)} all-to-all(f32[64,24,128]{2,1,0:T(8,128)S(1)} %get-tuple-element.46), channel_id=1, replica_groups=mesh['y'=4,'z'=8,'core'=2,'x'=4] {'y','z','core'}, dimensions={0} | all-to-all | bytes 1572864 | tf_op jit(solution)/shard_map/all_to_all | solution.py:657
  83.5 1.8 %adjoint.1.x_ref = f32[2,2,24,128]{3,2,1,0:T(8,128)S(1)} custom-call(f32[1536,128]{1,0:T(8,128)S(1)} %bitcast.5, f32[4,8,128]{2,1,0:T(8,128)S(1)} %get-tuple-element.47.columns_ref, bf16[256,256]{1,0:T(8,128)(2,1)} %constant.53.clone.table_any, f32[16,128]{1,0:T(8,128)} %constant.54.clone.turn_any), custom_call_target="tpu_custom_call" | custom-call | tf_op jit(solution)/shard_map/adjoint/pallas_call | solution.py:659
  85.3 1.6 %collective-permute-start.13 = (f32[2,2,24,128]{3,2,1,0:T(8,128)S(1)}, f32[2,2,24,128]{3,2,1,0:T(8,128)S(1)}, u32[]{:S(2)}, u32[]{:S(2)}) collective-permute-start(f32[2,2,24,128]{3,2,1,0:T(8,128)S(1)} %adjoint.1.x_ref), channel_id=1, source_target_pairs={{0,3},{1,0},{2,1},{3,2},{4,7},{5,4},{6,5},{7,6},{8,11},{9,8},{10,9... | collective-permute-start | bytes 147464 | tf_op jit(solution)/shard_map/ppermute | solution.py:672
  86.9 0.3 collective-permute-start.12
  87.2 0.5 collective-permute-start.11
  87.7 0.5 collective-permute-done.13.three_ref
  88.3 3.1 %collective-permute-done.12.two_ref = f32[2,2,24,128]{3,2,1,0:T(8,128)S(1)} collective-permute-done((f32[2,2,24,128]{3,2,1,0:T(8,128)S(1)}, f32[2,2,24,128]{3,2,1,0:T(8,128)S(1)}, u32[]{:S(2)}, u32[]{:S(2)}) %collective-permute-start.12) | collective-permute-done | bytes 49184 | tf_op jit(solution)/shard_map/ppermute | solution.py:672
  91.4 0.5 collective-permute-done.11.one_ref
  91.9 16.7 %all_to_all.16.squares_ref = f32[64,1,128]{2,1,0:T(1,128)S(1)} all-to-all(f32[64,1,128]{2,1,0:T(1,128)S(1)} %get-tuple-element.49), channel_id=1, replica_groups=mesh['y'=4,'z'=8,'core'=2,'x'=4] {'y','z','core'}, dimensions={0} | all-to-all | bytes 65536 | tf_op jit(solution)/shard_map/all_to_all | solution.py:681
  108.6 0.8 scale.1
  (1 shorter events, 0.0 us)
Async XLA Ops:
  2.6 17.2 %all-to-all-start = ((f32[8,40,128]{2,1,0:T(8,128)}), f32[8,40,128]{2,1,0:T(8,128)S(1)}, u32[]{:S(2)}, u32[]{:S(2)}) async-start(f32[8,40,128]{2,1,0:T(8,128)} %analyse.1), calls=%async_computation | async-start | bytes 327680 | tf_op jit(solution)/shard_map/all_to_all | solution.py:634
  11.6 5.7 %collective-permute-start = (bf16[8,2048]{1,0:T(8,128)(2,1)}, bf16[8,2048]{1,0:T(8,128)(2,1)S(1)}, u32[]{:S(2)}, u32[]{:S(2)}) collective-permute-start(bf16[8,2048]{1,0:T(8,128)(2,1)} %refs_15_.1), channel_id=1, source_target_pairs={{0,4},{4,0},{8,12},{12,8},{16,20},{20,16},{24,28},{28,24},{32,36},... | collective-permute-start | bytes 98312 | tf_op jit(solution)/shard_map/ppermute | solution.py:618
  12.6 5.6 %collective-permute-start.1 = (bf16[8,2048]{1,0:T(8,128)(2,1)}, bf16[8,2048]{1,0:T(8,128)(2,1)S(1)}, u32[]{:S(2)}, u32[]{:S(2)}) collective-permute-start(bf16[8,2048]{1,0:T(8,128)(2,1)} %refs_15_.1), channel_id=1, source_target_pairs={{0,252},{4,8},{8,4},{12,16},{16,12},{20,24},{24,20},{28,32},{32,28... | collective-permute-start | bytes 98312 | tf_op jit(solution)/shard_map/ppermute | solution.py:619
  19.7 7.6 %collective-permute-start.4 = (f32[8,40,128]{2,1,0:T(8,128)S(1)}, f32[8,40,128]{2,1,0:T(8,128)S(1)}, u32[]{:S(2)}, u32[]{:S(2)}) collective-permute-start(f32[8,40,128]{2,1,0:T(8,128)S(1)} %all-to-all-done.refs_0_), channel_id=1, source_target_pairs={{0,192},{64,0},{128,64},{192,128},{1,193},{65,1},{129,65},{193,129... | collective-permute-start | bytes 491528 | tf_op jit(solution)/shard_map/ppermute | solution.py:641
  22.5 8.0 %collective-permute-start.3 = (f32[8,40,128]{2,1,0:T(8,128)S(1)}, f32[8,40,128]{2,1,0:T(8,128)S(1)}, u32[]{:S(2)}, u32[]{:S(2)}) collective-permute-start(f32[8,40,128]{2,1,0:T(8,128)S(1)} %all-to-all-done.refs_0_), channel_id=1, source_target_pairs={{0,128},{64,192},{128,0},{192,64},{1,129},{65,193},{129,1},{193,65... | collective-permute-start | bytes 491528 | tf_op jit(solution)/shard_map/ppermute | solution.py:641
  22.8 9.8 %collective-permute-start.2 = (f32[8,40,128]{2,1,0:T(8,128)S(1)}, f32[8,40,128]{2,1,0:T(8,128)S(1)}, u32[]{:S(2)}, u32[]{:S(2)}) collective-permute-start(f32[8,40,128]{2,1,0:T(8,128)S(1)} %all-to-all-done.refs_0_), channel_id=1, source_target_pairs={{0,64},{64,128},{128,192},{192,0},{1,65},{65,129},{129,193},{193,1... | collective-permute-start | bytes 491528 | tf_op jit(solution)/shard_map/ppermute | solution.py:641
  23.5 10.8 %collective-permute-start.5 = (f32[8,40,128]{2,1,0:T(8,128)S(1)}, f32[8,40,128]{2,1,0:T(8,128)S(1)}, u32[]{:S(2)}, u32[]{:S(2)}) collective-permute-start(f32[8,40,128]{2,1,0:T(8,128)S(1)} %all-to-all-done.refs_0_), channel_id=1, source_target_pairs={{0,4},{4,0},{1,5},{5,1},{2,6},{6,2},{3,7},{7,3},{8,12},{12,8},{9,1... | collective-permute-start | bytes 491528 | tf_op jit(solution)/shard_map/ppermute | solution.py:642
  27.3 7.0 %collective-permute-start.8 = (f32[8,40,128]{2,1,0:T(8,128)S(1)}, f32[8,40,128]{2,1,0:T(8,128)S(1)}, u32[]{:S(2)}, u32[]{:S(2)}) collective-permute-start(f32[8,40,128]{2,1,0:T(8,128)S(1)} %collective-permute-done.4.refs_3_), channel_id=1, source_target_pairs={{0,4},{4,0},{1,5},{5,1},{2,6},{6,2},{3,7},{7,3},{8,12},{12,8},{9,1... | collective-permute-start | bytes 491528 | tf_op jit(solution)/shard_map/ppermute | solution.py:642
  30.4 3.9 %collective-permute-start.7 = (f32[8,40,128]{2,1,0:T(8,128)S(1)}, f32[8,40,128]{2,1,0:T(8,128)S(1)}, u32[]{:S(2)}, u32[]{:S(2)}) collective-permute-start(f32[8,40,128]{2,1,0:T(8,128)S(1)} %collective-permute-done.3.refs_2_), channel_id=1, source_target_pairs={{0,4},{4,0},{1,5},{5,1},{2,6},{6,2},{3,7},{7,3},{8,12},{12,8},{9,1... | collective-permute-start | bytes 491528 | tf_op jit(solution)/shard_map/ppermute | solution.py:642
  32.6 2.7 %collective-permute-start.6 = (f32[8,40,128]{2,1,0:T(8,128)S(1)}, f32[8,40,128]{2,1,0:T(8,128)S(1)}, u32[]{:S(2)}, u32[]{:S(2)}) collective-permute-start(f32[8,40,128]{2,1,0:T(8,128)S(1)} %collective-permute-done.2.refs_1_), channel_id=1, source_target_pairs={{0,4},{4,0},{1,5},{5,1},{2,6},{6,2},{3,7},{7,3},{8,12},{12,8},{9,1... | collective-permute-start | bytes 491528 | tf_op jit(solution)/shard_map/ppermute | solution.py:642
  43.8 5.9 %collective-permute-start.9 = (f32[32,128]{1,0:T(8,128)S(1)}, f32[32,128]{1,0:T(8,128)S(1)}, u32[]{:S(2)}, u32[]{:S(2)}) collective-permute-start(f32[32,128]{1,0:T(8,128)S(1)} %get-tuple-element.36), channel_id=1, source_target_pairs={{0,1},{1,2},{2,3},{3,0},{4,5},{5,6},{6,7},{7,4},{8,9},{9,10},{10,1... | collective-permute-start | bytes 49160 | tf_op jit(solution)/shard_map/ppermute | solution.py:648
  45.1 4.7 %collective-permute-start.10 = (f32[32,128]{1,0:T(8,128)S(1)}, f32[32,128]{1,0:T(8,128)S(1)}, u32[]{:S(2)}, u32[]{:S(2)}) collective-permute-start(f32[32,128]{1,0:T(8,128)S(1)} %get-tuple-element.37), channel_id=1, source_target_pairs={{1,0},{2,1},{3,2},{0,3},{5,4},{6,5},{7,6},{4,7},{9,8},{10,9},{11,1... | collective-permute-start | bytes 49160 | tf_op jit(solution)/shard_map/ppermute | solution.py:649
  85.3 3.0 %collective-permute-start.13 = (f32[2,2,24,128]{3,2,1,0:T(8,128)S(1)}, f32[2,2,24,128]{3,2,1,0:T(8,128)S(1)}, u32[]{:S(2)}, u32[]{:S(2)}) collective-permute-start(f32[2,2,24,128]{3,2,1,0:T(8,128)S(1)} %adjoint.1.x_ref), channel_id=1, source_target_pairs={{0,3},{1,0},{2,1},{3,2},{4,7},{5,4},{6,5},{7,6},{8,11},{9,8},{10,9... | collective-permute-start | bytes 147464 | tf_op jit(solution)/shard_map/ppermute | solution.py:672
  86.9 4.5 %collective-permute-start.12 = (f32[2,2,24,128]{3,2,1,0:T(8,128)S(1)}, f32[2,2,24,128]{3,2,1,0:T(8,128)S(1)}, u32[]{:S(2)}, u32[]{:S(2)}) collective-permute-start(f32[2,2,24,128]{3,2,1,0:T(8,128)S(1)} %adjoint.1.x_ref), channel_id=1, source_target_pairs={{0,2},{1,3},{2,0},{3,1},{4,6},{5,7},{6,4},{7,5},{8,10},{9,11},{10,... | collective-permute-start | bytes 147464 | tf_op jit(solution)/shard_map/ppermute | solution.py:672
  87.2 4.6 %collective-permute-start.11 = (f32[2,2,24,128]{3,2,1,0:T(8,128)S(1)}, f32[2,2,24,128]{3,2,1,0:T(8,128)S(1)}, u32[]{:S(2)}, u32[]{:S(2)}) collective-permute-start(f32[2,2,24,128]{3,2,1,0:T(8,128)S(1)} %adjoint.1.x_ref), channel_id=1, source_target_pairs={{0,1},{1,2},{2,3},{3,0},{4,5},{5,6},{6,7},{7,4},{8,9},{9,10},{10,1... | collective-permute-start | bytes 147464 | tf_op jit(solution)/shard_map/ppermute | solution.py:672

commit v4 on v3

--- a/solution.py
+++ b/solution.py
@@ -389,6 +389,16 @@
         out_ref[i] = packed
 
 
+def repack_kernel(in_ref, out_ref):
+    last = in_ref[0, 32:40]
+    for z in range(8):
+        for t in range(4):
+            out_ref[4 * z + t] = in_ref[z, 8 * t : 8 * t + 8]
+        if z:
+            last = last + pltpu.roll(in_ref[z, 32:40], 4 * z, 1)
+    out_ref[32] = last
+
+
 def fields_kernel(*refs, rows, norm):
     slabs, refs = refs[:8], refs[8:]
     (
@@ -409,8 +419,11 @@
     row0 = r * 8
     kernels = real_ref.shape[0]
     for p, slab in enumerate(slabs):
+        last = slab[32]
+        last = jnp.concatenate([pltpu.roll(last, (BAND - 4 * z) % BAND, 1) if z else last for z in range(8)], 0)
         for t in range(5):
-            hi, lo = halves(slab[:, 8 * t : 8 * t + 8, :].reshape(64, BAND))
+            tile = jnp.concatenate([slab[4 * z + t] for z in range(8)], 0) if t < 4 else last
+            hi, lo = halves(tile)
             seen_ref[64 * p : 64 * p + 64, t * BAND : (t + 1) * BAND] = hi
             seen_ref[rows + 64 * p : rows + 64 * p + 64, t * BAND : (t + 1) * BAND] = lo
     table_hi = rows_ref[0 : 2 * BAND]
@@ -523,7 +536,14 @@
 
 
 def adjoint_kernel(got_ref, columns_ref, table_any, turn_any, out_ref, table_ref, turn_ref, sems):
-    for copy in fetch((table_any, turn_any), (table_ref, turn_ref), sems):
+    copies = fetch((table_any, turn_any), (table_ref, turn_ref), sems)
+    split = {}
+    for h in range(2):
+        for g in range(2):
+            at = 4 * h + 2 * g
+            x = [[got_ref[pl.ds(8 * b + at + i, 64, stride=24), :] for b in range(3)] for i in range(2)]
+            split[h, g] = halves(jnp.concatenate([jnp.concatenate(part, 1) for part in x], 0))
+    for copy in copies:
         copy.wait()
     table_hi, table_lo = table_ref[0:BAND], table_ref[BAND:]
     c, s = turn_ref[0:8], turn_ref[8:16]
@@ -534,10 +554,7 @@
             turned.append((c * re - s * im, s * re + c * im))
         a, b = (jnp.concatenate([x[i] for x in turned], 0)[None] for i in range(2))
         for h in range(2):
-            at = 4 * h + 2 * g
-            x = [[got_ref[pl.ds(8 * b + at + i, 64, stride=24), :] for b in range(3)] for i in range(2)]
-            x = jnp.concatenate([jnp.concatenate(part, 1) for part in x], 0)
-            hi, lo = halves(x)
+            hi, lo = split[h, g]
             sides = (((0,), (0,)), ((), ()))
             y = lax.dot_general(hi, table_hi, sides, preferred_element_type=jnp.float32)
             y = y + lax.dot_general(lo, table_hi, sides, preferred_element_type=jnp.float32)
@@ -638,6 +655,14 @@
     gathered, near_rows, far_rows, row_table, *tables = lax.optimization_barrier(
         (gathered, near_rows, far_rows, row_table, *tables)
     )
+    gathered = pl.pallas_call(
+        repack_kernel,
+        out_shape=jax.ShapeDtypeStruct((33, 8, BAND), jnp.float32),
+        in_specs=[VMEM],
+        out_specs=VMEM,
+        compiler_params=params(8),
+        name="repack",
+    )(gathered)
     slabs = [gathered] + [lax.ppermute(gathered, "y", [(i, (i + k) % 4) for i in range(4)]) for k in (1, 2, 3)]
     slabs = slabs + [lax.ppermute(slab, "core", [(0, 1), (1, 0)]) for slab in slabs]
 

time: 110 us -> 109 us (level)
  no operation moved by 1% of the time
where the time goes in v4:
time: 109 us; the launch traced here: 108 us
  blocking collectives  44.6 us (41%)
  starting transfers between devices  30.8 us (28%)
  Pallas kernels  22.9 us (21%)
  waiting for transfers between devices  7.49 us (7%)
  between operations  1.38 us (1%)
    all_to_all x1, blocking collectives, on_device(): got = lax.all_to_all(send, ROW, 0, 0, tiled=True)  27.9 us
    all_to_all x1, blocking collectives, on_device(): squares = lax.all_to_all(squares, ROW, 0, 0, tiled=True)  16.7 us
    ppermute x4, starting transfers between devices, on_device(): lax.ppermute(slab, 'core', [(0, 1), (1, 0)])  10.1 us
    all_to_all x1, starting transfers between devices, on_device(): gathered = lax.all_to_all(packed, 'z', 0, 0, tiled=True)  9.03 us
    pallas_call x1, Pallas kernels, fields_block(): pl.pallas_call(functools.partial(fields_kernel, rows=rows, norm=norm), ou...  8.48 us
    pallas_call x1, Pallas kernels, resist_block(): pl.pallas_call(functools.partial(resist_kernel, rows=rows, cols=cols), ou...  5.29 us
    ppermute x3, waiting for transfers between devices, on_device(): lax.ppermute(mine, 'x', [(i, (i + k) % 4) for i in range(4)])  4.1 us
    ppermute x3, starting transfers between devices, on_device(): lax.ppermute(gathered, 'y', [(i, (i + k) % 4) for i in range(4)])  3.8 us
  transfers between devices with their start and end apart: 15, of which 6 were waited for; matrix products, arithmetic and copies ran while one was open for 1% of the time, Pallas kernels for 4%

profile of v4, /device:TPU:1, one launch (start us, length us, event | category | flops | bytes accessed | tf_op | source)
XLA Modules:
  0.0 108.3 jit_solution(9466299090178136891)
XLA Ops:
  0.6 1.9 %analyse.1 = f32[8,40,128]{2,1,0:T(8,128)} custom-call(bf16[8,2048]{1,0:T(8,128)(2,1)} %layout_any.1, bf16[1024,256]{1,0:T(8,128)(2,1)} %constant.43.clone.table_any), custom_call_target="tpu_custom_call" | custom-call | tf_op jit(solution)/shard_map/analyse/pallas_call | solution.py:638
  2.6 9.0 %all-to-all-start = ((f32[8,40,128]{2,1,0:T(8,128)}), f32[8,40,128]{2,1,0:T(8,128)S(1)}, u32[]{:S(2)}, u32[]{:S(2)}) async-start(f32[8,40,128]{2,1,0:T(8,128)} %analyse.1), calls=%async_computation | async-start | bytes 327680 | tf_op jit(solution)/shard_map/all_to_all | solution.py:651
  11.6 1.0 collective-permute-start
  12.6 1.6 %collective-permute-start.1 = (bf16[8,2048]{1,0:T(8,128)(2,1)}, bf16[8,2048]{1,0:T(8,128)(2,1)S(1)}, u32[]{:S(2)}, u32[]{:S(2)}) collective-permute-start(bf16[8,2048]{1,0:T(8,128)(2,1)} %refs_15_.1), channel_id=1, source_target_pairs={{0,252},{4,8},{8,4},{12,16},{16,12},{20,24},{24,20},{28,32},{32,28... | collective-permute-start | bytes 98312 | tf_op jit(solution)/shard_map/ppermute | solution.py:636
  14.2 1.1 dynamic-slice_bitcast_fusion.refs_10_
  15.3 2.1 %tables.1 = (bf16[896,160]{1,0:T(8,128)(2,1)S(1)}, bf16[96,896]{1,0:T(8,128)(2,1)S(1)}, bf16[640,144]{1,0:T(8,128)(2,1)S(1)}, bf16[64,640]{1,0:T(8,128)(2,1)S(1)}) custom-call(f32[9,64]{1,0:T(8,128)} %first_taps_any.1, f32[9,64]{1,0:T(8,128)} %second_taps_any.1, f32[1,64]{1,0:T(1,128)} %bitcast.7, bf16[144,1792]{1,0:T(8,128)(2,1)} %constant.44.clone.choose_any, ...), custom_call_target="tpu_custom_call" | custom-call | tf_op jit(solution)/shard_map/tables/pallas_call | solution.py:207
  17.3 0.0 collective-permute-done.refs_8_
  17.3 0.8 collective-permute-done.1.refs_9_
  18.2 1.6 %all-to-all-done.in_ref = f32[8,40,128]{2,1,0:T(8,128)S(1)} async-done(((f32[8,40,128]{2,1,0:T(8,128)}), f32[8,40,128]{2,1,0:T(8,128)S(1)}, u32[]{:S(2)}, u32[]{:S(2)}) %all-to-all-start) | async-done | bytes 163872 | tf_op jit(solution)/shard_map/all_to_all | solution.py:651
  19.7 0.1 repack.1.refs_0_
  19.8 2.8 %collective-permute-start.4 = (f32[33,8,128]{2,1,0:T(8,128)S(1)}, f32[33,8,128]{2,1,0:T(8,128)S(1)}, u32[]{:S(2)}, u32[]{:S(2)}) collective-permute-start(f32[33,8,128]{2,1,0:T(8,128)S(1)} %repack.1.refs_0_), channel_id=1, source_target_pairs={{0,192},{64,0},{128,64},{192,128},{1,193},{65,1},{129,65},{193,129... | collective-permute-start | bytes 405512 | tf_op jit(solution)/shard_map/ppermute | solution.py:666
  22.6 0.3 collective-permute-start.3
  22.9 0.7 collective-permute-start.2
  23.6 3.8 %collective-permute-start.5 = (f32[33,8,128]{2,1,0:T(8,128)S(1)}, f32[33,8,128]{2,1,0:T(8,128)S(1)}, u32[]{:S(2)}, u32[]{:S(2)}) collective-permute-start(f32[33,8,128]{2,1,0:T(8,128)S(1)} %repack.1.refs_0_), channel_id=1, source_target_pairs={{0,4},{4,0},{1,5},{5,1},{2,6},{6,2},{3,7},{7,3},{8,12},{12,8},{9,1... | collective-permute-start | bytes 405512 | tf_op jit(solution)/shard_map/ppermute | solution.py:667
  27.4 0.0 collective-permute-done.4.refs_3_
  27.4 2.4 %collective-permute-start.8 = (f32[33,8,128]{2,1,0:T(8,128)S(1)}, f32[33,8,128]{2,1,0:T(8,128)S(1)}, u32[]{:S(2)}, u32[]{:S(2)}) collective-permute-start(f32[33,8,128]{2,1,0:T(8,128)S(1)} %collective-permute-done.4.refs_3_), channel_id=1, source_target_pairs={{0,4},{4,0},{1,5},{5,1},{2,6},{6,2},{3,7},{7,3},{8,12},{12,8},{9,1... | collective-permute-start | bytes 405512 | tf_op jit(solution)/shard_map/ppermute | solution.py:667
  29.8 0.0 collective-permute-done.3.refs_2_
  29.8 2.6 %collective-permute-start.7 = (f32[33,8,128]{2,1,0:T(8,128)S(1)}, f32[33,8,128]{2,1,0:T(8,128)S(1)}, u32[]{:S(2)}, u32[]{:S(2)}) collective-permute-start(f32[33,8,128]{2,1,0:T(8,128)S(1)} %collective-permute-done.3.refs_2_), channel_id=1, source_target_pairs={{0,4},{4,0},{1,5},{5,1},{2,6},{6,2},{3,7},{7,3},{8,12},{12,8},{9,1... | collective-permute-start | bytes 405512 | tf_op jit(solution)/shard_map/ppermute | solution.py:667
  32.4 0.0 collective-permute-done.2.refs_1_
  32.4 1.3 %collective-permute-start.6 = (f32[33,8,128]{2,1,0:T(8,128)S(1)}, f32[33,8,128]{2,1,0:T(8,128)S(1)}, u32[]{:S(2)}, u32[]{:S(2)}) collective-permute-start(f32[33,8,128]{2,1,0:T(8,128)S(1)} %collective-permute-done.2.refs_1_), channel_id=1, source_target_pairs={{0,4},{4,0},{1,5},{5,1},{2,6},{6,2},{3,7},{7,3},{8,12},{12,8},{9,1... | collective-permute-start | bytes 405512 | tf_op jit(solution)/shard_map/ppermute | solution.py:667
  33.8 0.0 collective-permute-done.5.refs_4_
  33.8 0.0 collective-permute-done.8.refs_7_
  33.8 0.0 collective-permute-done.7.refs_6_
  33.8 1.0 collective-permute-done.6.refs_5_
  34.8 8.5 %fields.1 = (f32[4,8,128]{2,1,0:T(8,128)S(1)}, f32[24,32,1024]{2,1,0:T(8,128)S(1)}, f32[16,2048]{1,0:T(8,128)S(1)}, f32[16,2048]{1,0:T(8,128)S(1)}, f32[32,128]{1,0:T(8,128)S(1)}, /*index=5*/f32[32,128]{1,0:T(8,128)S(1)}) custom-call(f32[33,8,128]{2,1,0:T(8,128)S(1)} %repack.1.refs_0_, f32[33,8,128]{2,1,0:T(8,128)S(1)} %collective-permute-done.2.refs_1_, ...), custom_call_target="tpu_custom_call" | custom-call | tf_op jit(solution)/shard_map/fields/pallas_call | solution.py:587
  43.2 1.3 %collective-permute-start.9 = (f32[32,128]{1,0:T(8,128)S(1)}, f32[32,128]{1,0:T(8,128)S(1)}, u32[]{:S(2)}, u32[]{:S(2)}) collective-permute-start(f32[32,128]{1,0:T(8,128)S(1)} %get-tuple-element.36), channel_id=1, source_target_pairs={{0,1},{1,2},{2,3},{3,0},{4,5},{5,6},{6,7},{7,4},{8,9},{9,10},{10,1... | collective-permute-start | bytes 49160 | tf_op jit(solution)/shard_map/ppermute | solution.py:673
  44.5 1.5 %collective-permute-start.10 = (f32[32,128]{1,0:T(8,128)S(1)}, f32[32,128]{1,0:T(8,128)S(1)}, u32[]{:S(2)}, u32[]{:S(2)}) collective-permute-start(f32[32,128]{1,0:T(8,128)S(1)} %get-tuple-element.37), channel_id=1, source_target_pairs={{1,0},{2,1},{3,2},{0,3},{5,4},{6,5},{7,6},{4,7},{9,8},{10,9},{11,1... | collective-permute-start | bytes 49160 | tf_op jit(solution)/shard_map/ppermute | solution.py:674
  46.7 2.5 %middle.1 = (f32[48,1536]{1,0:T(8,128)S(1)}, f32[640,1536]{1,0:T(8,128)S(1)}) custom-call(f32[16,2048]{1,0:T(8,128)S(1)} %get-tuple-element.34.field_ref, bf16[896,160]{1,0:T(8,128)(2,1)S(1)} %get-tuple-element.38.first_ref, bf16[96,896]{1,0:T(8,128)(2,1)S(1)} %get-tuple-element.39.second_ref), custom_call_target="tpu_custom_call" | custom-call | tf_op jit(solution)/shard_map/middle/pallas_call | solution.py:341
  49.2 0.0 collective-permute-done.9.left_ref
  49.2 0.0 collective-permute-done.10.right_ref
  49.2 5.3 %resist.1 = (f32[8,2048]{1,0:T(8,128)}, f32[64,24,128]{2,1,0:T(8,128)S(1)}) custom-call(f32[16,2048]{1,0:T(8,128)S(1)} %get-tuple-element.34.field_ref, f32[16,2048]{1,0:T(8,128)S(1)} %get-tuple-element.35.target_ref, f32[32,128]{1,0:T(8,128)S(1)} %collective-permute-done.9.left_ref, f32[32,128]{1,0:T(8,128)S(1)} %collective-permute-done.10.right_ref, ...), custom_call_target="tpu_custom_call" | custom-call | tf_op jit(solution)/shard_map/resist/pallas_call | solution.py:355
  54.5 27.9 %all_to_all.15 = f32[64,24,128]{2,1,0:T(8,128)S(1)} all-to-all(f32[64,24,128]{2,1,0:T(8,128)S(1)} %get-tuple-element.46), channel_id=1, replica_groups=mesh['y'=4,'z'=8,'core'=2,'x'=4] {'y','z','core'}, dimensions={0} | all-to-all | bytes 1572864 | tf_op jit(solution)/shard_map/all_to_all | solution.py:682
  82.4 1.8 %adjoint.1.x_ref = f32[2,2,24,128]{3,2,1,0:T(8,128)S(1)} custom-call(f32[1536,128]{1,0:T(8,128)S(1)} %bitcast.5, f32[4,8,128]{2,1,0:T(8,128)S(1)} %get-tuple-element.47.columns_ref, bf16[256,256]{1,0:T(8,128)(2,1)} %constant.53.clone.table_any, f32[16,128]{1,0:T(8,128)} %constant.54.clone.turn_any), custom_call_target="tpu_custom_call" | custom-call | tf_op jit(solution)/shard_map/adjoint/pallas_call | solution.py:684
  84.1 1.6 %collective-permute-start.13 = (f32[2,2,24,128]{3,2,1,0:T(8,128)S(1)}, f32[2,2,24,128]{3,2,1,0:T(8,128)S(1)}, u32[]{:S(2)}, u32[]{:S(2)}) collective-permute-start(f32[2,2,24,128]{3,2,1,0:T(8,128)S(1)} %adjoint.1.x_ref), channel_id=1, source_target_pairs={{0,3},{1,0},{2,1},{3,2},{4,7},{5,4},{6,5},{7,6},{8,11},{9,8},{10,9... | collective-permute-start | bytes 147464 | tf_op jit(solution)/shard_map/ppermute | solution.py:697
  85.7 0.3 collective-permute-start.12
  86.1 0.5 collective-permute-start.11
  86.6 0.5 collective-permute-done.13.three_ref
  87.2 3.1 %collective-permute-done.12.two_ref = f32[2,2,24,128]{3,2,1,0:T(8,128)S(1)} collective-permute-done((f32[2,2,24,128]{3,2,1,0:T(8,128)S(1)}, f32[2,2,24,128]{3,2,1,0:T(8,128)S(1)}, u32[]{:S(2)}, u32[]{:S(2)}) %collective-permute-start.12) | collective-permute-done | bytes 49184 | tf_op jit(solution)/shard_map/ppermute | solution.py:697
  90.2 0.5 collective-permute-done.11.one_ref
  90.8 16.7 %all_to_all.16.squares_ref = f32[64,1,128]{2,1,0:T(1,128)S(1)} all-to-all(f32[64,1,128]{2,1,0:T(1,128)S(1)} %get-tuple-element.49), channel_id=1, replica_groups=mesh['y'=4,'z'=8,'core'=2,'x'=4] {'y','z','core'}, dimensions={0} | all-to-all | bytes 65536 | tf_op jit(solution)/shard_map/all_to_all | solution.py:706
  107.5 0.8 scale.1
  (1 shorter events, 0.0 us)
Async XLA Ops:
  2.6 17.2 %all-to-all-start = ((f32[8,40,128]{2,1,0:T(8,128)}), f32[8,40,128]{2,1,0:T(8,128)S(1)}, u32[]{:S(2)}, u32[]{:S(2)}) async-start(f32[8,40,128]{2,1,0:T(8,128)} %analyse.1), calls=%async_computation | async-start | bytes 327680 | tf_op jit(solution)/shard_map/all_to_all | solution.py:651
  11.6 5.7 %collective-permute-start = (bf16[8,2048]{1,0:T(8,128)(2,1)}, bf16[8,2048]{1,0:T(8,128)(2,1)S(1)}, u32[]{:S(2)}, u32[]{:S(2)}) collective-permute-start(bf16[8,2048]{1,0:T(8,128)(2,1)} %refs_15_.1), channel_id=1, source_target_pairs={{0,4},{4,0},{8,12},{12,8},{16,20},{20,16},{24,28},{28,24},{32,36},... | collective-permute-start | bytes 98312 | tf_op jit(solution)/shard_map/ppermute | solution.py:635
  12.6 5.6 %collective-permute-start.1 = (bf16[8,2048]{1,0:T(8,128)(2,1)}, bf16[8,2048]{1,0:T(8,128)(2,1)S(1)}, u32[]{:S(2)}, u32[]{:S(2)}) collective-permute-start(bf16[8,2048]{1,0:T(8,128)(2,1)} %refs_15_.1), channel_id=1, source_target_pairs={{0,252},{4,8},{8,4},{12,16},{16,12},{20,24},{24,20},{28,32},{32,28... | collective-permute-start | bytes 98312 | tf_op jit(solution)/shard_map/ppermute | solution.py:636
  19.8 7.6 %collective-permute-start.4 = (f32[33,8,128]{2,1,0:T(8,128)S(1)}, f32[33,8,128]{2,1,0:T(8,128)S(1)}, u32[]{:S(2)}, u32[]{:S(2)}) collective-permute-start(f32[33,8,128]{2,1,0:T(8,128)S(1)} %repack.1.refs_0_), channel_id=1, source_target_pairs={{0,192},{64,0},{128,64},{192,128},{1,193},{65,1},{129,65},{193,129... | collective-permute-start | bytes 405512 | tf_op jit(solution)/shard_map/ppermute | solution.py:666
  22.6 7.2 %collective-permute-start.3 = (f32[33,8,128]{2,1,0:T(8,128)S(1)}, f32[33,8,128]{2,1,0:T(8,128)S(1)}, u32[]{:S(2)}, u32[]{:S(2)}) collective-permute-start(f32[33,8,128]{2,1,0:T(8,128)S(1)} %repack.1.refs_0_), channel_id=1, source_target_pairs={{0,128},{64,192},{128,0},{192,64},{1,129},{65,193},{129,1},{193,65... | collective-permute-start | bytes 405512 | tf_op jit(solution)/shard_map/ppermute | solution.py:666
  22.9 9.5 %collective-permute-start.2 = (f32[33,8,128]{2,1,0:T(8,128)S(1)}, f32[33,8,128]{2,1,0:T(8,128)S(1)}, u32[]{:S(2)}, u32[]{:S(2)}) collective-permute-start(f32[33,8,128]{2,1,0:T(8,128)S(1)} %repack.1.refs_0_), channel_id=1, source_target_pairs={{0,64},{64,128},{128,192},{192,0},{1,65},{65,129},{129,193},{193,1... | collective-permute-start | bytes 405512 | tf_op jit(solution)/shard_map/ppermute | solution.py:666
  23.6 10.2 %collective-permute-start.5 = (f32[33,8,128]{2,1,0:T(8,128)S(1)}, f32[33,8,128]{2,1,0:T(8,128)S(1)}, u32[]{:S(2)}, u32[]{:S(2)}) collective-permute-start(f32[33,8,128]{2,1,0:T(8,128)S(1)} %repack.1.refs_0_), channel_id=1, source_target_pairs={{0,4},{4,0},{1,5},{5,1},{2,6},{6,2},{3,7},{7,3},{8,12},{12,8},{9,1... | collective-permute-start | bytes 405512 | tf_op jit(solution)/shard_map/ppermute | solution.py:667
  27.4 6.4 %collective-permute-start.8 = (f32[33,8,128]{2,1,0:T(8,128)S(1)}, f32[33,8,128]{2,1,0:T(8,128)S(1)}, u32[]{:S(2)}, u32[]{:S(2)}) collective-permute-start(f32[33,8,128]{2,1,0:T(8,128)S(1)} %collective-permute-done.4.refs_3_), channel_id=1, source_target_pairs={{0,4},{4,0},{1,5},{5,1},{2,6},{6,2},{3,7},{7,3},{8,12},{12,8},{9,1... | collective-permute-start | bytes 405512 | tf_op jit(solution)/shard_map/ppermute | solution.py:667
  29.8 4.0 %collective-permute-start.7 = (f32[33,8,128]{2,1,0:T(8,128)S(1)}, f32[33,8,128]{2,1,0:T(8,128)S(1)}, u32[]{:S(2)}, u32[]{:S(2)}) collective-permute-start(f32[33,8,128]{2,1,0:T(8,128)S(1)} %collective-permute-done.3.refs_2_), channel_id=1, source_target_pairs={{0,4},{4,0},{1,5},{5,1},{2,6},{6,2},{3,7},{7,3},{8,12},{12,8},{9,1... | collective-permute-start | bytes 405512 | tf_op jit(solution)/shard_map/ppermute | solution.py:667
  32.4 2.3 %collective-permute-start.6 = (f32[33,8,128]{2,1,0:T(8,128)S(1)}, f32[33,8,128]{2,1,0:T(8,128)S(1)}, u32[]{:S(2)}, u32[]{:S(2)}) collective-permute-start(f32[33,8,128]{2,1,0:T(8,128)S(1)} %collective-permute-done.2.refs_1_), channel_id=1, source_target_pairs={{0,4},{4,0},{1,5},{5,1},{2,6},{6,2},{3,7},{7,3},{8,12},{12,8},{9,1... | collective-permute-start | bytes 405512 | tf_op jit(solution)/shard_map/ppermute | solution.py:667
  43.2 5.9 %collective-permute-start.9 = (f32[32,128]{1,0:T(8,128)S(1)}, f32[32,128]{1,0:T(8,128)S(1)}, u32[]{:S(2)}, u32[]{:S(2)}) collective-permute-start(f32[32,128]{1,0:T(8,128)S(1)} %get-tuple-element.36), channel_id=1, source_target_pairs={{0,1},{1,2},{2,3},{3,0},{4,5},{5,6},{6,7},{7,4},{8,9},{9,10},{10,1... | collective-permute-start | bytes 49160 | tf_op jit(solution)/shard_map/ppermute | solution.py:673
  44.5 4.7 %collective-permute-start.10 = (f32[32,128]{1,0:T(8,128)S(1)}, f32[32,128]{1,0:T(8,128)S(1)}, u32[]{:S(2)}, u32[]{:S(2)}) collective-permute-start(f32[32,128]{1,0:T(8,128)S(1)} %get-tuple-element.37), channel_id=1, source_target_pairs={{1,0},{2,1},{3,2},{0,3},{5,4},{6,5},{7,6},{4,7},{9,8},{10,9},{11,1... | collective-permute-start | bytes 49160 | tf_op jit(solution)/shard_map/ppermute | solution.py:674
  84.1 3.0 %collective-permute-start.13 = (f32[2,2,24,128]{3,2,1,0:T(8,128)S(1)}, f32[2,2,24,128]{3,2,1,0:T(8,128)S(1)}, u32[]{:S(2)}, u32[]{:S(2)}) collective-permute-start(f32[2,2,24,128]{3,2,1,0:T(8,128)S(1)} %adjoint.1.x_ref), channel_id=1, source_target_pairs={{0,3},{1,0},{2,1},{3,2},{4,7},{5,4},{6,5},{7,6},{8,11},{9,8},{10,9... | collective-permute-start | bytes 147464 | tf_op jit(solution)/shard_map/ppermute | solution.py:697
  85.7 4.5 %collective-permute-start.12 = (f32[2,2,24,128]{3,2,1,0:T(8,128)S(1)}, f32[2,2,24,128]{3,2,1,0:T(8,128)S(1)}, u32[]{:S(2)}, u32[]{:S(2)}) collective-permute-start(f32[2,2,24,128]{3,2,1,0:T(8,128)S(1)} %adjoint.1.x_ref), channel_id=1, source_target_pairs={{0,2},{1,3},{2,0},{3,1},{4,6},{5,7},{6,4},{7,5},{8,10},{9,11},{10,... | collective-permute-start | bytes 147464 | tf_op jit(solution)/shard_map/ppermute | solution.py:697
  86.1 4.6 %collective-permute-start.11 = (f32[2,2,24,128]{3,2,1,0:T(8,128)S(1)}, f32[2,2,24,128]{3,2,1,0:T(8,128)S(1)}, u32[]{:S(2)}, u32[]{:S(2)}) collective-permute-start(f32[2,2,24,128]{3,2,1,0:T(8,128)S(1)} %adjoint.1.x_ref), channel_id=1, source_target_pairs={{0,1},{1,2},{2,3},{3,0},{4,5},{5,6},{6,7},{7,4},{8,9},{9,10},{10,1... | collective-permute-start | bytes 147464 | tf_op jit(solution)/shard_map/ppermute | solution.py:697

commit v5 on v4

--- a/solution.py
+++ b/solution.py
@@ -245,12 +245,12 @@
     views_ref[144:160] = jnp.ones((16, width), jnp.bfloat16)
 
     def step(i, carry):
-        at = pl.multiple_of(i * 256, 256)
-        there = pl.ds(pl.multiple_of(at + SIDE, 256), 256)
-        mixed_ref[:, pl.ds(at, 256)], keep_ref[:, pl.ds(at, 256)] = hide(first_ref, second_ref, views_ref, there, keep_ref.shape[0])
+        at = pl.multiple_of(i * 768, 256)
+        there = pl.ds(pl.multiple_of(at + SIDE, 256), 768)
+        mixed_ref[:, pl.ds(at, 768)], keep_ref[:, pl.ds(at, 768)] = hide(first_ref, second_ref, views_ref, there, keep_ref.shape[0])
         return carry
 
-    lax.fori_loop(0, (width - 2 * SIDE) // 256, step, 0, unroll=3)
+    lax.fori_loop(0, (width - 2 * SIDE) // 768, step, 0)
 
 
 def resist_kernel(
@@ -344,7 +344,7 @@
         in_specs=[VMEM] * 3,
         out_specs=[VMEM] * 2,
         scratch_shapes=[pltpu.VMEM((160, width), jnp.bfloat16)],
-        compiler_params=params(16),
+        compiler_params=params(24),
         name="middle",
     )(*near(field, tables[0], tables[1]))
 

time: 109 us -> 109 us (level)
  no operation moved by 1% of the time
where the time goes in v5:
time: 109 us; the launch traced here: 108 us
  blocking collectives  44.6 us (41%)
  starting transfers between devices  31 us (28%)
  Pallas kernels  22.6 us (21%)
  waiting for transfers between devices  7.68 us (7%)
  between operations  1.38 us (1%)
    all_to_all x1, blocking collectives, on_device(): got = lax.all_to_all(send, ROW, 0, 0, tiled=True)  27.9 us
    all_to_all x1, blocking collectives, on_device(): squares = lax.all_to_all(squares, ROW, 0, 0, tiled=True)  16.7 us
    ppermute x4, starting transfers between devices, on_device(): lax.ppermute(slab, 'core', [(0, 1), (1, 0)])  10.1 us
    all_to_all x1, starting transfers between devices, on_device(): gathered = lax.all_to_all(packed, 'z', 0, 0, tiled=True)  9.03 us
    pallas_call x1, Pallas kernels, fields_block(): pl.pallas_call(functools.partial(fields_kernel, rows=rows, norm=norm), ou...  8.48 us
    pallas_call x1, Pallas kernels, resist_block(): pl.pallas_call(functools.partial(resist_kernel, rows=rows, cols=cols), ou...  5.29 us
    ppermute x3, waiting for transfers between devices, on_device(): lax.ppermute(mine, 'x', [(i, (i + k) % 4) for i in range(4)])  4.29 us
    ppermute x3, starting transfers between devices, on_device(): lax.ppermute(gathered, 'y', [(i, (i + k) % 4) for i in range(4)])  3.8 us
  transfers between devices with their start and end apart: 15, of which 6 were waited for; matrix products, arithmetic and copies ran while one was open for 1% of the time, Pallas kernels for 4%

profile of v5, /device:TPU:1, one launch (start us, length us, event | category | flops | bytes accessed | tf_op | source)
XLA Modules:
  0.0 108.3 jit_solution(6105795189028815200)
XLA Ops:
  0.6 1.9 %analyse.1 = f32[8,40,128]{2,1,0:T(8,128)} custom-call(bf16[8,2048]{1,0:T(8,128)(2,1)} %layout_any.1, bf16[1024,256]{1,0:T(8,128)(2,1)} %constant.43.clone.table_any), custom_call_target="tpu_custom_call" | custom-call | tf_op jit(solution)/shard_map/analyse/pallas_call | solution.py:638
  2.6 9.0 %all-to-all-start = ((f32[8,40,128]{2,1,0:T(8,128)}), f32[8,40,128]{2,1,0:T(8,128)S(1)}, u32[]{:S(2)}, u32[]{:S(2)}) async-start(f32[8,40,128]{2,1,0:T(8,128)} %analyse.1), calls=%async_computation | async-start | bytes 327680 | tf_op jit(solution)/shard_map/all_to_all | solution.py:651
  11.6 1.0 collective-permute-start
  12.6 1.6 %collective-permute-start.1 = (bf16[8,2048]{1,0:T(8,128)(2,1)}, bf16[8,2048]{1,0:T(8,128)(2,1)S(1)}, u32[]{:S(2)}, u32[]{:S(2)}) collective-permute-start(bf16[8,2048]{1,0:T(8,128)(2,1)} %refs_15_.1), channel_id=1, source_target_pairs={{0,252},{4,8},{8,4},{12,16},{16,12},{20,24},{24,20},{28,32},{32,28... | collective-permute-start | bytes 98312 | tf_op jit(solution)/shard_map/ppermute | solution.py:636
  14.2 1.1 dynamic-slice_bitcast_fusion.refs_10_
  15.3 2.1 %tables.1 = (bf16[896,160]{1,0:T(8,128)(2,1)S(1)}, bf16[96,896]{1,0:T(8,128)(2,1)S(1)}, bf16[640,144]{1,0:T(8,128)(2,1)S(1)}, bf16[64,640]{1,0:T(8,128)(2,1)S(1)}) custom-call(f32[9,64]{1,0:T(8,128)} %first_taps_any.1, f32[9,64]{1,0:T(8,128)} %second_taps_any.1, f32[1,64]{1,0:T(1,128)} %bitcast.7, bf16[144,1792]{1,0:T(8,128)(2,1)} %constant.44.clone.choose_any, ...), custom_call_target="tpu_custom_call" | custom-call | tf_op jit(solution)/shard_map/tables/pallas_call | solution.py:207
  17.3 0.0 collective-permute-done.refs_8_
  17.3 0.8 collective-permute-done.1.refs_9_
  18.2 1.6 %all-to-all-done.in_ref = f32[8,40,128]{2,1,0:T(8,128)S(1)} async-done(((f32[8,40,128]{2,1,0:T(8,128)}), f32[8,40,128]{2,1,0:T(8,128)S(1)}, u32[]{:S(2)}, u32[]{:S(2)}) %all-to-all-start) | async-done | bytes 163872 | tf_op jit(solution)/shard_map/all_to_all | solution.py:651
  19.7 0.1 repack.1.refs_0_
  19.8 2.8 %collective-permute-start.4 = (f32[33,8,128]{2,1,0:T(8,128)S(1)}, f32[33,8,128]{2,1,0:T(8,128)S(1)}, u32[]{:S(2)}, u32[]{:S(2)}) collective-permute-start(f32[33,8,128]{2,1,0:T(8,128)S(1)} %repack.1.refs_0_), channel_id=1, source_target_pairs={{0,192},{64,0},{128,64},{192,128},{1,193},{65,1},{129,65},{193,129... | collective-permute-start | bytes 405512 | tf_op jit(solution)/shard_map/ppermute | solution.py:666
  22.6 0.3 collective-permute-start.3
  22.9 0.7 collective-permute-start.2
  23.6 3.8 %collective-permute-start.5 = (f32[33,8,128]{2,1,0:T(8,128)S(1)}, f32[33,8,128]{2,1,0:T(8,128)S(1)}, u32[]{:S(2)}, u32[]{:S(2)}) collective-permute-start(f32[33,8,128]{2,1,0:T(8,128)S(1)} %repack.1.refs_0_), channel_id=1, source_target_pairs={{0,4},{4,0},{1,5},{5,1},{2,6},{6,2},{3,7},{7,3},{8,12},{12,8},{9,1... | collective-permute-start | bytes 405512 | tf_op jit(solution)/shard_map/ppermute | solution.py:667
  27.4 0.0 collective-permute-done.4.refs_3_
  27.4 2.4 %collective-permute-start.8 = (f32[33,8,128]{2,1,0:T(8,128)S(1)}, f32[33,8,128]{2,1,0:T(8,128)S(1)}, u32[]{:S(2)}, u32[]{:S(2)}) collective-permute-start(f32[33,8,128]{2,1,0:T(8,128)S(1)} %collective-permute-done.4.refs_3_), channel_id=1, source_target_pairs={{0,4},{4,0},{1,5},{5,1},{2,6},{6,2},{3,7},{7,3},{8,12},{12,8},{9,1... | collective-permute-start | bytes 405512 | tf_op jit(solution)/shard_map/ppermute | solution.py:667
  29.8 0.0 collective-permute-done.3.refs_2_
  29.8 2.6 %collective-permute-start.7 = (f32[33,8,128]{2,1,0:T(8,128)S(1)}, f32[33,8,128]{2,1,0:T(8,128)S(1)}, u32[]{:S(2)}, u32[]{:S(2)}) collective-permute-start(f32[33,8,128]{2,1,0:T(8,128)S(1)} %collective-permute-done.3.refs_2_), channel_id=1, source_target_pairs={{0,4},{4,0},{1,5},{5,1},{2,6},{6,2},{3,7},{7,3},{8,12},{12,8},{9,1... | collective-permute-start | bytes 405512 | tf_op jit(solution)/shard_map/ppermute | solution.py:667
  32.4 0.0 collective-permute-done.2.refs_1_
  32.4 1.3 %collective-permute-start.6 = (f32[33,8,128]{2,1,0:T(8,128)S(1)}, f32[33,8,128]{2,1,0:T(8,128)S(1)}, u32[]{:S(2)}, u32[]{:S(2)}) collective-permute-start(f32[33,8,128]{2,1,0:T(8,128)S(1)} %collective-permute-done.2.refs_1_), channel_id=1, source_target_pairs={{0,4},{4,0},{1,5},{5,1},{2,6},{6,2},{3,7},{7,3},{8,12},{12,8},{9,1... | collective-permute-start | bytes 405512 | tf_op jit(solution)/shard_map/ppermute | solution.py:667
  33.8 0.0 collective-permute-done.5.refs_4_
  33.8 0.0 collective-permute-done.8.refs_7_
  33.8 0.0 collective-permute-done.7.refs_6_
  33.8 1.0 collective-permute-done.6.refs_5_
  34.8 8.5 %fields.1 = (f32[4,8,128]{2,1,0:T(8,128)S(1)}, f32[24,32,1024]{2,1,0:T(8,128)S(1)}, f32[16,2048]{1,0:T(8,128)S(1)}, f32[16,2048]{1,0:T(8,128)S(1)}, f32[32,128]{1,0:T(8,128)S(1)}, /*index=5*/f32[32,128]{1,0:T(8,128)S(1)}) custom-call(f32[33,8,128]{2,1,0:T(8,128)S(1)} %repack.1.refs_0_, f32[33,8,128]{2,1,0:T(8,128)S(1)} %collective-permute-done.2.refs_1_, ...), custom_call_target="tpu_custom_call" | custom-call | tf_op jit(solution)/shard_map/fields/pallas_call | solution.py:587
  43.2 1.3 %collective-permute-start.9 = (f32[32,128]{1,0:T(8,128)S(1)}, f32[32,128]{1,0:T(8,128)S(1)}, u32[]{:S(2)}, u32[]{:S(2)}) collective-permute-start(f32[32,128]{1,0:T(8,128)S(1)} %get-tuple-element.36), channel_id=1, source_target_pairs={{0,1},{1,2},{2,3},{3,0},{4,5},{5,6},{6,7},{7,4},{8,9},{9,10},{10,1... | collective-permute-start | bytes 49160 | tf_op jit(solution)/shard_map/ppermute | solution.py:673
  44.5 1.5 %collective-permute-start.10 = (f32[32,128]{1,0:T(8,128)S(1)}, f32[32,128]{1,0:T(8,128)S(1)}, u32[]{:S(2)}, u32[]{:S(2)}) collective-permute-start(f32[32,128]{1,0:T(8,128)S(1)} %get-tuple-element.37), channel_id=1, source_target_pairs={{1,0},{2,1},{3,2},{0,3},{5,4},{6,5},{7,6},{4,7},{9,8},{10,9},{11,1... | collective-permute-start | bytes 49160 | tf_op jit(solution)/shard_map/ppermute | solution.py:674
  46.7 2.1 %middle.1 = (f32[48,1536]{1,0:T(8,128)S(1)}, f32[640,1536]{1,0:T(8,128)S(1)}) custom-call(f32[16,2048]{1,0:T(8,128)S(1)} %get-tuple-element.34.field_ref, bf16[896,160]{1,0:T(8,128)(2,1)S(1)} %get-tuple-element.38.first_ref, bf16[96,896]{1,0:T(8,128)(2,1)S(1)} %get-tuple-element.39.second_ref), custom_call_target="tpu_custom_call" | custom-call | tf_op jit(solution)/shard_map/middle/pallas_call | solution.py:341
  48.8 0.0 collective-permute-done.9.left_ref
  48.9 0.0 collective-permute-done.10.right_ref
  48.9 5.3 %resist.1 = (f32[8,2048]{1,0:T(8,128)}, f32[64,24,128]{2,1,0:T(8,128)S(1)}) custom-call(f32[16,2048]{1,0:T(8,128)S(1)} %get-tuple-element.34.field_ref, f32[16,2048]{1,0:T(8,128)S(1)} %get-tuple-element.35.target_ref, f32[32,128]{1,0:T(8,128)S(1)} %collective-permute-done.9.left_ref, f32[32,128]{1,0:T(8,128)S(1)} %collective-permute-done.10.right_ref, ...), custom_call_target="tpu_custom_call" | custom-call | tf_op jit(solution)/shard_map/resist/pallas_call | solution.py:355
  54.2 27.9 %all_to_all.15 = f32[64,24,128]{2,1,0:T(8,128)S(1)} all-to-all(f32[64,24,128]{2,1,0:T(8,128)S(1)} %get-tuple-element.46), channel_id=1, replica_groups=mesh['y'=4,'z'=8,'core'=2,'x'=4] {'y','z','core'}, dimensions={0} | all-to-all | bytes 1572864 | tf_op jit(solution)/shard_map/all_to_all | solution.py:682
  82.0 1.8 %adjoint.1.x_ref = f32[2,2,24,128]{3,2,1,0:T(8,128)S(1)} custom-call(f32[1536,128]{1,0:T(8,128)S(1)} %bitcast.5, f32[4,8,128]{2,1,0:T(8,128)S(1)} %get-tuple-element.47.columns_ref, bf16[256,256]{1,0:T(8,128)(2,1)} %constant.53.clone.table_any, f32[16,128]{1,0:T(8,128)} %constant.54.clone.turn_any), custom_call_target="tpu_custom_call" | custom-call | tf_op jit(solution)/shard_map/adjoint/pallas_call | solution.py:684
  83.8 2.0 %collective-permute-start.13 = (f32[2,2,24,128]{3,2,1,0:T(8,128)S(1)}, f32[2,2,24,128]{3,2,1,0:T(8,128)S(1)}, u32[]{:S(2)}, u32[]{:S(2)}) collective-permute-start(f32[2,2,24,128]{3,2,1,0:T(8,128)S(1)} %adjoint.1.x_ref), channel_id=1, source_target_pairs={{0,3},{1,0},{2,1},{3,2},{4,7},{5,4},{6,5},{7,6},{8,11},{9,8},{10,9... | collective-permute-start | bytes 147464 | tf_op jit(solution)/shard_map/ppermute | solution.py:697
  85.7 0.3 collective-permute-start.12
  86.1 0.4 collective-permute-start.11
  86.4 0.5 collective-permute-done.13.three_ref
  86.9 3.3 %collective-permute-done.12.two_ref = f32[2,2,24,128]{3,2,1,0:T(8,128)S(1)} collective-permute-done((f32[2,2,24,128]{3,2,1,0:T(8,128)S(1)}, f32[2,2,24,128]{3,2,1,0:T(8,128)S(1)}, u32[]{:S(2)}, u32[]{:S(2)}) %collective-permute-start.12) | collective-permute-done | bytes 49184 | tf_op jit(solution)/shard_map/ppermute | solution.py:697
  90.2 0.5 collective-permute-done.11.one_ref
  90.8 16.7 %all_to_all.16.squares_ref = f32[64,1,128]{2,1,0:T(1,128)S(1)} all-to-all(f32[64,1,128]{2,1,0:T(1,128)S(1)} %get-tuple-element.49), channel_id=1, replica_groups=mesh['y'=4,'z'=8,'core'=2,'x'=4] {'y','z','core'}, dimensions={0} | all-to-all | bytes 65536 | tf_op jit(solution)/shard_map/all_to_all | solution.py:706
  107.5 0.8 scale.1
  (1 shorter events, 0.0 us)
Async XLA Ops:
  2.6 17.2 %all-to-all-start = ((f32[8,40,128]{2,1,0:T(8,128)}), f32[8,40,128]{2,1,0:T(8,128)S(1)}, u32[]{:S(2)}, u32[]{:S(2)}) async-start(f32[8,40,128]{2,1,0:T(8,128)} %analyse.1), calls=%async_computation | async-start | bytes 327680 | tf_op jit(solution)/shard_map/all_to_all | solution.py:651
  11.6 5.7 %collective-permute-start = (bf16[8,2048]{1,0:T(8,128)(2,1)}, bf16[8,2048]{1,0:T(8,128)(2,1)S(1)}, u32[]{:S(2)}, u32[]{:S(2)}) collective-permute-start(bf16[8,2048]{1,0:T(8,128)(2,1)} %refs_15_.1), channel_id=1, source_target_pairs={{0,4},{4,0},{8,12},{12,8},{16,20},{20,16},{24,28},{28,24},{32,36},... | collective-permute-start | bytes 98312 | tf_op jit(solution)/shard_map/ppermute | solution.py:635
  12.6 5.6 %collective-permute-start.1 = (bf16[8,2048]{1,0:T(8,128)(2,1)}, bf16[8,2048]{1,0:T(8,128)(2,1)S(1)}, u32[]{:S(2)}, u32[]{:S(2)}) collective-permute-start(bf16[8,2048]{1,0:T(8,128)(2,1)} %refs_15_.1), channel_id=1, source_target_pairs={{0,252},{4,8},{8,4},{12,16},{16,12},{20,24},{24,20},{28,32},{32,28... | collective-permute-start | bytes 98312 | tf_op jit(solution)/shard_map/ppermute | solution.py:636
  19.8 7.6 %collective-permute-start.4 = (f32[33,8,128]{2,1,0:T(8,128)S(1)}, f32[33,8,128]{2,1,0:T(8,128)S(1)}, u32[]{:S(2)}, u32[]{:S(2)}) collective-permute-start(f32[33,8,128]{2,1,0:T(8,128)S(1)} %repack.1.refs_0_), channel_id=1, source_target_pairs={{0,192},{64,0},{128,64},{192,128},{1,193},{65,1},{129,65},{193,129... | collective-permute-start | bytes 405512 | tf_op jit(solution)/shard_map/ppermute | solution.py:666
  22.6 7.2 %collective-permute-start.3 = (f32[33,8,128]{2,1,0:T(8,128)S(1)}, f32[33,8,128]{2,1,0:T(8,128)S(1)}, u32[]{:S(2)}, u32[]{:S(2)}) collective-permute-start(f32[33,8,128]{2,1,0:T(8,128)S(1)} %repack.1.refs_0_), channel_id=1, source_target_pairs={{0,128},{64,192},{128,0},{192,64},{1,129},{65,193},{129,1},{193,65... | collective-permute-start | bytes 405512 | tf_op jit(solution)/shard_map/ppermute | solution.py:666
  22.9 9.5 %collective-permute-start.2 = (f32[33,8,128]{2,1,0:T(8,128)S(1)}, f32[33,8,128]{2,1,0:T(8,128)S(1)}, u32[]{:S(2)}, u32[]{:S(2)}) collective-permute-start(f32[33,8,128]{2,1,0:T(8,128)S(1)} %repack.1.refs_0_), channel_id=1, source_target_pairs={{0,64},{64,128},{128,192},{192,0},{1,65},{65,129},{129,193},{193,1... | collective-permute-start | bytes 405512 | tf_op jit(solution)/shard_map/ppermute | solution.py:666
  23.6 10.2 %collective-permute-start.5 = (f32[33,8,128]{2,1,0:T(8,128)S(1)}, f32[33,8,128]{2,1,0:T(8,128)S(1)}, u32[]{:S(2)}, u32[]{:S(2)}) collective-permute-start(f32[33,8,128]{2,1,0:T(8,128)S(1)} %repack.1.refs_0_), channel_id=1, source_target_pairs={{0,4},{4,0},{1,5},{5,1},{2,6},{6,2},{3,7},{7,3},{8,12},{12,8},{9,1... | collective-permute-start | bytes 405512 | tf_op jit(solution)/shard_map/ppermute | solution.py:667
  27.4 6.4 %collective-permute-start.8 = (f32[33,8,128]{2,1,0:T(8,128)S(1)}, f32[33,8,128]{2,1,0:T(8,128)S(1)}, u32[]{:S(2)}, u32[]{:S(2)}) collective-permute-start(f32[33,8,128]{2,1,0:T(8,128)S(1)} %collective-permute-done.4.refs_3_), channel_id=1, source_target_pairs={{0,4},{4,0},{1,5},{5,1},{2,6},{6,2},{3,7},{7,3},{8,12},{12,8},{9,1... | collective-permute-start | bytes 405512 | tf_op jit(solution)/shard_map/ppermute | solution.py:667
  29.8 4.0 %collective-permute-start.7 = (f32[33,8,128]{2,1,0:T(8,128)S(1)}, f32[33,8,128]{2,1,0:T(8,128)S(1)}, u32[]{:S(2)}, u32[]{:S(2)}) collective-permute-start(f32[33,8,128]{2,1,0:T(8,128)S(1)} %collective-permute-done.3.refs_2_), channel_id=1, source_target_pairs={{0,4},{4,0},{1,5},{5,1},{2,6},{6,2},{3,7},{7,3},{8,12},{12,8},{9,1... | collective-permute-start | bytes 405512 | tf_op jit(solution)/shard_map/ppermute | solution.py:667
  32.4 2.3 %collective-permute-start.6 = (f32[33,8,128]{2,1,0:T(8,128)S(1)}, f32[33,8,128]{2,1,0:T(8,128)S(1)}, u32[]{:S(2)}, u32[]{:S(2)}) collective-permute-start(f32[33,8,128]{2,1,0:T(8,128)S(1)} %collective-permute-done.2.refs_1_), channel_id=1, source_target_pairs={{0,4},{4,0},{1,5},{5,1},{2,6},{6,2},{3,7},{7,3},{8,12},{12,8},{9,1... | collective-permute-start | bytes 405512 | tf_op jit(solution)/shard_map/ppermute | solution.py:667
  43.2 5.6 %collective-permute-start.9 = (f32[32,128]{1,0:T(8,128)S(1)}, f32[32,128]{1,0:T(8,128)S(1)}, u32[]{:S(2)}, u32[]{:S(2)}) collective-permute-start(f32[32,128]{1,0:T(8,128)S(1)} %get-tuple-element.36), channel_id=1, source_target_pairs={{0,1},{1,2},{2,3},{3,0},{4,5},{5,6},{6,7},{7,4},{8,9},{9,10},{10,1... | collective-permute-start | bytes 49160 | tf_op jit(solution)/shard_map/ppermute | solution.py:673
  44.5 4.3 %collective-permute-start.10 = (f32[32,128]{1,0:T(8,128)S(1)}, f32[32,128]{1,0:T(8,128)S(1)}, u32[]{:S(2)}, u32[]{:S(2)}) collective-permute-start(f32[32,128]{1,0:T(8,128)S(1)} %get-tuple-element.37), channel_id=1, source_target_pairs={{1,0},{2,1},{3,2},{0,3},{5,4},{6,5},{7,6},{4,7},{9,8},{10,9},{11,1... | collective-permute-start | bytes 49160 | tf_op jit(solution)/shard_map/ppermute | solution.py:674
  83.8 3.1 %collective-permute-start.13 = (f32[2,2,24,128]{3,2,1,0:T(8,128)S(1)}, f32[2,2,24,128]{3,2,1,0:T(8,128)S(1)}, u32[]{:S(2)}, u32[]{:S(2)}) collective-permute-start(f32[2,2,24,128]{3,2,1,0:T(8,128)S(1)} %adjoint.1.x_ref), channel_id=1, source_target_pairs={{0,3},{1,0},{2,1},{3,2},{4,7},{5,4},{6,5},{7,6},{8,11},{9,8},{10,9... | collective-permute-start | bytes 147464 | tf_op jit(solution)/shard_map/ppermute | solution.py:697
  85.7 4.5 %collective-permute-start.12 = (f32[2,2,24,128]{3,2,1,0:T(8,128)S(1)}, f32[2,2,24,128]{3,2,1,0:T(8,128)S(1)}, u32[]{:S(2)}, u32[]{:S(2)}) collective-permute-start(f32[2,2,24,128]{3,2,1,0:T(8,128)S(1)} %adjoint.1.x_ref), channel_id=1, source_target_pairs={{0,2},{1,3},{2,0},{3,1},{4,6},{5,7},{6,4},{7,5},{8,10},{9,11},{10,... | collective-permute-start | bytes 147464 | tf_op jit(solution)/shard_map/ppermute | solution.py:697
  86.1 4.6 %collective-permute-start.11 = (f32[2,2,24,128]{3,2,1,0:T(8,128)S(1)}, f32[2,2,24,128]{3,2,1,0:T(8,128)S(1)}, u32[]{:S(2)}, u32[]{:S(2)}) collective-permute-start(f32[2,2,24,128]{3,2,1,0:T(8,128)S(1)} %adjoint.1.x_ref), channel_id=1, source_target_pairs={{0,1},{1,2},{2,3},{3,0},{4,5},{5,6},{6,7},{7,4},{8,9},{9,10},{10,1... | collective-permute-start | bytes 147464 | tf_op jit(solution)/shard_map/ppermute | solution.py:697

commit v6 on v5

--- a/solution.py
+++ b/solution.py
@@ -245,12 +245,12 @@
     views_ref[144:160] = jnp.ones((16, width), jnp.bfloat16)
 
     def step(i, carry):
-        at = pl.multiple_of(i * 768, 256)
-        there = pl.ds(pl.multiple_of(at + SIDE, 256), 768)
-        mixed_ref[:, pl.ds(at, 768)], keep_ref[:, pl.ds(at, 768)] = hide(first_ref, second_ref, views_ref, there, keep_ref.shape[0])
+        at = pl.multiple_of(i * 1536, 256)
+        there = pl.ds(pl.multiple_of(at + SIDE, 256), 1536)
+        mixed_ref[:, pl.ds(at, 1536)], keep_ref[:, pl.ds(at, 1536)] = hide(first_ref, second_ref, views_ref, there, keep_ref.shape[0])
         return carry
 
-    lax.fori_loop(0, (width - 2 * SIDE) // 768, step, 0)
+    lax.fori_loop(0, (width - 2 * SIDE) // 1536, step, 0)
 
 
 def resist_kernel(
@@ -306,11 +306,11 @@
         summed_ref[:, here] = both[:32] + both[32:] + dot(first_back_ref[0:32], lo)
 
     def middle(i, carry):
-        at = pl.multiple_of(i * 768, 256)
-        backward(pl.ds(pl.multiple_of(SIDE + at, 256), 768), keep_mid_ref[:, pl.ds(at, 768)])
+        at = pl.multiple_of(i * 1536, 256)
+        backward(pl.ds(pl.multiple_of(SIDE + at, 256), 1536), keep_mid_ref[:, pl.ds(at, 1536)])
         return carry
 
-    lax.fori_loop(0, keep_mid_ref.shape[1] // 768, middle, 0)
+    lax.fori_loop(0, keep_mid_ref.shape[1] // 1536, middle, 0)
     for here, place in zip(edges, kept, strict=True):
         backward(here, keep_ref[:, place])
     grad = summed_ref[8:16] + pltpu.roll(summed_ref[0:8], WIDE - 1, 1) + pltpu.roll(summed_ref[16:24], 1, 1)
@@ -344,7 +344,7 @@
         in_specs=[VMEM] * 3,
         out_specs=[VMEM] * 2,
         scratch_shapes=[pltpu.VMEM((160, width), jnp.bfloat16)],
-        compiler_params=params(24),
+        compiler_params=params(32),
         name="middle",
     )(*near(field, tables[0], tables[1]))
 

time: 109 us -> 110 us (level)
  no operation moved by 1% of the time
where the time goes in v6:
time: 110 us; the launch traced here: 109 us
  blocking collectives  44.6 us (41%)
  starting transfers between devices  30.9 us (28%)
  Pallas kernels  23.5 us (21%)
  waiting for transfers between devices  7.68 us (7%)
  between operations  1.38 us (1%)
    all_to_all x1, blocking collectives, on_device(): got = lax.all_to_all(send, ROW, 0, 0, tiled=True)  27.9 us
    all_to_all x1, blocking collectives, on_device(): squares = lax.all_to_all(squares, ROW, 0, 0, tiled=True)  16.7 us
    ppermute x4, starting transfers between devices, on_device(): lax.ppermute(slab, 'core', [(0, 1), (1, 0)])  10.1 us
    all_to_all x1, starting transfers between devices, on_device(): gathered = lax.all_to_all(packed, 'z', 0, 0, tiled=True)  9.03 us
    pallas_call x1, Pallas kernels, fields_block(): pl.pallas_call(functools.partial(fields_kernel, rows=rows, norm=norm), ou...  8.46 us
    pallas_call x1, Pallas kernels, resist_block(): pl.pallas_call(functools.partial(resist_kernel, rows=rows, cols=cols), ou...  6.18 us
    ppermute x3, waiting for transfers between devices, on_device(): lax.ppermute(mine, 'x', [(i, (i + k) % 4) for i in range(4)])  4.29 us
    ppermute x3, starting transfers between devices, on_device(): lax.ppermute(gathered, 'y', [(i, (i + k) % 4) for i in range(4)])  3.8 us
  transfers between devices with their start and end apart: 15, of which 6 were waited for; matrix products, arithmetic and copies ran while one was open for 1% of the time, Pallas kernels for 4%

profile of v6, /device:TPU:1, one launch (start us, length us, event | category | flops | bytes accessed | tf_op | source)
XLA Modules:
  0.0 109.2 jit_solution(17932885134271019515)
XLA Ops:
  0.6 1.9 %analyse.1 = f32[8,40,128]{2,1,0:T(8,128)} custom-call(bf16[8,2048]{1,0:T(8,128)(2,1)} %layout_any.1, bf16[1024,256]{1,0:T(8,128)(2,1)} %constant.43.clone.table_any), custom_call_target="tpu_custom_call" | custom-call | tf_op jit(solution)/shard_map/analyse/pallas_call | solution.py:638
  2.6 9.0 %all-to-all-start = ((f32[8,40,128]{2,1,0:T(8,128)}), f32[8,40,128]{2,1,0:T(8,128)S(1)}, u32[]{:S(2)}, u32[]{:S(2)}) async-start(f32[8,40,128]{2,1,0:T(8,128)} %analyse.1), calls=%async_computation | async-start | bytes 327680 | tf_op jit(solution)/shard_map/all_to_all | solution.py:651
  11.6 1.0 collective-permute-start
  12.6 1.6 %collective-permute-start.1 = (bf16[8,2048]{1,0:T(8,128)(2,1)}, bf16[8,2048]{1,0:T(8,128)(2,1)S(1)}, u32[]{:S(2)}, u32[]{:S(2)}) collective-permute-start(bf16[8,2048]{1,0:T(8,128)(2,1)} %refs_15_.1), channel_id=1, source_target_pairs={{0,252},{4,8},{8,4},{12,16},{16,12},{20,24},{24,20},{28,32},{32,28... | collective-permute-start | bytes 98312 | tf_op jit(solution)/shard_map/ppermute | solution.py:636
  14.2 1.1 dynamic-slice_bitcast_fusion.refs_10_
  15.3 2.1 %tables.1 = (bf16[896,160]{1,0:T(8,128)(2,1)S(1)}, bf16[96,896]{1,0:T(8,128)(2,1)S(1)}, bf16[640,144]{1,0:T(8,128)(2,1)S(1)}, bf16[64,640]{1,0:T(8,128)(2,1)S(1)}) custom-call(f32[9,64]{1,0:T(8,128)} %first_taps_any.1, f32[9,64]{1,0:T(8,128)} %second_taps_any.1, f32[1,64]{1,0:T(1,128)} %bitcast.7, bf16[144,1792]{1,0:T(8,128)(2,1)} %constant.44.clone.choose_any, ...), custom_call_target="tpu_custom_call" | custom-call | tf_op jit(solution)/shard_map/tables/pallas_call | solution.py:207
  17.3 0.0 collective-permute-done.refs_8_
  17.3 0.8 collective-permute-done.1.refs_9_
  18.2 1.6 %all-to-all-done.in_ref = f32[8,40,128]{2,1,0:T(8,128)S(1)} async-done(((f32[8,40,128]{2,1,0:T(8,128)}), f32[8,40,128]{2,1,0:T(8,128)S(1)}, u32[]{:S(2)}, u32[]{:S(2)}) %all-to-all-start) | async-done | bytes 163872 | tf_op jit(solution)/shard_map/all_to_all | solution.py:651
  19.7 0.1 repack.1.refs_0_
  19.8 2.8 %collective-permute-start.4 = (f32[33,8,128]{2,1,0:T(8,128)S(1)}, f32[33,8,128]{2,1,0:T(8,128)S(1)}, u32[]{:S(2)}, u32[]{:S(2)}) collective-permute-start(f32[33,8,128]{2,1,0:T(8,128)S(1)} %repack.1.refs_0_), channel_id=1, source_target_pairs={{0,192},{64,0},{128,64},{192,128},{1,193},{65,1},{129,65},{193,129... | collective-permute-start | bytes 405512 | tf_op jit(solution)/shard_map/ppermute | solution.py:666
  22.6 0.3 collective-permute-start.3
  22.9 0.7 collective-permute-start.2
  23.6 3.8 %collective-permute-start.5 = (f32[33,8,128]{2,1,0:T(8,128)S(1)}, f32[33,8,128]{2,1,0:T(8,128)S(1)}, u32[]{:S(2)}, u32[]{:S(2)}) collective-permute-start(f32[33,8,128]{2,1,0:T(8,128)S(1)} %repack.1.refs_0_), channel_id=1, source_target_pairs={{0,4},{4,0},{1,5},{5,1},{2,6},{6,2},{3,7},{7,3},{8,12},{12,8},{9,1... | collective-permute-start | bytes 405512 | tf_op jit(solution)/shard_map/ppermute | solution.py:667
  27.4 0.0 collective-permute-done.4.refs_3_
  27.4 2.4 %collective-permute-start.8 = (f32[33,8,128]{2,1,0:T(8,128)S(1)}, f32[33,8,128]{2,1,0:T(8,128)S(1)}, u32[]{:S(2)}, u32[]{:S(2)}) collective-permute-start(f32[33,8,128]{2,1,0:T(8,128)S(1)} %collective-permute-done.4.refs_3_), channel_id=1, source_target_pairs={{0,4},{4,0},{1,5},{5,1},{2,6},{6,2},{3,7},{7,3},{8,12},{12,8},{9,1... | collective-permute-start | bytes 405512 | tf_op jit(solution)/shard_map/ppermute | solution.py:667
  29.8 0.0 collective-permute-done.3.refs_2_
  29.8 2.6 %collective-permute-start.7 = (f32[33,8,128]{2,1,0:T(8,128)S(1)}, f32[33,8,128]{2,1,0:T(8,128)S(1)}, u32[]{:S(2)}, u32[]{:S(2)}) collective-permute-start(f32[33,8,128]{2,1,0:T(8,128)S(1)} %collective-permute-done.3.refs_2_), channel_id=1, source_target_pairs={{0,4},{4,0},{1,5},{5,1},{2,6},{6,2},{3,7},{7,3},{8,12},{12,8},{9,1... | collective-permute-start | bytes 405512 | tf_op jit(solution)/shard_map/ppermute | solution.py:667
  32.4 0.0 collective-permute-done.2.refs_1_
  32.4 1.3 %collective-permute-start.6 = (f32[33,8,128]{2,1,0:T(8,128)S(1)}, f32[33,8,128]{2,1,0:T(8,128)S(1)}, u32[]{:S(2)}, u32[]{:S(2)}) collective-permute-start(f32[33,8,128]{2,1,0:T(8,128)S(1)} %collective-permute-done.2.refs_1_), channel_id=1, source_target_pairs={{0,4},{4,0},{1,5},{5,1},{2,6},{6,2},{3,7},{7,3},{8,12},{12,8},{9,1... | collective-permute-start | bytes 405512 | tf_op jit(solution)/shard_map/ppermute | solution.py:667
  33.8 0.0 collective-permute-done.5.refs_4_
  33.8 0.0 collective-permute-done.8.refs_7_
  33.8 0.0 collective-permute-done.7.refs_6_
  33.8 1.0 collective-permute-done.6.refs_5_
  34.8 8.5 %fields.1 = (f32[4,8,128]{2,1,0:T(8,128)S(1)}, f32[24,32,1024]{2,1,0:T(8,128)S(1)}, f32[16,2048]{1,0:T(8,128)S(1)}, f32[16,2048]{1,0:T(8,128)S(1)}, f32[32,128]{1,0:T(8,128)S(1)}, /*index=5*/f32[32,128]{1,0:T(8,128)S(1)}) custom-call(f32[33,8,128]{2,1,0:T(8,128)S(1)} %repack.1.refs_0_, f32[33,8,128]{2,1,0:T(8,128)S(1)} %collective-permute-done.2.refs_1_, ...), custom_call_target="tpu_custom_call" | custom-call | tf_op jit(solution)/shard_map/fields/pallas_call | solution.py:587
  43.2 1.3 %collective-permute-start.9 = (f32[32,128]{1,0:T(8,128)S(1)}, f32[32,128]{1,0:T(8,128)S(1)}, u32[]{:S(2)}, u32[]{:S(2)}) collective-permute-start(f32[32,128]{1,0:T(8,128)S(1)} %get-tuple-element.36), channel_id=1, source_target_pairs={{0,1},{1,2},{2,3},{3,0},{4,5},{5,6},{6,7},{7,4},{8,9},{9,10},{10,1... | collective-permute-start | bytes 49160 | tf_op jit(solution)/shard_map/ppermute | solution.py:673
  44.5 1.5 %collective-permute-start.10 = (f32[32,128]{1,0:T(8,128)S(1)}, f32[32,128]{1,0:T(8,128)S(1)}, u32[]{:S(2)}, u32[]{:S(2)}) collective-permute-start(f32[32,128]{1,0:T(8,128)S(1)} %get-tuple-element.37), channel_id=1, source_target_pairs={{1,0},{2,1},{3,2},{0,3},{5,4},{6,5},{7,6},{4,7},{9,8},{10,9},{11,1... | collective-permute-start | bytes 49160 | tf_op jit(solution)/shard_map/ppermute | solution.py:674
  46.7 2.2 %middle.1 = (f32[48,1536]{1,0:T(8,128)S(1)}, f32[640,1536]{1,0:T(8,128)S(1)}) custom-call(f32[16,2048]{1,0:T(8,128)S(1)} %get-tuple-element.34.field_ref, bf16[896,160]{1,0:T(8,128)(2,1)S(1)} %get-tuple-element.38.first_ref, bf16[96,896]{1,0:T(8,128)(2,1)S(1)} %get-tuple-element.39.second_ref), custom_call_target="tpu_custom_call" | custom-call | tf_op jit(solution)/shard_map/middle/pallas_call | solution.py:341
  48.9 0.0 collective-permute-done.9.left_ref
  48.9 0.0 collective-permute-done.10.right_ref
  48.9 6.2 %resist.1 = (f32[8,2048]{1,0:T(8,128)}, f32[64,24,128]{2,1,0:T(8,128)S(1)}) custom-call(f32[16,2048]{1,0:T(8,128)S(1)} %get-tuple-element.34.field_ref, f32[16,2048]{1,0:T(8,128)S(1)} %get-tuple-element.35.target_ref, f32[32,128]{1,0:T(8,128)S(1)} %collective-permute-done.9.left_ref, f32[32,128]{1,0:T(8,128)S(1)} %collective-permute-done.10.right_ref, ...), custom_call_target="tpu_custom_call" | custom-call | tf_op jit(solution)/shard_map/resist/pallas_call | solution.py:355
  55.1 27.9 %all_to_all.15 = f32[64,24,128]{2,1,0:T(8,128)S(1)} all-to-all(f32[64,24,128]{2,1,0:T(8,128)S(1)} %get-tuple-element.46), channel_id=1, replica_groups=mesh['y'=4,'z'=8,'core'=2,'x'=4] {'y','z','core'}, dimensions={0} | all-to-all | bytes 1572864 | tf_op jit(solution)/shard_map/all_to_all | solution.py:682
  83.0 1.8 %adjoint.1.x_ref = f32[2,2,24,128]{3,2,1,0:T(8,128)S(1)} custom-call(f32[1536,128]{1,0:T(8,128)S(1)} %bitcast.5, f32[4,8,128]{2,1,0:T(8,128)S(1)} %get-tuple-element.47.columns_ref, bf16[256,256]{1,0:T(8,128)(2,1)} %constant.53.clone.table_any, f32[16,128]{1,0:T(8,128)} %constant.54.clone.turn_any), custom_call_target="tpu_custom_call" | custom-call | tf_op jit(solution)/shard_map/adjoint/pallas_call | solution.py:684
  84.7 1.9 %collective-permute-start.13 = (f32[2,2,24,128]{3,2,1,0:T(8,128)S(1)}, f32[2,2,24,128]{3,2,1,0:T(8,128)S(1)}, u32[]{:S(2)}, u32[]{:S(2)}) collective-permute-start(f32[2,2,24,128]{3,2,1,0:T(8,128)S(1)} %adjoint.1.x_ref), channel_id=1, source_target_pairs={{0,3},{1,0},{2,1},{3,2},{4,7},{5,4},{6,5},{7,6},{8,11},{9,8},{10,9... | collective-permute-start | bytes 147464 | tf_op jit(solution)/shard_map/ppermute | solution.py:697
  86.6 0.3 collective-permute-start.12
  86.9 0.4 collective-permute-start.11
  87.3 0.5 collective-permute-done.13.three_ref
  87.8 3.3 %collective-permute-done.12.two_ref = f32[2,2,24,128]{3,2,1,0:T(8,128)S(1)} collective-permute-done((f32[2,2,24,128]{3,2,1,0:T(8,128)S(1)}, f32[2,2,24,128]{3,2,1,0:T(8,128)S(1)}, u32[]{:S(2)}, u32[]{:S(2)}) %collective-permute-start.12) | collective-permute-done | bytes 49184 | tf_op jit(solution)/shard_map/ppermute | solution.py:697
  91.1 0.5 collective-permute-done.11.one_ref
  91.6 16.7 %all_to_all.16.squares_ref = f32[64,1,128]{2,1,0:T(1,128)S(1)} all-to-all(f32[64,1,128]{2,1,0:T(1,128)S(1)} %get-tuple-element.49), channel_id=1, replica_groups=mesh['y'=4,'z'=8,'core'=2,'x'=4] {'y','z','core'}, dimensions={0} | all-to-all | bytes 65536 | tf_op jit(solution)/shard_map/all_to_all | solution.py:706
  108.4 0.8 scale.1
  (1 shorter events, 0.0 us)
Async XLA Ops:
  2.6 17.2 %all-to-all-start = ((f32[8,40,128]{2,1,0:T(8,128)}), f32[8,40,128]{2,1,0:T(8,128)S(1)}, u32[]{:S(2)}, u32[]{:S(2)}) async-start(f32[8,40,128]{2,1,0:T(8,128)} %analyse.1), calls=%async_computation | async-start | bytes 327680 | tf_op jit(solution)/shard_map/all_to_all | solution.py:651
  11.6 5.7 %collective-permute-start = (bf16[8,2048]{1,0:T(8,128)(2,1)}, bf16[8,2048]{1,0:T(8,128)(2,1)S(1)}, u32[]{:S(2)}, u32[]{:S(2)}) collective-permute-start(bf16[8,2048]{1,0:T(8,128)(2,1)} %refs_15_.1), channel_id=1, source_target_pairs={{0,4},{4,0},{8,12},{12,8},{16,20},{20,16},{24,28},{28,24},{32,36},... | collective-permute-start | bytes 98312 | tf_op jit(solution)/shard_map/ppermute | solution.py:635
  12.6 5.6 %collective-permute-start.1 = (bf16[8,2048]{1,0:T(8,128)(2,1)}, bf16[8,2048]{1,0:T(8,128)(2,1)S(1)}, u32[]{:S(2)}, u32[]{:S(2)}) collective-permute-start(bf16[8,2048]{1,0:T(8,128)(2,1)} %refs_15_.1), channel_id=1, source_target_pairs={{0,252},{4,8},{8,4},{12,16},{16,12},{20,24},{24,20},{28,32},{32,28... | collective-permute-start | bytes 98312 | tf_op jit(solution)/shard_map/ppermute | solution.py:636
  19.8 7.6 %collective-permute-start.4 = (f32[33,8,128]{2,1,0:T(8,128)S(1)}, f32[33,8,128]{2,1,0:T(8,128)S(1)}, u32[]{:S(2)}, u32[]{:S(2)}) collective-permute-start(f32[33,8,128]{2,1,0:T(8,128)S(1)} %repack.1.refs_0_), channel_id=1, source_target_pairs={{0,192},{64,0},{128,64},{192,128},{1,193},{65,1},{129,65},{193,129... | collective-permute-start | bytes 405512 | tf_op jit(solution)/shard_map/ppermute | solution.py:666
  22.6 7.2 %collective-permute-start.3 = (f32[33,8,128]{2,1,0:T(8,128)S(1)}, f32[33,8,128]{2,1,0:T(8,128)S(1)}, u32[]{:S(2)}, u32[]{:S(2)}) collective-permute-start(f32[33,8,128]{2,1,0:T(8,128)S(1)} %repack.1.refs_0_), channel_id=1, source_target_pairs={{0,128},{64,192},{128,0},{192,64},{1,129},{65,193},{129,1},{193,65... | collective-permute-start | bytes 405512 | tf_op jit(solution)/shard_map/ppermute | solution.py:666
  22.9 9.5 %collective-permute-start.2 = (f32[33,8,128]{2,1,0:T(8,128)S(1)}, f32[33,8,128]{2,1,0:T(8,128)S(1)}, u32[]{:S(2)}, u32[]{:S(2)}) collective-permute-start(f32[33,8,128]{2,1,0:T(8,128)S(1)} %repack.1.refs_0_), channel_id=1, source_target_pairs={{0,64},{64,128},{128,192},{192,0},{1,65},{65,129},{129,193},{193,1... | collective-permute-start | bytes 405512 | tf_op jit(solution)/shard_map/ppermute | solution.py:666
  23.6 10.2 %collective-permute-start.5 = (f32[33,8,128]{2,1,0:T(8,128)S(1)}, f32[33,8,128]{2,1,0:T(8,128)S(1)}, u32[]{:S(2)}, u32[]{:S(2)}) collective-permute-start(f32[33,8,128]{2,1,0:T(8,128)S(1)} %repack.1.refs_0_), channel_id=1, source_target_pairs={{0,4},{4,0},{1,5},{5,1},{2,6},{6,2},{3,7},{7,3},{8,12},{12,8},{9,1... | collective-permute-start | bytes 405512 | tf_op jit(solution)/shard_map/ppermute | solution.py:667
  27.4 6.4 %collective-permute-start.8 = (f32[33,8,128]{2,1,0:T(8,128)S(1)}, f32[33,8,128]{2,1,0:T(8,128)S(1)}, u32[]{:S(2)}, u32[]{:S(2)}) collective-permute-start(f32[33,8,128]{2,1,0:T(8,128)S(1)} %collective-permute-done.4.refs_3_), channel_id=1, source_target_pairs={{0,4},{4,0},{1,5},{5,1},{2,6},{6,2},{3,7},{7,3},{8,12},{12,8},{9,1... | collective-permute-start | bytes 405512 | tf_op jit(solution)/shard_map/ppermute | solution.py:667
  29.8 4.0 %collective-permute-start.7 = (f32[33,8,128]{2,1,0:T(8,128)S(1)}, f32[33,8,128]{2,1,0:T(8,128)S(1)}, u32[]{:S(2)}, u32[]{:S(2)}) collective-permute-start(f32[33,8,128]{2,1,0:T(8,128)S(1)} %collective-permute-done.3.refs_2_), channel_id=1, source_target_pairs={{0,4},{4,0},{1,5},{5,1},{2,6},{6,2},{3,7},{7,3},{8,12},{12,8},{9,1... | collective-permute-start | bytes 405512 | tf_op jit(solution)/shard_map/ppermute | solution.py:667
  32.4 2.3 %collective-permute-start.6 = (f32[33,8,128]{2,1,0:T(8,128)S(1)}, f32[33,8,128]{2,1,0:T(8,128)S(1)}, u32[]{:S(2)}, u32[]{:S(2)}) collective-permute-start(f32[33,8,128]{2,1,0:T(8,128)S(1)} %collective-permute-done.2.refs_1_), channel_id=1, source_target_pairs={{0,4},{4,0},{1,5},{5,1},{2,6},{6,2},{3,7},{7,3},{8,12},{12,8},{9,1... | collective-permute-start | bytes 405512 | tf_op jit(solution)/shard_map/ppermute | solution.py:667
  43.2 5.7 %collective-permute-start.9 = (f32[32,128]{1,0:T(8,128)S(1)}, f32[32,128]{1,0:T(8,128)S(1)}, u32[]{:S(2)}, u32[]{:S(2)}) collective-permute-start(f32[32,128]{1,0:T(8,128)S(1)} %get-tuple-element.36), channel_id=1, source_target_pairs={{0,1},{1,2},{2,3},{3,0},{4,5},{5,6},{6,7},{7,4},{8,9},{9,10},{10,1... | collective-permute-start | bytes 49160 | tf_op jit(solution)/shard_map/ppermute | solution.py:673
  44.5 4.4 %collective-permute-start.10 = (f32[32,128]{1,0:T(8,128)S(1)}, f32[32,128]{1,0:T(8,128)S(1)}, u32[]{:S(2)}, u32[]{:S(2)}) collective-permute-start(f32[32,128]{1,0:T(8,128)S(1)} %get-tuple-element.37), channel_id=1, source_target_pairs={{1,0},{2,1},{3,2},{0,3},{5,4},{6,5},{7,6},{4,7},{9,8},{10,9},{11,1... | collective-permute-start | bytes 49160 | tf_op jit(solution)/shard_map/ppermute | solution.py:674
  84.7 3.1 %collective-permute-start.13 = (f32[2,2,24,128]{3,2,1,0:T(8,128)S(1)}, f32[2,2,24,128]{3,2,1,0:T(8,128)S(1)}, u32[]{:S(2)}, u32[]{:S(2)}) collective-permute-start(f32[2,2,24,128]{3,2,1,0:T(8,128)S(1)} %adjoint.1.x_ref), channel_id=1, source_target_pairs={{0,3},{1,0},{2,1},{3,2},{4,7},{5,4},{6,5},{7,6},{8,11},{9,8},{10,9... | collective-permute-start | bytes 147464 | tf_op jit(solution)/shard_map/ppermute | solution.py:697
  86.6 4.5 %collective-permute-start.12 = (f32[2,2,24,128]{3,2,1,0:T(8,128)S(1)}, f32[2,2,24,128]{3,2,1,0:T(8,128)S(1)}, u32[]{:S(2)}, u32[]{:S(2)}) collective-permute-start(f32[2,2,24,128]{3,2,1,0:T(8,128)S(1)} %adjoint.1.x_ref), channel_id=1, source_target_pairs={{0,2},{1,3},{2,0},{3,1},{4,6},{5,7},{6,4},{7,5},{8,10},{9,11},{10,... | collective-permute-start | bytes 147464 | tf_op jit(solution)/shard_map/ppermute | solution.py:697
  86.9 4.7 %collective-permute-start.11 = (f32[2,2,24,128]{3,2,1,0:T(8,128)S(1)}, f32[2,2,24,128]{3,2,1,0:T(8,128)S(1)}, u32[]{:S(2)}, u32[]{:S(2)}) collective-permute-start(f32[2,2,24,128]{3,2,1,0:T(8,128)S(1)} %adjoint.1.x_ref), channel_id=1, source_target_pairs={{0,1},{1,2},{2,3},{3,0},{4,5},{5,6},{6,7},{7,4},{8,9},{9,10},{10,1... | collective-permute-start | bytes 147464 | tf_op jit(solution)/shard_map/ppermute | solution.py:697
